TPU v7x, 1024 devices: a whole 4x8x16 slice. The times are simulated.
1024 devices in a mesh: replica: 32 (over y_hi, z), expert: 32 (over x, y_lo, core).
Axes of the slice: x: 4, y: 8 (y_hi: 2, y_lo: 4; y = y_hi * 4 + y_lo), z: 16, core: 2. Of those that a mesh axis runs over, the one named last changes fastest.
Arguments:
- tokens: bfloat16 [2, 65536, 2048], P(None, ('replica', 'expert')), may hold values from -6 to 6
- targets: bfloat16 [2, 65536, 2048], P(None, ('replica', 'expert')), may hold values from -6 to 6
- expert_ids: int32 [2, 65536, 1], P(None, ('replica', 'expert')), may hold values from 0 to 15; in each aligned block of 64 rows (0 to 63, 64 to 127, ..., all dimensions but the last counted through in order) at most 6 rows name the same one
- route_weight: float32 [2, 65536], P(None, ('replica', 'expert')), may hold values from 0.3 to 1
- gate_weight: bfloat16 [32, 2048, 384], P('expert'), may hold values from -6 to 6
- up_weight: bfloat16 [32, 2048, 384], P('expert'), may hold values from -6 to 6
- down_weight: bfloat16 [32, 384, 2048], P('expert'), may hold values from -6 to 6
- fragment_delta: bfloat16 [32, 32, 3, 32, 2048], P('replica', 'expert'), may hold values from -6 to 6
- global_fragment: float32 [32, 3, 32, 2048], P('expert'), may hold values from -6 to 6
- outer_momentum: float32 [32, 3, 32, 2048], P('expert'), may hold values from -2 to 2
- fragment_index: int32 [12], replicated, may hold values from 0 to 11, each once
Outputs:
- next_delta: float32 [32, 32, 3, 32, 2048], P('replica', 'expert')
- new_global: float32 [32, 3, 32, 2048], P('expert')
- new_momentum: float32 [32, 3, 32, 2048], P('expert')
Inputs may be any that keep to these rules, and one draw needn't show every extreme that they name: `expert_ids`: within the rows of one device in one inner step, no expert is named more than 6 times; in some such blocks one expert is named exactly 6 times. `fragment_index`: each fragment appears exactly once.
All inputs are finite; a program needn't handle non-finite values.
Results may differ from a plain program's by a relative error of at most 0.015.
Values may be sent and summed in bfloat16 or wider, within the bound.
No kernel may reach another device: no remote copies, remote signals or barrier semaphores. Data moves between devices by JAX's collectives and lax.ppermute only.
A program may use at most 64 MiB of HBM per device.

v0:
```python
import math

import jax
import jax.numpy as jnp
from jax import lax
from jax.sharding import PartitionSpec as P

D = 2048
F = 768
FRAG = 32


INNER_RATE = 0.8
OUTER_RATE = 0.7
MOMENTUM = 0.9


def silu_parts(pre_act):
    sigmoid_value = jax.nn.sigmoid(pre_act)
    return (pre_act * sigmoid_value, sigmoid_value * (1.0 + pre_act * (1.0 - sigmoid_value)))


def slot_table(expert_row, experts, capacity):
    onehot = (expert_row[:, None] == jnp.arange(experts, dtype=jnp.int32)[None, :]).astype(
        jnp.int32
    )
    before = jnp.cumsum(onehot, axis=0) - onehot
    return expert_row * capacity + jnp.sum(before * onehot, axis=1)


def contract(left_part, right_part, left_dim, right_dim):
    return lax.dot_general(
        left_part,
        right_part,
        (((left_dim,), (right_dim,)), ((), ())),
        preferred_element_type=jnp.float32,
    )


def exact_contract(left_part, right_part, left_dim, right_dim):
    return lax.dot_general(
        left_part.astype(jnp.float32),
        right_part.astype(jnp.float32),
        (((left_dim,), (right_dim,)), ((), ())),
        precision=lax.Precision.HIGHEST,
        preferred_element_type=jnp.float32,
    )


def deliver(send_table, experts, capacity):
    row_width = send_table.shape[-1]
    doubled = jnp.repeat(send_table.reshape(experts, capacity, row_width), 2, axis=0)
    received = lax.all_to_all(doubled, "expert", split_axis=0, concat_axis=0, tiled=True)
    return received.reshape(-1, row_width)


def gather_back(partial_rows, experts, capacity):
    row_width = partial_rows.shape[-1]
    slice_rows = partial_rows.reshape(2 * experts, capacity, row_width)
    returned = lax.all_to_all(slice_rows, "expert", split_axis=0, concat_axis=0, tiled=True)
    summed = returned.reshape(experts, 2, capacity, row_width).sum(axis=1).astype(jnp.bfloat16)
    summed = lax.optimization_barrier(summed).reshape(experts * capacity, row_width)
    return summed


def take_columns(matrix, start_unit):
    return jnp.transpose(lax.dynamic_slice_in_dim(matrix, start_unit, FRAG, 1))


def take_rows(matrix, start_unit):
    return lax.dynamic_slice_in_dim(matrix, start_unit, FRAG, 0)


def shards(
    tokens,
    targets,
    expert_ids,
    route_weight,
    gate_weight,
    up_weight,
    down_weight,
    fragment_delta,
    global_fragment,
    outer_momentum,
    fragment_index,
):
    experts = lax.axis_size("expert") // 2
    replicas = lax.axis_size("replica")
    token_rows = tokens.shape[1]
    capacity = 2 * min(token_rows // 2, max(1, token_rows * 3 // (experts * 4)))
    scale_model = 1.0 / math.sqrt(D)
    scale_hidden = 1.0 / math.sqrt(F)
    start_unit = fragment_index[0] * FRAG
    slot_range = jnp.arange(experts * capacity, dtype=jnp.int32)
    delta_total = lax.psum(
        fragment_delta[0, 0].astype(jnp.float32).astype(jnp.bfloat16), "replica"
    ).astype(jnp.float32)

    def expert_step(inner_step, project_in, project_out):
        flat_slot = slot_table(expert_ids[inner_step, :, 0], experts, capacity)
        placing = (flat_slot[:, None] == slot_range[None, :]).astype(jnp.bfloat16)
        token_table = contract(placing, tokens[inner_step], 0, 0).astype(jnp.bfloat16)
        expert_rows = deliver(token_table, experts, capacity)
        pre_gate, pre_up = project_in(expert_rows)
        activated, silu_slope = silu_parts(pre_gate)
        hidden = (activated * pre_up).astype(jnp.bfloat16)
        partial_rows = project_out(hidden)
        summed = gather_back(partial_rows, experts, capacity)
        combined = jnp.take(summed, flat_slot, axis=0).astype(jnp.float32)
        route_column = route_weight[inner_step][:, None]
        output = route_column * combined
        cotangent = (route_column * (output - targets[inner_step].astype(jnp.float32))).astype(
            jnp.bfloat16
        )
        cotangent_table = contract(placing, cotangent, 0, 0).astype(jnp.bfloat16)
        cotangent_rows = deliver(cotangent_table, experts, capacity)
        return (expert_rows, pre_gate, pre_up, activated, silu_slope, hidden, cotangent_rows)

    gate_matrix = gate_weight[0]
    up_matrix = up_weight[0]
    down_matrix = down_weight[0]

    def first_in(rows):
        return (
            jnp.dot(rows, gate_matrix, preferred_element_type=jnp.float32) * scale_model,
            jnp.dot(rows, up_matrix, preferred_element_type=jnp.float32) * scale_model,
        )

    def first_out(hidden_rows):
        return jnp.dot(hidden_rows, down_matrix, preferred_element_type=jnp.float32) * scale_hidden

    rows_first, pre_gate, pre_up, activated, silu_slope, hidden_first, cot_first = expert_step(
        0, first_in, first_out
    )
    hidden_cot = contract(cot_first, down_matrix, 1, 1) * scale_hidden
    gate_first = (hidden_cot * pre_up * silu_slope).astype(jnp.bfloat16)
    up_first = (hidden_cot * activated).astype(jnp.bfloat16)
    first_grads = jnp.stack(
        [
            contract(lax.dynamic_slice_in_dim(gate_first, start_unit, FRAG, 1), rows_first, 0, 0)
            * scale_model,
            contract(lax.dynamic_slice_in_dim(up_first, start_unit, FRAG, 1), rows_first, 0, 0)
            * scale_model,
            contract(lax.dynamic_slice_in_dim(hidden_first, start_unit, FRAG, 1), cot_first, 0, 0)
            * scale_hidden,
        ]
    )
    shrink_model = INNER_RATE * scale_model * scale_model
    shrink_hidden = INNER_RATE * scale_hidden * scale_hidden

    def second_in(rows):
        intersection = contract(rows, rows_first, 1, 1)
        gate_value = jnp.dot(
            rows, gate_matrix, preferred_element_type=jnp.float32
        ) * scale_model - shrink_model * exact_contract(intersection, gate_first, 1, 0)
        up_value = jnp.dot(
            rows, up_matrix, preferred_element_type=jnp.float32
        ) * scale_model - shrink_model * exact_contract(intersection, up_first, 1, 0)
        return (gate_value, up_value)

    def second_out(hidden_rows):
        intersection = contract(hidden_rows, hidden_first, 1, 1)
        return jnp.dot(
            hidden_rows, down_matrix, preferred_element_type=jnp.float32
        ) * scale_hidden - shrink_hidden * exact_contract(intersection, cot_first, 1, 0)

    expert_rows, pre_gate, pre_up, activated, silu_slope, hidden, cotangent_rows = expert_step(
        1, second_in, second_out
    )
    down_part = take_rows(down_matrix, start_unit).astype(jnp.float32) - INNER_RATE * first_grads[2]
    hidden_part = lax.dynamic_slice_in_dim(hidden, start_unit, FRAG, 1)
    up_part = lax.dynamic_slice_in_dim(pre_up, start_unit, FRAG, 1)
    slope_part = lax.dynamic_slice_in_dim(silu_slope, start_unit, FRAG, 1)
    act_part = lax.dynamic_slice_in_dim(activated, start_unit, FRAG, 1)
    hidden_cot = exact_contract(cotangent_rows, down_part, 1, 1) * scale_hidden
    down_fragment = contract(hidden_part, cotangent_rows, 0, 0) * scale_hidden
    gate_cot = (hidden_cot * up_part * slope_part).astype(jnp.bfloat16)
    up_cot = (hidden_cot * act_part).astype(jnp.bfloat16)
    gate_fragment = contract(gate_cot, expert_rows, 0, 0) * scale_model
    up_fragment = contract(up_cot, expert_rows, 0, 0) * scale_model
    second_grads = jnp.stack([gate_fragment, up_fragment, down_fragment])
    start_values = jnp.stack(
        [
            take_columns(gate_matrix, start_unit),
            take_columns(up_matrix, start_unit),
            take_rows(down_matrix, start_unit),
        ]
    ).astype(jnp.float32)
    local_fragment = start_values - INNER_RATE * (first_grads + second_grads)
    next_delta = global_fragment[0] - local_fragment
    mean_delta = delta_total / replicas
    new_momentum = MOMENTUM * outer_momentum[0] + mean_delta
    new_global = global_fragment[0] - OUTER_RATE * (mean_delta + MOMENTUM * new_momentum)
    return (next_delta[None, None], new_global[None], new_momentum[None])


def solution(mesh):
    placed = (
        P(None, ("replica", "expert"), None),
        P(None, ("replica", "expert"), None),
        P(None, ("replica", "expert"), None),
        P(None, ("replica", "expert")),
        P("expert", None, None),
        P("expert", None, None),
        P("expert", None, None),
        P("replica", "expert", None, None, None),
        P("expert", None, None, None),
        P("expert", None, None, None),
        P(),
    )
    return jax.shard_map(
        shards,
        mesh=mesh,
        in_specs=placed,
        out_specs=(
            P("replica", "expert", None, None, None),
            P("expert", None, None, None),
            P("expert", None, None, None),
        ),
        check_vma=False,
    )
```

profile of v0, /device:TPU:56, one launch (start us, length us, event | category | flops | bytes accessed | tf_op | source)
XLA Modules:
  0.0 591.6 jit_solution(4843088031974442225)
XLA Ops:
  11.2 31.6 %all_to_all.30 = bf16[32,6,2048]{2,1,0:T(8,128)(2,1)} all-to-all(bf16[32,6,2048]{2,1,0:T(8,128)(2,1)S(1)} %bitcast.152), channel_id=1, replica_groups=mesh['replica'=32,'expert'=32] {'expert'}, dimensions={0} | all-to-all | bytes 1572864 | tf_op jit(solution)/shard_map/all_to_all | solution.py:53
  42.8 1.4 reshape.248
  47.1 1.8 convolution_multiply_fusion.2
  48.9 2.6 reshape.249
  51.6 8.8 %all-to-all-start.1 = ((f32[32,6,2048]{2,1,0:T(8,128)}), f32[32,6,2048]{2,1,0:T(8,128)}, u32[]{:S(2)}, u32[]{:S(2)}) async-start(f32[32,6,2048]{2,1,0:T(8,128)} %reshape.249), calls=%async_computation.1 | async-start | bytes 4194304 | tf_op jit(solution)/shard_map/all_to_all | solution.py:60
  60.9 45.9 %all-to-all-done.1 = f32[32,6,2048]{2,1,0:T(8,128)} async-done(((f32[32,6,2048]{2,1,0:T(8,128)}), f32[32,6,2048]{2,1,0:T(8,128)}, u32[]{:S(2)}, u32[]{:S(2)}) %all-to-all-start.1) | async-done | bytes 1572896 | tf_op jit(solution)/shard_map/all_to_all | solution.py:60
  107.9 8.7 %all-to-all-start.3 = ((bf16[32,6,2048]{2,1,0:T(8,128)(2,1)}), bf16[32,6,2048]{2,1,0:T(8,128)(2,1)}, u32[]{:S(2)}, u32[]{:S(2)}) async-start(bf16[32,6,2048]{2,1,0:T(8,128)(2,1)} %bitcast.150), calls=%async_computation.3 | async-start | bytes 2097152 | tf_op jit(solution)/shard_map/all_to_all | solution.py:53
  117.2 2.7 bitcast_reduce_fusion.1
  123.3 17.2 %all-to-all-done.3 = bf16[32,6,2048]{2,1,0:T(8,128)(2,1)} async-done(((bf16[32,6,2048]{2,1,0:T(8,128)(2,1)}), bf16[32,6,2048]{2,1,0:T(8,128)(2,1)}, u32[]{:S(2)}, u32[]{:S(2)}) %all-to-all-start.3) | async-done | bytes 786464 | tf_op jit(solution)/shard_map/all_to_all | solution.py:53
  141.5 8.7 %all-to-all-start.2 = ((bf16[32,6,2048]{2,1,0:T(8,128)(2,1)}), bf16[32,6,2048]{2,1,0:T(8,128)(2,1)}, u32[]{:S(2)}, u32[]{:S(2)}) async-start(bf16[32,6,2048]{2,1,0:T(8,128)(2,1)} %bitcast.151), calls=%async_computation.2 | async-start | bytes 2097152 | tf_op jit(solution)/shard_map/all_to_all | solution.py:53
  150.3 1.4 reshape.257
  152.1 22.1 %all-to-all-done.2 = bf16[32,6,2048]{2,1,0:T(8,128)(2,1)} async-done(((bf16[32,6,2048]{2,1,0:T(8,128)(2,1)}), bf16[32,6,2048]{2,1,0:T(8,128)(2,1)}, u32[]{:S(2)}, u32[]{:S(2)}) %all-to-all-start.2) | async-done | bytes 786464 | tf_op jit(solution)/shard_map/all_to_all | solution.py:53
  174.2 2.1 reshape.254
  176.3 2.6 multiply_convert_fusion.2
  180.2 1.6 add_divide_fusion
  183.2 1.7 fusion
  184.9 2.7 reshape.258
  187.6 8.9 %all-to-all-start.4 = ((f32[32,6,2048]{2,1,0:T(8,128)}), f32[32,6,2048]{2,1,0:T(8,128)}, u32[]{:S(2)}, u32[]{:S(2)}) async-start(f32[32,6,2048]{2,1,0:T(8,128)} %reshape.258), calls=%async_computation.4 | async-start | bytes 4194304 | tf_op jit(solution)/shard_map/all_to_all | solution.py:60
  197.3 2.4 constant_dynamic-slice_fusion
  199.7 1.9 copy.18
  201.6 1.9 copy.17
  203.5 1.6 dynamic-slice_bitcast_fusion
  205.1 38.6 %all-to-all-done.4 = f32[32,6,2048]{2,1,0:T(8,128)} async-done(((f32[32,6,2048]{2,1,0:T(8,128)}), f32[32,6,2048]{2,1,0:T(8,128)}, u32[]{:S(2)}, u32[]{:S(2)}) %all-to-all-start.4) | async-done | bytes 1572896 | tf_op jit(solution)/shard_map/all_to_all | solution.py:60
  243.7 1.8 bitcast_reduce_fusion
  248.2 9.1 %all-to-all-start.5 = ((bf16[32,6,2048]{2,1,0:T(8,128)(2,1)}), bf16[32,6,2048]{2,1,0:T(8,128)(2,1)}, u32[]{:S(2)}, u32[]{:S(2)}) async-start(bf16[32,6,2048]{2,1,0:T(8,128)(2,1)} %bitcast.28), calls=%async_computation.5 | async-start | bytes 2097152 | tf_op jit(solution)/shard_map/all_to_all | solution.py:53
  257.3 312.8 %all-reduce.2.cloned.1.call-done = bf16[3,32,2048]{2,1,0:T(8,128)(2,1)} async-done(((bf16[3,32,2048]{2,1,0:T(8,128)(2,1)}), bf16[3,32,2048]{2,1,0:T(8,128)(2,1)}) %all-reduce.2.cloned.1.call-update) | async-done | bytes 393232 | tf_op jit(solution)/shard_map/psum | solution.py:95
  570.0 2.4 fusion.43
  572.4 1.9 fusion.4
  574.4 1.9 fusion.5
  577.4 1.4 reshape.263
  579.2 1.7 convolution_multiply_fusion.10
  582.2 1.4 fusion.3
  (102 shorter events, 23.9 us)
Async XLA Ops:
  9.6 50.8 %copy-start.21 = (s32[64]{0:T(128)}, s32[64]{0:T(128)S(1)}, u32[]{:S(2)}) copy-start(s32[64]{0:T(128)S(1)} %get-tuple-element.5) | copy-start | bytes 772
  11.2 33.0 %copy-start = (bf16[1,2048,384]{2,1,0:T(8,128)(2,1)S(1)}, bf16[1,2048,384]{2,1,0:T(8,128)(2,1)}, u32[]{:S(2)}) copy-start(bf16[1,2048,384]{2,1,0:T(8,128)(2,1)} %param.17) | copy-start | bytes 4718596
  44.2 1.4 copy-start.6
  45.6 1.3 copy-start.18
  45.6 1.5 copy-start.1
  46.9 2.0 copy-start.11
  51.6 8.8 %copy-start.17 = (bf16[2,64,2048]{2,1,0:T(8,128)(2,1)S(1)}, bf16[2,64,2048]{2,1,0:T(8,128)(2,1)}, u32[]{:S(2)}) copy-start(bf16[2,64,2048]{2,1,0:T(8,128)(2,1)} %param.13) | copy-start | bytes 1572868
  51.6 55.2 %all-to-all-start.1 = ((f32[32,6,2048]{2,1,0:T(8,128)}), f32[32,6,2048]{2,1,0:T(8,128)}, u32[]{:S(2)}, u32[]{:S(2)}) async-start(f32[32,6,2048]{2,1,0:T(8,128)} %reshape.249), calls=%async_computation.1 | async-start | bytes 4194304 | tf_op jit(solution)/shard_map/all_to_all | solution.py:60
  60.9 55.7 %copy-start.24 = (f32[2,64]{1,0:T(2,128)S(1)}, f32[2,64]{1,0:T(2,128)}, u32[]{:S(2)}) copy-start(f32[2,64]{1,0:T(2,128)} %param.16) | copy-start | bytes 1540
  107.9 32.6 %all-to-all-start.3 = ((bf16[32,6,2048]{2,1,0:T(8,128)(2,1)}), bf16[32,6,2048]{2,1,0:T(8,128)(2,1)}, u32[]{:S(2)}, u32[]{:S(2)}) async-start(bf16[32,6,2048]{2,1,0:T(8,128)(2,1)} %bitcast.150), calls=%async_computation.3 | async-start | bytes 2097152 | tf_op jit(solution)/shard_map/all_to_all | solution.py:53
  141.5 32.6 %all-to-all-start.2 = ((bf16[32,6,2048]{2,1,0:T(8,128)(2,1)}), bf16[32,6,2048]{2,1,0:T(8,128)(2,1)}, u32[]{:S(2)}, u32[]{:S(2)}) async-start(bf16[32,6,2048]{2,1,0:T(8,128)(2,1)} %bitcast.151), calls=%async_computation.2 | async-start | bytes 2097152 | tf_op jit(solution)/shard_map/all_to_all | solution.py:53
  176.3 3.0 copy-start.7
  178.9 1.0 copy-start.20
  178.9 1.0 copy-start.19
  179.9 1.9 copy-start.8
  180.2 1.6 copy-start.12
  180.2 1.8 copy-start.3
  181.8 1.4 copy-start.2
  187.6 9.7 %copy-start.28 = (s32[12]{0:T(128)S(1)}, s32[12]{0:T(128)}, u32[]{:S(2)}) copy-start(s32[12]{0:T(128)} %param.23) | copy-start | bytes 148
  187.6 56.0 %all-to-all-start.4 = ((f32[32,6,2048]{2,1,0:T(8,128)}), f32[32,6,2048]{2,1,0:T(8,128)}, u32[]{:S(2)}, u32[]{:S(2)}) async-start(f32[32,6,2048]{2,1,0:T(8,128)} %reshape.258), calls=%async_computation.4 | async-start | bytes 4194304 | tf_op jit(solution)/shard_map/all_to_all | solution.py:60
  196.6 373.5 %all-reduce.2.cloned.1.call-start = ((), (), s32[]{:S(2)}) async-start(), calls=%async_computation.6 | async-start | bytes 786432 | tf_op jit(solution)/shard_map/psum | solution.py:95
  197.3 6.1 %copy-start.22 = (s32[64]{0:T(128)S(1)}, s32[64]{0:T(128)}, u32[]{:S(2)}) copy-start(s32[64]{0:T(128)} %copy-done.21) | copy-start | bytes 772
  245.5 1.0 copy-start.27
  247.1 323.0 %copy-start.5 = (f32[1,3,32,2048]{3,2,1,0:T(8,128)S(1)}, f32[1,3,32,2048]{3,2,1,0:T(8,128)}, u32[]{:S(2)}) copy-start(f32[1,3,32,2048]{3,2,1,0:T(8,128)} %param.21) | copy-start | bytes 2359300
  248.2 321.9 %copy-start.13 = (f32[1,3,32,2048]{3,2,1,0:T(8,128)S(1)}, f32[1,3,32,2048]{3,2,1,0:T(8,128)}, u32[]{:S(2)}) copy-start(f32[1,3,32,2048]{3,2,1,0:T(8,128)} %param.22) | copy-start | bytes 2359300
  248.2 329.3 %all-to-all-start.5 = ((bf16[32,6,2048]{2,1,0:T(8,128)(2,1)}), bf16[32,6,2048]{2,1,0:T(8,128)(2,1)}, u32[]{:S(2)}, u32[]{:S(2)}) async-start(bf16[32,6,2048]{2,1,0:T(8,128)(2,1)} %bitcast.28), calls=%async_computation.5 | async-start | bytes 2097152 | tf_op jit(solution)/shard_map/all_to_all | solution.py:53
  572.4 3.8 copy-start.4
  580.9 2.8 copy-start.9
  580.9 2.8 copy-start.10
  580.9 2.8 copy-start.14
  580.9 2.8 copy-start.15
  580.9 2.8 copy-start.16
  (3 other events, 2.8 us)
Sparse Core Ops, SparseCore 0:
  200.9 369.1 all-reduce.1
where the time goes:
time: 593 us; the launch traced here: 592 us
  waiting for transfers between devices  437 us (74%)
  starting transfers between devices  44.4 us (7%)
  blocking collectives  31.6 us (5%)
  local copies, waits for them, and re-layouts  29 us (5%)
  matrix products  25.2 us (4%)
  between operations  14.6 us (2%)
  other arithmetic  9.71 us (2%)
    psum x1, waiting for transfers between devices, shards(): lax.psum(fragment_delta[0, 0].astype(jnp.float32).astype(jnp.bfloat16), '...  313 us
    all_to_all x2, waiting for transfers between devices, gather_back(): lax.all_to_all(slice_rows, 'expert', split_axis=0, concat_axis=0, tiled=T...  84.5 us
    all_to_all x3, waiting for transfers between devices, deliver(): lax.all_to_all(doubled, 'expert', split_axis=0, concat_axis=0, tiled=True)  39.3 us
    all_to_all x1, blocking collectives, deliver(): lax.all_to_all(doubled, 'expert', split_axis=0, concat_axis=0, tiled=True)  31.6 us
    all_to_all x3, starting transfers between devices, deliver(): lax.all_to_all(doubled, 'expert', split_axis=0, concat_axis=0, tiled=True)  26.5 us
    all_to_all x2, starting transfers between devices, gather_back(): lax.all_to_all(slice_rows, 'expert', split_axis=0, concat_axis=0, tiled=T...  17.8 us
    dot_general x13, matrix products, contract(): lax.dot_general(left_part, right_part, (((left_dim,), (right_dim,)), ((),...  14.6 us
  transfers between devices with their start and end apart: 6, of which 5 were waited for; matrix products, arithmetic and copies ran while one was open for 5% of the time, Pallas kernels for 0%

commit v1 on v0

v1 whole, which is shorter than its diff:
```python
import functools
import math

import jax
import jax.numpy as jnp
from jax import lax
from jax.experimental import pallas as pl
from jax.experimental.pallas import tpu as pltpu
from jax.sharding import PartitionSpec as P

D = 2048
F = 768
FS = 384
FRAG = 32
EXT = 128

INNER_RATE = 0.8
OUTER_RATE = 0.7
MOMENTUM = 0.9
SCALE_MODEL = 1.0 / math.sqrt(D)
SCALE_HIDDEN = 1.0 / math.sqrt(F)
SHRINK_MODEL = INNER_RATE * SCALE_MODEL * SCALE_MODEL
SHRINK_HIDDEN = INNER_RATE * SCALE_HIDDEN * SCALE_HIDDEN

F32 = jnp.float32
BF16 = jnp.bfloat16


def iota(shape, dim):
    return lax.broadcasted_iota(jnp.int32, shape, dim)


def mm(a, b, adim=1, bdim=0, precision=None):
    return lax.dot_general(
        a, b, (((adim,), (bdim,)), ((), ())), precision=precision, preferred_element_type=F32
    )


def split_two(x):
    high = x.astype(BF16)
    return high, (x - high.astype(F32)).astype(BF16)


def silu_parts(pre):
    sig = jax.nn.sigmoid(pre)
    return pre * sig, sig * (1.0 + pre * (1.0 - sig))


def call(kernel, outs, limit=56, flops=1_000_000_000, bytes_accessed=8_000_000):
    return pl.pallas_call(
        kernel,
        out_shape=outs,
        compiler_params=pltpu.CompilerParams(vmem_limit_bytes=limit * 1024 * 1024),
        cost_estimate=pl.CostEstimate(
            flops=flops, bytes_accessed=bytes_accessed, transcendentals=0
        ),
    )


def sds(shape, dtype):
    return jax.ShapeDtypeStruct(shape, dtype)


def pack_kernel(cap, tokens, targets, ids, weight, table):
    rows = table.shape[0]
    count = 2 * tokens.shape[1]
    half = tokens.shape[1]
    ids_col = ids[...].reshape(count, 1)
    first, second = iota((count, count), 0), iota((count, count), 1)
    ids_row = jnp.sum(jnp.where(first == second, ids_col, 0), axis=0, keepdims=True)
    together = (first < half) == (second < half)
    earlier = (ids_col == ids_row) & (first < second) & together
    slot = jnp.sum(jnp.where(earlier, 1, 0), axis=0, keepdims=True)
    step_row = jnp.where(iota((1, count), 1) < half, 0, cap)
    place = ids_row * (4 * cap) + slot + step_row
    row = iota((rows, count), 0)
    put_token = (row == place).astype(BF16)
    put_target = (row == place + 2 * cap).astype(BF16)
    w_row = jnp.concatenate([weight[0:1, :], weight[1:2, :]], axis=1)
    w_col = jnp.sum(jnp.where(first == second, w_row, 0.0), axis=1, keepdims=True)
    high, rest = split_two(w_col)
    rest = w_col - high.astype(F32)
    middle = rest.astype(BF16)
    low = (rest - middle.astype(F32)).astype(BF16)
    lane = iota((count, EXT), 1)
    w_terms = jnp.where(
        lane == 0,
        high.astype(F32),
        jnp.where(lane == 1, middle.astype(F32), jnp.where(lane == 2, low.astype(F32), 0.0)),
    ).astype(BF16)
    step = 512
    for c in range(0, D, step):
        tok = tokens[:, :, c : c + step].reshape(count, step)
        tgt = targets[:, :, c : c + step].reshape(count, step)
        table[:, c : c + step] = (mm(put_token, tok) + mm(put_target, tgt)).astype(BF16)
    table[:, D : D + EXT] = mm(put_target, w_terms).astype(BF16)


def picker(cap, sources, kind):
    rows = sources * cap
    j = iota((rows, 4 * rows), 0)
    source = (j.astype(F32) * (1.0 / cap) + 0.5 / cap).astype(jnp.int32)
    wanted = j + source * (3 * cap) + kind * cap
    return (iota((rows, 4 * rows), 1) == wanted).astype(BF16)


def first_kernel(cap, own, other, gate, up, down, x_out, partial, act, slope_up, hidden_out):
    sources = own.shape[0] // (4 * cap)
    pick = picker(cap, sources, 0)
    half = sources * cap
    x_out[0:half, :] = mm(pick, own[:, 0:D]).astype(BF16)
    x_out[half:, :] = mm(pick, other[:, 0:D]).astype(BF16)
    x = x_out[...]
    pre_gate = mm(x, gate[...]) * SCALE_MODEL
    pre_up = mm(x, up[...]) * SCALE_MODEL
    activated, slope = silu_parts(pre_gate)
    act[...] = activated
    slope_up[...] = pre_up * slope
    hidden = (activated * pre_up).astype(BF16)
    hidden_out[...] = hidden
    partial[...] = mm(hidden, down[...]) * SCALE_HIDDEN


def unpack_kernel(
    cap, own, other, gate, up, x1, x2_out, t1_out, t2_out, w_out, gate_out, up_out, cross
):
    sources = own.shape[0] // (4 * cap)
    half = sources * cap
    pick = picker(cap, sources, 1)
    x2_out[0:half, :] = mm(pick, own[:, 0:D]).astype(BF16)
    x2_out[half:, :] = mm(pick, other[:, 0:D]).astype(BF16)
    for k, t_out in ((2, t1_out), (3, t2_out)):
        pick = picker(cap, sources, k)
        for part, ref in ((0, own), (half, other)):
            t_out[part : part + half, :] = mm(pick, ref[:, 0:D]).astype(BF16)
            terms = mm(pick, ref[:, D : D + EXT])
            w_out[k - 2, part : part + half, :] = jnp.broadcast_to(
                jnp.sum(terms, axis=1, keepdims=True), (half, EXT)
            )
    x2 = x2_out[...]
    gate_out[...] = mm(x2, gate[...]) * SCALE_MODEL
    up_out[...] = mm(x2, up[...]) * SCALE_MODEL
    cross[...] = mm(x2, x1[...], 1, 1)


def cotangent(partial, received, target, weight):
    half = partial.shape[0] // 2
    swapped = jnp.concatenate([received[half:, :], received[:half, :]], axis=0)
    combined = (partial + swapped).astype(BF16).astype(F32)
    return (weight * (weight * combined - target.astype(F32))).astype(BF16)


def second_kernel(
    partial, received, t1, w, down, act, slope_up, hidden1, gate2, up2, cross,
    cot_out, gate_first_out, up_first_out, partial2, hidden2_out, act2_out, slope_up2_out,
):
    cot = cotangent(partial[...], received[...], t1[...], w[0, :, 0:1])
    cot_out[...] = cot
    hidden_cot = mm(cot, down[...], 1, 1) * SCALE_HIDDEN
    gate_first = (hidden_cot * slope_up[...]).astype(BF16)
    up_first = (hidden_cot * act[...]).astype(BF16)
    gate_first_out[...] = gate_first
    up_first_out[...] = up_first
    high, low = split_two(cross[...])
    pre_gate = gate2[...] - SHRINK_MODEL * (mm(high, gate_first) + mm(low, gate_first))
    pre_up = up2[...] - SHRINK_MODEL * (mm(high, up_first) + mm(low, up_first))
    activated, slope = silu_parts(pre_gate)
    hidden = (activated * pre_up).astype(BF16)
    hidden2_out[...] = hidden
    act2_out[...] = activated
    slope_up2_out[...] = pre_up * slope
    high, low = split_two(mm(hidden, hidden1[...], 1, 1))
    partial2[...] = mm(hidden, down[...]) * SCALE_HIDDEN - SHRINK_HIDDEN * (
        mm(high, cot) + mm(low, cot)
    )


def fragment_kernel(
    index, gate, up, down, x1, cot, gate_first, up_first, hidden1, hidden2, act2, slope_up2,
    global_fragment, base, down_part, frag2, hidden_frag2,
):
    start = index[0] * FRAG
    pick = iota((FS, FRAG), 0) == iota((FS, FRAG), 1) + start
    pick_t = (iota((FRAG, FS), 1) == iota((FRAG, FS), 0) + start).astype(BF16)
    pick_f = pick.astype(F32)
    pick = pick.astype(BF16)
    gate_f = mm(gate_first[...], pick).astype(BF16)
    up_f = mm(up_first[...], pick).astype(BF16)
    hidden_f = mm(hidden1[...], pick).astype(BF16)
    base[0] = global_fragment[0] - (
        mm(pick_t, gate[...], 1, 1) - INNER_RATE * (mm(gate_f, x1[...], 0, 0) * SCALE_MODEL)
    )
    base[1] = global_fragment[1] - (
        mm(pick_t, up[...], 1, 1) - INNER_RATE * (mm(up_f, x1[...], 0, 0) * SCALE_MODEL)
    )
    down_rows = mm(pick_t, down[...])
    new_rows = down_rows - INNER_RATE * (mm(hidden_f, cot[...], 0, 0) * SCALE_HIDDEN)
    down_part[...] = new_rows
    base[2] = global_fragment[2] - new_rows
    frag2[0] = mm(slope_up2[...], pick_f, precision=lax.Precision.HIGHEST)
    frag2[1] = mm(act2[...], pick_f, precision=lax.Precision.HIGHEST)
    hidden_frag2[...] = mm(hidden2[...], pick).astype(BF16)


def last_kernel(partial, received, t2, w, x2, down_part, frag2, hidden_frag2, base, out):
    cot = cotangent(partial[...], received[...], t2[...], w[1, :, 0:1])
    high, low = split_two(down_part[...])
    hidden_cot = (mm(cot, high, 1, 1) + mm(cot, low, 1, 1)) * SCALE_HIDDEN
    gate_cot = (hidden_cot * frag2[0]).astype(BF16)
    up_cot = (hidden_cot * frag2[1]).astype(BF16)
    out[0, 0, 0] = base[0] + INNER_RATE * (mm(gate_cot, x2[...], 0, 0) * SCALE_MODEL)
    out[0, 0, 1] = base[1] + INNER_RATE * (mm(up_cot, x2[...], 0, 0) * SCALE_MODEL)
    out[0, 0, 2] = base[2] + INNER_RATE * (mm(hidden_frag2[...], cot, 0, 0) * SCALE_HIDDEN)


def replica_sum(delta):
    return lax.psum(delta, "replica").astype(F32)


def shards(
    tokens,
    targets,
    expert_ids,
    route_weight,
    gate_weight,
    up_weight,
    down_weight,
    fragment_delta,
    global_fragment,
    outer_momentum,
    fragment_index,
):
    size = lax.axis_size("expert")
    experts = size // 2
    replicas = lax.axis_size("replica")
    token_rows = tokens.shape[1]
    cap = 2 * min(token_rows // 2, max(1, token_rows * 3 // (experts * 4)))
    rows = 4 * cap * experts
    slots = 2 * cap * experts
    same_core = [[2 * e + c for e in range(experts)] for c in range(2)]
    pairs = [(i, i ^ 1) for i in range(size)]

    delta_total = replica_sum(fragment_delta[0, 0])

    table = call(functools.partial(pack_kernel, cap), sds((rows, D + EXT), BF16))(
        tokens, targets, expert_ids, route_weight
    )
    own = lax.all_to_all(
        table.reshape(experts, 4 * cap, D + EXT),
        "expert",
        split_axis=0,
        concat_axis=0,
        tiled=True,
        axis_index_groups=same_core,
    ).reshape(rows, D + EXT)
    other = lax.ppermute(own, "expert", pairs)
    gate, up, down = gate_weight[0], up_weight[0], down_weight[0]

    x1, partial, act, slope_up, hidden1 = call(
        functools.partial(first_kernel, cap),
        (
            sds((slots, D), BF16),
            sds((slots, D), F32),
            sds((slots, FS), F32),
            sds((slots, FS), F32),
            sds((slots, FS), BF16),
        ),
    )(own, other, gate, up, down)
    received = lax.ppermute(partial, "expert", pairs)
    x2, t1, t2, w, gate2, up2, cross = call(
        functools.partial(unpack_kernel, cap),
        (
            sds((slots, D), BF16),
            sds((slots, D), BF16),
            sds((slots, D), BF16),
            sds((2, slots, EXT), F32),
            sds((slots, FS), F32),
            sds((slots, FS), F32),
            sds((slots, slots), F32),
        ),
    )(own, other, gate, up, x1)
    cot, gate_first, up_first, partial2, hidden2, act2, slope_up2 = call(
        second_kernel,
        (
            sds((slots, D), BF16),
            sds((slots, FS), BF16),
            sds((slots, FS), BF16),
            sds((slots, D), F32),
            sds((slots, FS), BF16),
            sds((slots, FS), F32),
            sds((slots, FS), F32),
        ),
    )(partial, received, t1, w, down, act, slope_up, hidden1, gate2, up2, cross)
    received2 = lax.ppermute(partial2, "expert", pairs)
    base, down_part, frag2, hidden_frag2 = pl.pallas_call(
        fragment_kernel,
        out_shape=(
            sds((3, FRAG, D), F32),
            sds((FRAG, D), F32),
            sds((2, slots, FRAG), F32),
            sds((slots, FRAG), BF16),
        ),
        in_specs=[pl.BlockSpec(memory_space=pltpu.SMEM)]
        + [pl.BlockSpec(memory_space=pltpu.VMEM)] * 12,
        compiler_params=pltpu.CompilerParams(vmem_limit_bytes=56 * 1024 * 1024),
        cost_estimate=pl.CostEstimate(
            flops=1_000_000_000, bytes_accessed=8_000_000, transcendentals=0
        ),
    )(
        fragment_index, gate, up, down, x1, cot, gate_first, up_first, hidden1, hidden2, act2,
        slope_up2, global_fragment[0],
    )
    next_delta = call(last_kernel, sds((1, 1, 3, FRAG, D), F32))(
        partial2, received2, t2, w, x2, down_part, frag2, hidden_frag2, base
    )
    mean_delta = delta_total / replicas
    new_momentum = MOMENTUM * outer_momentum[0] + mean_delta
    new_global = global_fragment[0] - OUTER_RATE * (mean_delta + MOMENTUM * new_momentum)
    return (next_delta, new_global[None], new_momentum[None])


def solution(mesh):
    placed = (
        P(None, ("replica", "expert"), None),
        P(None, ("replica", "expert"), None),
        P(None, ("replica", "expert"), None),
        P(None, ("replica", "expert")),
        P("expert", None, None),
        P("expert", None, None),
        P("expert", None, None),
        P("replica", "expert", None, None, None),
        P("expert", None, None, None),
        P("expert", None, None, None),
        P(),
    )
    return jax.shard_map(
        shards,
        mesh=mesh,
        in_specs=placed,
        out_specs=(
            P("replica", "expert", None, None, None),
            P("expert", None, None, None),
            P("expert", None, None, None),
        ),
        check_vma=False,
    )
```

time: 593 us -> 482 us (0.81)
  waiting for transfers between devices: 437 us -> 372 us
  starting transfers between devices: 44.4 us -> 6.25 us
  Pallas kernels: 0 us -> 35.2 us
  matrix products: 25.2 us -> 0 us
  local copies, waits for them, and re-layouts: 29 us -> 5.01 us
  blocking collectives: 31.6 us -> 46.3 us
  other arithmetic: 9.71 us -> 2.35 us
    all_to_all x5 -> x0, waiting for transfers between devices: 124 us -> none  [the longest x2 84.5 us: gather_back(): lax.all_to_all(slice_rows, 'expert', split_axis=0, concat_axis=0, tiled=T...]
    psum x1, waiting for transfers between devices: 313 us -> 368 us  [replica_sum(): return lax.psum(delta, 'replica').astype(F32)]
    all_to_all x5 -> x0, starting transfers between devices: 44.2 us -> none  [the longest x3 26.5 us: deliver(): lax.all_to_all(doubled, 'expert', split_axis=0, concat_axis=0, tiled=True)]
    pallas_call x0 -> x6, Pallas kernels: none -> 35.2 us  [the longest x1 6.66 us: shards(): call(functools.partial(first_kernel, cap), (sds((slots, D), BF16), sds((s...]
    dot_general x23 -> x0, matrix products: 25.2 us -> none  [the longest x13 14.6 us: contract(): lax.dot_general(left_part, right_part, (((left_dim,), (right_dim,)), ((),...]
    all_to_all x1, blocking collectives: 31.6 us -> 46.3 us  [shards(): lax.all_to_all(table.reshape(experts, 4 * cap, D + EXT), 'expert', split_...]
    reshape x12 -> x0, local copies, waits for them, and re-layouts: 13.5 us -> none  [the longest x4 6.34 us: deliver(): return received.reshape(-1, row_width)]
    ppermute x0 -> x3, starting transfers between devices: none -> 6.21 us  [the longest x1 2.28 us: shards(): received2 = lax.ppermute(partial2, 'expert', pairs)]
  transfers between devices with their start and end apart: 6 -> 4, of which waited for: 5 -> 2; matrix products, arithmetic and copies ran while one was open for 5% -> 0% of each run, Pallas kernels for 0% -> 3%
where the time goes in v1:
time: 482 us; the launch traced here: 481 us
  waiting for transfers between devices  372 us (77%)
  blocking collectives  46.3 us (10%)
  Pallas kernels  35.2 us (7%)
  between operations  14.1 us (3%)
  starting transfers between devices  6.25 us (1%)
  local copies, waits for them, and re-layouts  5.01 us (1%)
    psum x1, waiting for transfers between devices, replica_sum(): return lax.psum(delta, 'replica').astype(F32)  368 us
    all_to_all x1, blocking collectives, shards(): lax.all_to_all(table.reshape(experts, 4 * cap, D + EXT), 'expert', split_...  46.3 us
  transfers between devices with their start and end apart: 4, of which 2 were waited for; matrix products, arithmetic and copies ran while one was open for 0% of the time, Pallas kernels for 3%

profile of v1, /device:TPU:56, one launch (start us, length us, event | category | flops | bytes accessed | tf_op | source)
XLA Modules:
  0.0 481.2 jit_solution(15112267457586170003)
XLA Ops:
  7.2 0.0 all-reduce.2.cloned.1.call-start
  7.2 1.4 copy.14.ids
  8.6 3.5 shard_map.130
  12.1 46.3 %all_to_all.5 = bf16[16,24,2176]{2,1,0:T(8,128)(2,1)S(1)} all-to-all(bf16[16,24,2176]{2,1,0:T(8,128)(2,1)} %bitcast.31), channel_id=1, replica_groups={{0,2,4,6,8,10,12,14,16,18,20,22,24,26,28,30},{1,3,5,7,9,11,13,15,17,19,..., dimensions={0} | all-to-all | bytes 3342336 | tf_op jit(solution)/shard_map/all_to_all | solution.py:248
  58.4 0.0 copy-start
  58.4 1.9 collective-permute-start
  60.3 3.5 collective-permute-done.other
  63.8 0.0 copy-start.1
  63.8 0.0 copy-done
  63.8 1.2 copy-done.1
  65.0 6.7 %shard_map.131 = (bf16[192,2048]{1,0:T(8,128)(2,1)}, f32[192,2048]{1,0:T(8,128)}, f32[192,384]{1,0:T(8,128)}, f32[192,384]{1,0:T(8,128)}, bf16[192,384]{1,0:T(8,128)(2,1)}) custom-call(bf16[384,2176]{1,0:T(8,128)(2,1)} %bitcast.19, bf16[384,2176]{1,0:T(8,128)(2,1)} %copy-done.1, bf16[2048,384]{1,0:T(8,128)(2,1)} %bitcast.21, bf16[2048,384]{1,0:T(8,128)(2,1)} %bitcast.24, ...), custom_call_target="tpu_custom_call" | custom-call | flops 1000000000 | bytes 8000000 | tf_op jit(solution)/shard_map/pallas_call | solution.py:259
  71.7 2.0 collective-permute-start.1
  73.7 6.6 %shard_map.132 = (bf16[192,2048]{1,0:T(8,128)(2,1)}, bf16[192,2048]{1,0:T(8,128)(2,1)}, bf16[192,2048]{1,0:T(8,128)(2,1)}, f32[2,192,128]{2,1,0:T(8,128)}, f32[1...) custom-call(bf16[384,2176]{1,0:T(8,128)(2,1)} %bitcast.20, bf16[384,2176]{1,0:T(8,128)(2,1)} %copy-done.1, ...), custom_call_target="tpu_custom_call" | custom-call | flops 1000000000 | bytes 8000000 | tf_op jit(solution)/shard_map/pallas_call | solution.py:270
  80.3 0.0 collective-permute-done.1.received
  80.3 0.0 copy-start.3
  80.3 1.2 copy-done.3
  81.6 0.0 copy-start.2
  81.6 0.0 copy-start.5
  81.6 6.6 %shard_map.133 = (bf16[192,2048]{1,0:T(8,128)(2,1)}, bf16[192,384]{1,0:T(8,128)(2,1)}, bf16[192,384]{1,0:T(8,128)(2,1)}, f32[192,2048]{1,0:T(8,128)}, bf16[192,3...) custom-call(f32[192,2048]{1,0:T(8,128)} %get-tuple-element.26.partial, f32[192,2048]{1,0:T(8,128)} %copy-done.3, ...), custom_call_target="tpu_custom_call" | custom-call | flops 1000000000 | bytes 8000000 | tf_op jit(solution)/shard_map/pallas_call | solution.py:282
  88.2 2.3 collective-permute-start.2
  90.5 0.0 all-reduce.2.cloned.1.call-update
  90.5 368.4 %all-reduce.2.cloned.1.call-done = bf16[3,32,2048]{2,1,0:T(8,128)(2,1)} async-done(((bf16[3,32,2048]{2,1,0:T(8,128)(2,1)}), bf16[3,32,2048]{2,1,0:T(8,128)(2,1)}) %all-reduce.2.cloned.1.call-update) | async-done | bytes 393232 | tf_op jit(solution)/shard_map/psum | solution.py:217
  458.9 0.0 copy-done.2
  458.9 0.0 copy-done.5
  458.9 2.3 fusion
  461.3 6.5 %shard_map.134 = (f32[3,32,2048]{2,1,0:T(8,128)}, f32[32,2048]{1,0:T(8,128)}, f32[2,192,32]{2,1,0:T(8,128)}, bf16[192,32]{1,0:T(8,128)(2,1)}) custom-call(s32[12]{0:T(128)} %index.1, bf16[2048,384]{1,0:T(8,128)(2,1)} %bitcast.23, bf16[2048,384]{1,0:T(8,128)(2,1)} %bitcast.26, bf16[384,2048]{1,0:T(8,128)(2,1)} %bitcast.29, ...), custom_call_target="tpu_custom_call" | custom-call | flops 1000000000 | bytes 8000000 | tf_op jit(solution)/shard_map/pallas_call | solution.py:295
  467.8 0.0 collective-permute-done.2.received
  467.8 0.0 copy-start.4
  467.8 1.1 copy-done.4
  468.9 5.4 %shard_map.135 = f32[1,1,3,32,2048]{4,3,2,1,0:T(8,128)} custom-call(f32[192,2048]{1,0:T(8,128)} %get-tuple-element.36.partial, f32[192,2048]{1,0:T(8,128)} %copy-done.4, bf16[192,2048]{1,0:T(8,128)(2,1)} %get-tuple-element.37.t2, f32[2,192,128]{2,1,0:T(8,128)} %get-tuple-element.29.w, bf16[192,2048]{1,0:T(8,128)(2,1)} %get-tuple-element.38.x2, ...), custom_call_target="tpu_custom_call" | custom-call | flops 1000000000 | bytes 8000000 | tf_op jit(solution)/shard_map/pallas_call | solution.py:313
Async XLA Ops:
  7.2 451.8 %all-reduce.2.cloned.1.call-start = ((), (), s32[]{:S(2)}) async-start(), calls=%async_computation.1 | async-start | bytes 786432 | tf_op jit(solution)/shard_map/psum | solution.py:217
  58.4 5.4 %copy-start = (bf16[16,24,2176]{2,1,0:T(8,128)(2,1)}, bf16[16,24,2176]{2,1,0:T(8,128)(2,1)S(1)}, u32[]{:S(2)}) copy-start(bf16[16,24,2176]{2,1,0:T(8,128)(2,1)S(1)} %all_to_all.5) | copy-start | bytes 5013508
  58.4 5.4 %collective-permute-start = (bf16[384,2176]{1,0:T(8,128)(2,1)S(1)}, bf16[384,2176]{1,0:T(8,128)(2,1)S(1)}, u32[]{:S(2)}, u32[]{:S(2)}) collective-permute-start(bf16[384,2176]{1,0:T(8,128)(2,1)S(1)} %bitcast.18), channel_id=1, source_target_pairs={{0,1},{1,0},{2,3},{3,2},{4,5},{5,4},{6,7},{7,6},{8,9},{9,8},{10,11... | collective-permute-start | bytes 5013512 | tf_op jit(solution)/shard_map/ppermute | solution.py:256
  63.8 1.2 copy-start.1
  71.7 8.6 %collective-permute-start.1 = (f32[192,2048]{1,0:T(8,128)}, f32[192,2048]{1,0:T(8,128)S(1)}, u32[]{:S(2)}, u32[]{:S(2)}) collective-permute-start(f32[192,2048]{1,0:T(8,128)} %get-tuple-element.26.partial), channel_id=1, source_target_pairs={{0,1},{1,0},{2,3},{3,2},{4,5},{5,4},{6,7},{7,6},{8,9},{9,8},{10,11... | collective-permute-start | bytes 4718600 | tf_op jit(solution)/shard_map/ppermute | solution.py:269
  80.3 1.3 copy-start.3
  81.6 377.4 %copy-start.2 = (f32[1,3,32,2048]{3,2,1,0:T(8,128)S(1)}, f32[1,3,32,2048]{3,2,1,0:T(8,128)}, u32[]{:S(2)}) copy-start(f32[1,3,32,2048]{3,2,1,0:T(8,128)} %param.19) | copy-start | bytes 2359300
  81.6 377.4 %copy-start.5 = (f32[1,3,32,2048]{3,2,1,0:T(8,128)S(1)}, f32[1,3,32,2048]{3,2,1,0:T(8,128)}, u32[]{:S(2)}) copy-start(f32[1,3,32,2048]{3,2,1,0:T(8,128)} %param.20) | copy-start | bytes 2359300
  88.2 379.6 %collective-permute-start.2 = (f32[192,2048]{1,0:T(8,128)}, f32[192,2048]{1,0:T(8,128)S(1)}, u32[]{:S(2)}, u32[]{:S(2)}) collective-permute-start(f32[192,2048]{1,0:T(8,128)} %get-tuple-element.36.partial), channel_id=1, source_target_pairs={{0,1},{1,0},{2,3},{3,2},{4,5},{5,4},{6,7},{7,6},{8,9},{9,8},{10,11... | collective-permute-start | bytes 4718600 | tf_op jit(solution)/shard_map/ppermute | solution.py:294
  467.8 1.2 copy-start.4
Sparse Core Ops, SparseCore 0:
  90.6 368.2 all-reduce.1

commit v2 on v1

--- a/solution.py
+++ b/solution.py
@@ -46,7 +46,7 @@
     return pre * sig, sig * (1.0 + pre * (1.0 - sig))
 
 
-def call(kernel, outs, limit=56, flops=1_000_000_000, bytes_accessed=8_000_000):
+def call(kernel, outs, limit=20, flops=1_000, bytes_accessed=8_000):
     return pl.pallas_call(
         kernel,
         out_shape=outs,
@@ -65,9 +65,9 @@
     rows = table.shape[0]
     count = 2 * tokens.shape[1]
     half = tokens.shape[1]
-    ids_col = ids[...].reshape(count, 1)
     first, second = iota((count, count), 0), iota((count, count), 1)
-    ids_row = jnp.sum(jnp.where(first == second, ids_col, 0), axis=0, keepdims=True)
+    ids_row = jnp.concatenate([ids[0], ids[1]], axis=1)
+    ids_col = jnp.sum(jnp.where(first == second, ids_row, 0), axis=1, keepdims=True)
     together = (first < half) == (second < half)
     earlier = (ids_col == ids_row) & (first < second) & together
     slot = jnp.sum(jnp.where(earlier, 1, 0), axis=0, keepdims=True)
@@ -104,7 +104,9 @@
     return (iota((rows, 4 * rows), 1) == wanted).astype(BF16)
 
 
-def first_kernel(cap, own, other, gate, up, down, x_out, partial, act, slope_up, hidden_out):
+def first_kernel(
+    cap, own, other, gate, up, down, x_out, partial, sent, act, slope_up, hidden_out
+):
     sources = own.shape[0] // (4 * cap)
     pick = picker(cap, sources, 0)
     half = sources * cap
@@ -118,7 +120,9 @@
     slope_up[...] = pre_up * slope
     hidden = (activated * pre_up).astype(BF16)
     hidden_out[...] = hidden
-    partial[...] = mm(hidden, down[...]) * SCALE_HIDDEN
+    result = mm(hidden, down[...]) * SCALE_HIDDEN
+    partial[...] = result
+    sent[...] = result.astype(BF16)
 
 
 def unpack_kernel(
@@ -146,13 +150,13 @@
 def cotangent(partial, received, target, weight):
     half = partial.shape[0] // 2
     swapped = jnp.concatenate([received[half:, :], received[:half, :]], axis=0)
-    combined = (partial + swapped).astype(BF16).astype(F32)
+    combined = (partial + swapped.astype(F32)).astype(BF16).astype(F32)
     return (weight * (weight * combined - target.astype(F32))).astype(BF16)
 
 
 def second_kernel(
     partial, received, t1, w, down, act, slope_up, hidden1, gate2, up2, cross,
-    cot_out, gate_first_out, up_first_out, partial2, hidden2_out, act2_out, slope_up2_out,
+    cot_out, gate_first_out, up_first_out, partial2, sent, hidden2_out, act2_out, slope_up2_out,
 ):
     cot = cotangent(partial[...], received[...], t1[...], w[0, :, 0:1])
     cot_out[...] = cot
@@ -170,9 +174,9 @@
     act2_out[...] = activated
     slope_up2_out[...] = pre_up * slope
     high, low = split_two(mm(hidden, hidden1[...], 1, 1))
-    partial2[...] = mm(hidden, down[...]) * SCALE_HIDDEN - SHRINK_HIDDEN * (
-        mm(high, cot) + mm(low, cot)
-    )
+    result = mm(hidden, down[...]) * SCALE_HIDDEN - SHRINK_HIDDEN * (mm(high, cot) + mm(low, cot))
+    partial2[...] = result
+    sent[...] = result.astype(BF16)
 
 
 def fragment_kernel(
@@ -213,8 +217,65 @@
     out[0, 0, 2] = base[2] + INNER_RATE * (mm(hidden_frag2[...], cot, 0, 0) * SCALE_HIDDEN)
 
 
-def replica_sum(delta):
-    return lax.psum(delta, "replica").astype(F32)
+def inner_of(replicas):
+    return min(replicas, 8)
+
+
+def outer_of(replicas):
+    return min(replicas, 16)
+
+
+def lane_of(place, inner, lanes):
+    lane = 0
+    while inner > 1:
+        lanes //= 2
+        lane += place % 2 * lanes
+        place //= 2
+        inner //= 2
+    return lane
+
+
+def halve(values, distance):
+    replicas = lax.axis_size("replica")
+    half = values.shape[1] // 2
+    bit = lax.bitwise_and(lax.axis_index("replica") // distance, 1)
+    sent = lax.dynamic_slice_in_dim(values, (1 - bit) * half, half, 1)
+    kept = lax.dynamic_slice_in_dim(values, bit * half, half, 1)
+    if half > 256:
+        sent = sent.astype(BF16)
+    got = lax.ppermute(sent, "replica", [(i, i ^ distance) for i in range(replicas)])
+    return kept, got
+
+
+def scatter_sum(values, inner, span):
+    distance = 2
+    while distance < inner:
+        kept, got = halve(values, distance)
+        values = kept + got.astype(F32)
+        distance *= 2
+    replicas = lax.axis_size("replica")
+    distance = span
+    while distance < replicas:
+        got = lax.ppermute(values, "replica", [(i, i ^ distance) for i in range(replicas)])
+        values = values + got
+        distance *= 2
+    return values.astype(BF16)
+
+
+def outer_kernel(replicas, pieces, global_fragment, momentum, new_global, new_momentum):
+    span, _, width = pieces.shape
+    lanes = global_fragment.shape[1]
+    inner = lanes // width
+    for place in range(inner):
+        lane = lane_of(place, inner, lanes)
+        at = (slice(None), slice(lane, lane + width))
+        total = pieces[place].astype(F32)
+        for other in range(place + inner, span, inner):
+            total += pieces[other].astype(F32)
+        mean = total * (1.0 / replicas)
+        moved = MOMENTUM * momentum[at] + mean
+        new_momentum[at] = moved
+        new_global[at] = global_fragment[at] - OUTER_RATE * (mean + MOMENTUM * moved)
 
 
 def shards(
@@ -240,11 +301,14 @@
     same_core = [[2 * e + c for e in range(experts)] for c in range(2)]
     pairs = [(i, i ^ 1) for i in range(size)]
 
-    delta_total = replica_sum(fragment_delta[0, 0])
-
-    table = call(functools.partial(pack_kernel, cap), sds((rows, D + EXT), BF16))(
-        tokens, targets, expert_ids, route_weight
-    )
+    inner, span = inner_of(replicas), outer_of(replicas)
+    kept, got = halve(fragment_delta.reshape(3 * FRAG, D), 1)
+
+    table = call(functools.partial(pack_kernel, cap), sds((rows, D + EXT), BF16), 56)(
+        tokens, targets, expert_ids.transpose(0, 2, 1), route_weight
+    )
+    table, got = lax.optimization_barrier((table, got))
+    piece = scatter_sum(kept.astype(F32) + got.astype(F32), inner, span)
     own = lax.all_to_all(
         table.reshape(experts, 4 * cap, D + EXT),
         "expert",
@@ -253,20 +317,32 @@
         tiled=True,
         axis_index_groups=same_core,
     ).reshape(rows, D + EXT)
+    own, piece = lax.optimization_barrier((own, piece))
+    pieces = lax.all_to_all(
+        jnp.broadcast_to(piece[None], (span,) + piece.shape),
+        "replica",
+        split_axis=0,
+        concat_axis=0,
+        tiled=True,
+        axis_index_groups=[
+            list(range(start, start + span)) for start in range(0, replicas, span)
+        ],
+    )
     other = lax.ppermute(own, "expert", pairs)
     gate, up, down = gate_weight[0], up_weight[0], down_weight[0]
 
-    x1, partial, act, slope_up, hidden1 = call(
+    x1, partial, sent, act, slope_up, hidden1 = call(
         functools.partial(first_kernel, cap),
         (
             sds((slots, D), BF16),
             sds((slots, D), F32),
+            sds((slots, D), BF16),
             sds((slots, FS), F32),
             sds((slots, FS), F32),
             sds((slots, FS), BF16),
         ),
     )(own, other, gate, up, down)
-    received = lax.ppermute(partial, "expert", pairs)
+    received = lax.ppermute(sent, "expert", pairs)
     x2, t1, t2, w, gate2, up2, cross = call(
         functools.partial(unpack_kernel, cap),
         (
@@ -279,19 +355,20 @@
             sds((slots, slots), F32),
         ),
     )(own, other, gate, up, x1)
-    cot, gate_first, up_first, partial2, hidden2, act2, slope_up2 = call(
+    cot, gate_first, up_first, partial2, sent2, hidden2, act2, slope_up2 = call(
         second_kernel,
         (
             sds((slots, D), BF16),
             sds((slots, FS), BF16),
             sds((slots, FS), BF16),
             sds((slots, D), F32),
+            sds((slots, D), BF16),
             sds((slots, FS), BF16),
             sds((slots, FS), F32),
             sds((slots, FS), F32),
         ),
     )(partial, received, t1, w, down, act, slope_up, hidden1, gate2, up2, cross)
-    received2 = lax.ppermute(partial2, "expert", pairs)
+    received2 = lax.ppermute(sent2, "expert", pairs)
     base, down_part, frag2, hidden_frag2 = pl.pallas_call(
         fragment_kernel,
         out_shape=(
@@ -302,9 +379,9 @@
         ),
         in_specs=[pl.BlockSpec(memory_space=pltpu.SMEM)]
         + [pl.BlockSpec(memory_space=pltpu.VMEM)] * 12,
-        compiler_params=pltpu.CompilerParams(vmem_limit_bytes=56 * 1024 * 1024),
+        compiler_params=pltpu.CompilerParams(vmem_limit_bytes=20 * 1024 * 1024),
         cost_estimate=pl.CostEstimate(
-            flops=1_000_000_000, bytes_accessed=8_000_000, transcendentals=0
+            flops=1_000, bytes_accessed=8_000, transcendentals=0
         ),
     )(
         fragment_index, gate, up, down, x1, cot, gate_first, up_first, hidden1, hidden2, act2,
@@ -313,10 +390,13 @@
     next_delta = call(last_kernel, sds((1, 1, 3, FRAG, D), F32))(
         partial2, received2, t2, w, x2, down_part, frag2, hidden_frag2, base
     )
-    mean_delta = delta_total / replicas
-    new_momentum = MOMENTUM * outer_momentum[0] + mean_delta
-    new_global = global_fragment[0] - OUTER_RATE * (mean_delta + MOMENTUM * new_momentum)
-    return (next_delta, new_global[None], new_momentum[None])
+    next_delta, pieces = lax.optimization_barrier((next_delta, pieces))
+    new_global, new_momentum = call(
+        functools.partial(outer_kernel, replicas),
+        (sds((3 * FRAG, D), F32), sds((3 * FRAG, D), F32)),
+    )(pieces, global_fragment.reshape(3 * FRAG, D), outer_momentum.reshape(3 * FRAG, D))
+    whole = (1, 3, FRAG, D)
+    return (next_delta, new_global.reshape(whole), new_momentum.reshape(whole))
 
 
 def solution(mesh):

time: 482 us -> 127 us (0.26)
  the two profiles are of different devices: /device:TPU:56 before, /device:TPU:64 now
where the time goes in v2:
time: 127 us; the launch traced here: 126 us
  starting transfers between devices  56.8 us (45%)
  waiting for transfers between devices  40.6 us (32%)
  Pallas kernels  22 us (17%)
  local copies, waits for them, and re-layouts  4.8 us (4%)
    ppermute x3, starting transfers between devices, halve(): lax.ppermute(sent, 'replica', [(i, i ^ distance) for i in range(replicas)])  23.2 us
    all_to_all x1, starting transfers between devices, shards(): lax.all_to_all(jnp.broadcast_to(piece[None], (span,) + piece.shape), 'rep...  18.4 us
    all_to_all x1, waiting for transfers between devices, shards(): lax.all_to_all(jnp.broadcast_to(piece[None], (span,) + piece.shape), 'rep...  16.7 us
    ppermute x3, waiting for transfers between devices, halve(): lax.ppermute(sent, 'replica', [(i, i ^ distance) for i in range(replicas)])  11.5 us
    all_to_all x1, waiting for transfers between devices, shards(): lax.all_to_all(table.reshape(experts, 4 * cap, D + EXT), 'expert', split_...  6.65 us
    ppermute x1, waiting for transfers between devices, scatter_sum(): lax.ppermute(values, 'replica', [(i, i ^ distance) for i in range(replica...  5.72 us
    ppermute x1, starting transfers between devices, scatter_sum(): lax.ppermute(values, 'replica', [(i, i ^ distance) for i in range(replica...  4.89 us
    pallas_call x1, Pallas kernels, shards(): call(functools.partial(unpack_kernel, cap), (sds((slots, D), BF16), sds((...  4.3 us
  transfers between devices with their start and end apart: 9, of which 5 were waited for; matrix products, arithmetic and copies ran while one was open for 2% of the time, Pallas kernels for 15%

profile of v2, /device:TPU:64, one launch (start us, length us, event | category | flops | bytes accessed | tf_op | source)
XLA Modules:
  0.0 126.1 jit_solution(262128049390060919)
XLA Ops:
  0.6 0.9 constant_dynamic-slice_fusion.1
  1.6 14.2 %collective-permute-start = (bf16[96,1024]{1,0:T(8,128)(2,1)S(1)}, bf16[96,1024]{1,0:T(8,128)(2,1)S(1)}, u32[]{:S(2)}, u32[]{:S(2)}) collective-permute-start(bf16[96,1024]{1,0:T(8,128)(2,1)S(1)} %constant_dynamic-slice_fusion.1), channel_id=1, source_target_pairs={{0,32},{32,0},{64,96},{96,64},{128,160},{160,128},{192,224},{224,1... | collective-permute-start | bytes 589832 | tf_op jit(solution)/shard_map/ppermute | solution.py:246
  15.8 3.6 %shard_map.130 = bf16[384,2176]{1,0:T(8,128)(2,1)} custom-call(bf16[2,64,2048]{2,1,0:T(8,128)(2,1)} %tokens.1, bf16[2,64,2048]{2,1,0:T(8,128)(2,1)} %targets.1, s32[2,1,64]{2,1,0:T(1,128)} %bitcast.32, f32[2,64]{1,0:T(2,128)} %weight.1), custom_call_target="tpu_custom_call" | custom-call | flops 1000 | bytes 8000 | tf_op jit(solution)/shard_map/pallas_call | solution.py:307
  19.4 0.0 collective-permute-done
  19.4 3.8 %all-to-all-start = ((bf16[16,24,2176]{2,1,0:T(8,128)(2,1)}), bf16[16,24,2176]{2,1,0:T(8,128)(2,1)S(1)}, u32[]{:S(2)}, u32[]{:S(2)}) async-start(bf16[16,24,2176]{2,1,0:T(8,128)(2,1)} %bitcast.29), calls=%async_computation | async-start | bytes 3342336 | tf_op jit(solution)/shard_map/all_to_all | solution.py:312
  23.4 1.9 %collective-permute-start.1 = (bf16[96,512]{1,0:T(8,128)(2,1)S(1)}, bf16[96,512]{1,0:T(8,128)(2,1)S(1)}, u32[]{:S(2)}, u32[]{:S(2)}) collective-permute-start(bf16[96,512]{1,0:T(8,128)(2,1)S(1)} %dynamic-slice_convert_fusion), channel_id=1, source_target_pairs={{0,64},{32,96},{64,0},{96,32},{128,192},{160,224},{192,128},{224,1... | collective-permute-start | bytes 294920 | tf_op jit(solution)/shard_map/ppermute | solution.py:246
  25.4 5.5 %collective-permute-done.1 = bf16[96,512]{1,0:T(8,128)(2,1)S(1)} collective-permute-done((bf16[96,512]{1,0:T(8,128)(2,1)S(1)}, bf16[96,512]{1,0:T(8,128)(2,1)S(1)}, u32[]{:S(2)}, u32[]{:S(2)}) %collective-permute-start.1) | collective-permute-done | bytes 98336 | tf_op jit(solution)/shard_map/ppermute | solution.py:246
  30.9 0.0 copy-start
  30.9 7.1 %collective-permute-start.2 = (f32[96,256]{1,0:T(8,128)S(1)}, f32[96,256]{1,0:T(8,128)}, u32[]{:S(2)}, u32[]{:S(2)}) collective-permute-start(f32[96,256]{1,0:T(8,128)S(1)} %constant_dynamic-slice_fusion), channel_id=1, source_target_pairs={{0,128},{32,160},{64,192},{96,224},{128,0},{160,32},{192,64},{224,... | collective-permute-start | bytes 294920 | tf_op jit(solution)/shard_map/ppermute | solution.py:246
  38.0 6.0 %collective-permute-done.2 = f32[96,256]{1,0:T(8,128)} collective-permute-done((f32[96,256]{1,0:T(8,128)S(1)}, f32[96,256]{1,0:T(8,128)}, u32[]{:S(2)}, u32[]{:S(2)}) %collective-permute-start.2) | collective-permute-done | bytes 98336 | tf_op jit(solution)/shard_map/ppermute | solution.py:246
  44.0 0.9 dynamic-slice_add_fusion
  44.9 4.9 %collective-permute-start.3 = (f32[96,256]{1,0:T(8,128)S(1)}, f32[96,256]{1,0:T(8,128)S(1)}, u32[]{:S(2)}, u32[]{:S(2)}) collective-permute-start(f32[96,256]{1,0:T(8,128)S(1)} %dynamic-slice_add_fusion), channel_id=1, source_target_pairs={{0,512},{32,544},{64,576},{96,608},{128,640},{160,672},{192,704},{... | collective-permute-start | bytes 294920 | tf_op jit(solution)/shard_map/ppermute | solution.py:259
  49.8 5.7 %collective-permute-done.3 = f32[96,256]{1,0:T(8,128)S(1)} collective-permute-done((f32[96,256]{1,0:T(8,128)S(1)}, f32[96,256]{1,0:T(8,128)S(1)}, u32[]{:S(2)}, u32[]{:S(2)}) %collective-permute-start.3) | collective-permute-done | bytes 98336 | tf_op jit(solution)/shard_map/ppermute | solution.py:259
  55.6 6.6 %all-to-all-done = bf16[16,24,2176]{2,1,0:T(8,128)(2,1)S(1)} async-done(((bf16[16,24,2176]{2,1,0:T(8,128)(2,1)}), bf16[16,24,2176]{2,1,0:T(8,128)(2,1)S(1)}, u32[]{:S(2)}, u32[]{:S(2)}) %all-to-all-start) | async-done | bytes 1671200 | tf_op jit(solution)/shard_map/all_to_all | solution.py:312
  62.2 1.9 %collective-permute-start.4 = (bf16[384,2176]{1,0:T(8,128)(2,1)S(1)}, bf16[384,2176]{1,0:T(8,128)(2,1)}, u32[]{:S(2)}, u32[]{:S(2)}) collective-permute-start(bf16[384,2176]{1,0:T(8,128)(2,1)S(1)} %bitcast.14), channel_id=1, source_target_pairs={{0,1},{1,0},{2,3},{3,2},{4,5},{5,4},{6,7},{7,6},{8,9},{9,8},{10,11... | collective-permute-start | bytes 5013512 | tf_op jit(solution)/shard_map/ppermute | solution.py:331
  64.1 1.0 broadcast_in_dim.2
  65.1 18.4 %all-to-all-start.1 = ((bf16[16,96,256]{2,1,0:T(8,128)(2,1)}), bf16[16,96,256]{2,1,0:T(8,128)(2,1)}, u32[]{:S(2)}, u32[]{:S(2)}) async-start(bf16[16,96,256]{2,1,0:T(8,128)(2,1)} %broadcast_in_dim.2), calls=%async_computation.1 | async-start | bytes 1572864 | tf_op jit(solution)/shard_map/all_to_all | solution.py:321
  83.5 0.0 copy-start.1
  83.5 1.4 %copy-done.1 = bf16[1,2048,384]{2,1,0:T(8,128)(2,1)S(1)} copy-done((bf16[1,2048,384]{2,1,0:T(8,128)(2,1)S(1)}, bf16[1,2048,384]{2,1,0:T(8,128)(2,1)}, u32[]{:S(2)}) %copy-start.1) | copy-done | bytes 1572888
  84.9 1.4 %copy-done.3 = bf16[1,384,2048]{2,1,0:T(8,128)(2,1)S(1)} copy-done((bf16[1,384,2048]{2,1,0:T(8,128)(2,1)S(1)}, bf16[1,384,2048]{2,1,0:T(8,128)(2,1)}, u32[]{:S(2)}) %copy-start.3) | copy-done | bytes 1572888
  86.3 3.5 %shard_map.131 = (bf16[192,2048]{1,0:T(8,128)(2,1)S(1)}, f32[192,2048]{1,0:T(8,128)S(1)}, bf16[192,2048]{1,0:T(8,128)(2,1)S(1)}, f32[192,384]{1,0:T(8,128)S(1)},...) custom-call(bf16[384,2176]{1,0:T(8,128)(2,1)S(1)} %bitcast.15, bf16[384,2176]{1,0:T(8,128)(2,1)} %collective-permute-done.4.other, ...), custom_call_target="tpu_custom_call" | custom-call | flops 1000 | bytes 8000 | tf_op jit(solution)/shard_map/pallas_call | solution.py:334
  89.9 1.9 %collective-permute-start.5 = (bf16[192,2048]{1,0:T(8,128)(2,1)S(1)}, bf16[192,2048]{1,0:T(8,128)(2,1)S(1)}, u32[]{:S(2)}, u32[]{:S(2)}) collective-permute-start(bf16[192,2048]{1,0:T(8,128)(2,1)S(1)} %get-tuple-element.40), channel_id=1, source_target_pairs={{0,1},{1,0},{2,3},{3,2},{4,5},{5,4},{6,7},{7,6},{8,9},{9,8},{10,11... | collective-permute-start | bytes 2359304 | tf_op jit(solution)/shard_map/ppermute | solution.py:345
  91.8 0.0 copy-start.4
  91.8 4.3 %shard_map.132 = (bf16[192,2048]{1,0:T(8,128)(2,1)S(1)}, bf16[192,2048]{1,0:T(8,128)(2,1)S(1)}, bf16[192,2048]{1,0:T(8,128)(2,1)S(1)}, f32[2,192,128]{2,1,0:T(8,...) custom-call(bf16[384,2176]{1,0:T(8,128)(2,1)S(1)} %bitcast.16, ...), custom_call_target="tpu_custom_call" | custom-call | flops 1000 | bytes 8000 | tf_op jit(solution)/shard_map/pallas_call | solution.py:346
  96.1 0.0 copy-start.7
  96.2 2.2 %shard_map.133 = (bf16[192,2048]{1,0:T(8,128)(2,1)S(1)}, bf16[192,384]{1,0:T(8,128)(2,1)S(1)}, bf16[192,384]{1,0:T(8,128)(2,1)S(1)}, f32[192,2048]{1,0:T(8,128)S...) custom-call(f32[192,2048]{1,0:T(8,128)S(1)} %get-tuple-element.39.pa, ...), custom_call_target="tpu_custom_call" | custom-call | flops 1000 | bytes 8000 | tf_op jit(solution)/shard_map/pallas_call | solution.py:358
  98.4 2.6 %collective-permute-start.6 = (bf16[192,2048]{1,0:T(8,128)(2,1)S(1)}, bf16[192,2048]{1,0:T(8,128)(2,1)S(1)}, u32[]{:S(2)}, u32[]{:S(2)}) collective-permute-start(bf16[192,2048]{1,0:T(8,128)(2,1)S(1)} %get-tuple-element.51), channel_id=1, source_target_pairs={{0,1},{1,0},{2,3},{3,2},{4,5},{5,4},{6,7},{7,6},{8,9},{9,8},{10,11... | collective-permute-start | bytes 2359304 | tf_op jit(solution)/shard_map/ppermute | solution.py:371
  101.0 3.0 %shard_map.134 = (f32[3,32,2048]{2,1,0:T(8,128)S(1)}, f32[32,2048]{1,0:T(8,128)S(1)}, f32[2,192,32]{2,1,0:T(8,128)S(1)}, bf16[192,32]{1,0:T(8,128)(2,1)S(1)}) custom-call(s32[12]{0:T(128)S(1)} %copy-done.7, bf16[2048,384]{1,0:T(8,128)(2,1)S(1)} %bitcast.19, bf16[2048,384]{1,0:T(8,128)(2,1)S(1)} %bitcast.22, bf16[384,2048]{1,0:T(8,128)(2,1)S(1)} %bitcast.25, ...), custom_call_target="tpu_custom_call" | custom-call | flops 1000 | bytes 8000 | tf_op jit(solution)/shard_map/pallas_call | solution.py:372
  104.1 0.0 copy-start.6
  104.1 2.7 %shard_map.135 = f32[1,1,3,32,2048]{4,3,2,1,0:T(8,128)} custom-call(f32[192,2048]{1,0:T(8,128)S(1)} %get-tuple-element.50.partial, bf16[192,2048]{1,0:T(8,128)(2,1)S(1)} %collective-permute-done.6.received, bf16[192,2048]{1,0:T(8,128)(2,1)S(1)} %get-tuple-element.52.t2, f32[2,192,128]{2,1,0:T(8,128)S(1)} %get-tuple-element.43.w, ...), custom_call_target="tpu_custom_call" | custom-call | flops 1000 | bytes 8000 | tf_op jit(solution)/shard_map/pallas_call | solution.py:390
  106.8 16.7 %all-to-all-done.1.pieces = bf16[16,96,256]{2,1,0:T(8,128)(2,1)} async-done(((bf16[16,96,256]{2,1,0:T(8,128)(2,1)}), bf16[16,96,256]{2,1,0:T(8,128)(2,1)}, u32[]{:S(2)}, u32[]{:S(2)}) %all-to-all-start.1) | async-done | bytes 786464 | tf_op jit(solution)/shard_map/all_to_all | solution.py:321
  123.5 2.5 %shard_map.136 = (f32[96,2048]{1,0:T(8,128)}, f32[96,2048]{1,0:T(8,128)}) custom-call(bf16[16,96,256]{2,1,0:T(8,128)(2,1)} %all-to-all-done.1.pieces, f32[96,2048]{1,0:T(8,128)S(1)} %bitcast.27, f32[96,2048]{1,0:T(8,128)S(1)} %bitcast.28), custom_call_target="tpu_custom_call" | custom-call | flops 1000 | bytes 8000 | tf_op jit(solution)/shard_map/pallas_call | solution.py:394
  (19 shorter events, 0.2 us)
Async XLA Ops:
  1.6 17.9 %collective-permute-start = (bf16[96,1024]{1,0:T(8,128)(2,1)S(1)}, bf16[96,1024]{1,0:T(8,128)(2,1)S(1)}, u32[]{:S(2)}, u32[]{:S(2)}) collective-permute-start(bf16[96,1024]{1,0:T(8,128)(2,1)S(1)} %constant_dynamic-slice_fusion.1), channel_id=1, source_target_pairs={{0,32},{32,0},{64,96},{96,64},{128,160},{160,128},{192,224},{224,1... | collective-permute-start | bytes 589832 | tf_op jit(solution)/shard_map/ppermute | solution.py:246
  19.4 3.9 %copy-start.8 = (bf16[1,1,3,32,2048]{4,3,2,1,0:T(8,128)(2,1)S(1)}, bf16[1,1,3,32,2048]{4,3,2,1,0:T(8,128)(2,1)}, u32[]{:S(2)}) copy-start(bf16[1,1,3,32,2048]{4,3,2,1,0:T(8,128)(2,1)} %param.18) | copy-start | bytes 1179652
  19.4 42.8 %all-to-all-start = ((bf16[16,24,2176]{2,1,0:T(8,128)(2,1)}), bf16[16,24,2176]{2,1,0:T(8,128)(2,1)S(1)}, u32[]{:S(2)}, u32[]{:S(2)}) async-start(bf16[16,24,2176]{2,1,0:T(8,128)(2,1)} %bitcast.29), calls=%async_computation | async-start | bytes 3342336 | tf_op jit(solution)/shard_map/all_to_all | solution.py:312
  23.4 7.5 %collective-permute-start.1 = (bf16[96,512]{1,0:T(8,128)(2,1)S(1)}, bf16[96,512]{1,0:T(8,128)(2,1)S(1)}, u32[]{:S(2)}, u32[]{:S(2)}) collective-permute-start(bf16[96,512]{1,0:T(8,128)(2,1)S(1)} %dynamic-slice_convert_fusion), channel_id=1, source_target_pairs={{0,64},{32,96},{64,0},{96,32},{128,192},{160,224},{192,128},{224,1... | collective-permute-start | bytes 294920 | tf_op jit(solution)/shard_map/ppermute | solution.py:246
  30.9 52.6 %copy-start = (bf16[1,2048,384]{2,1,0:T(8,128)(2,1)S(1)}, bf16[1,2048,384]{2,1,0:T(8,128)(2,1)}, u32[]{:S(2)}) copy-start(bf16[1,2048,384]{2,1,0:T(8,128)(2,1)} %param.15) | copy-start | bytes 4718596
  30.9 13.1 %collective-permute-start.2 = (f32[96,256]{1,0:T(8,128)S(1)}, f32[96,256]{1,0:T(8,128)}, u32[]{:S(2)}, u32[]{:S(2)}) collective-permute-start(f32[96,256]{1,0:T(8,128)S(1)} %constant_dynamic-slice_fusion), channel_id=1, source_target_pairs={{0,128},{32,160},{64,192},{96,224},{128,0},{160,32},{192,64},{224,... | collective-permute-start | bytes 294920 | tf_op jit(solution)/shard_map/ppermute | solution.py:246
  44.9 10.6 %collective-permute-start.3 = (f32[96,256]{1,0:T(8,128)S(1)}, f32[96,256]{1,0:T(8,128)S(1)}, u32[]{:S(2)}, u32[]{:S(2)}) collective-permute-start(f32[96,256]{1,0:T(8,128)S(1)} %dynamic-slice_add_fusion), channel_id=1, source_target_pairs={{0,512},{32,544},{64,576},{96,608},{128,640},{160,672},{192,704},{... | collective-permute-start | bytes 294920 | tf_op jit(solution)/shard_map/ppermute | solution.py:259
  62.2 21.3 %collective-permute-start.4 = (bf16[384,2176]{1,0:T(8,128)(2,1)S(1)}, bf16[384,2176]{1,0:T(8,128)(2,1)}, u32[]{:S(2)}, u32[]{:S(2)}) collective-permute-start(bf16[384,2176]{1,0:T(8,128)(2,1)S(1)} %bitcast.14), channel_id=1, source_target_pairs={{0,1},{1,0},{2,3},{3,2},{4,5},{5,4},{6,7},{7,6},{8,9},{9,8},{10,11... | collective-permute-start | bytes 5013512 | tf_op jit(solution)/shard_map/ppermute | solution.py:331
  65.1 58.4 %all-to-all-start.1 = ((bf16[16,96,256]{2,1,0:T(8,128)(2,1)}), bf16[16,96,256]{2,1,0:T(8,128)(2,1)}, u32[]{:S(2)}, u32[]{:S(2)}) async-start(bf16[16,96,256]{2,1,0:T(8,128)(2,1)} %broadcast_in_dim.2), calls=%async_computation.1 | async-start | bytes 1572864 | tf_op jit(solution)/shard_map/all_to_all | solution.py:321
  83.5 1.4 %copy-start.1 = (bf16[1,2048,384]{2,1,0:T(8,128)(2,1)S(1)}, bf16[1,2048,384]{2,1,0:T(8,128)(2,1)}, u32[]{:S(2)}) copy-start(bf16[1,2048,384]{2,1,0:T(8,128)(2,1)} %param.16) | copy-start | bytes 4718596
  84.9 1.4 %copy-start.3 = (bf16[1,384,2048]{2,1,0:T(8,128)(2,1)S(1)}, bf16[1,384,2048]{2,1,0:T(8,128)(2,1)}, u32[]{:S(2)}) copy-start(bf16[1,384,2048]{2,1,0:T(8,128)(2,1)} %param.17) | copy-start | bytes 4718596
  89.9 6.3 %collective-permute-start.5 = (bf16[192,2048]{1,0:T(8,128)(2,1)S(1)}, bf16[192,2048]{1,0:T(8,128)(2,1)S(1)}, u32[]{:S(2)}, u32[]{:S(2)}) collective-permute-start(bf16[192,2048]{1,0:T(8,128)(2,1)S(1)} %get-tuple-element.40), channel_id=1, source_target_pairs={{0,1},{1,0},{2,3},{3,2},{4,5},{5,4},{6,7},{7,6},{8,9},{9,8},{10,11... | collective-permute-start | bytes 2359304 | tf_op jit(solution)/shard_map/ppermute | solution.py:345
  91.8 4.3 %copy-start.4 = (bf16[1,384,2048]{2,1,0:T(8,128)(2,1)S(1)}, bf16[1,384,2048]{2,1,0:T(8,128)(2,1)}, u32[]{:S(2)}) copy-start(bf16[1,384,2048]{2,1,0:T(8,128)(2,1)} %param.17) | copy-start | bytes 4718596
  96.1 4.9 %copy-start.2 = (bf16[1,2048,384]{2,1,0:T(8,128)(2,1)S(1)}, bf16[1,2048,384]{2,1,0:T(8,128)(2,1)}, u32[]{:S(2)}) copy-start(bf16[1,2048,384]{2,1,0:T(8,128)(2,1)} %param.16) | copy-start | bytes 4718596
  96.1 4.9 %copy-start.5 = (f32[1,3,32,2048]{3,2,1,0:T(8,128)S(1)}, f32[1,3,32,2048]{3,2,1,0:T(8,128)}, u32[]{:S(2)}) copy-start(f32[1,3,32,2048]{3,2,1,0:T(8,128)} %param.19) | copy-start | bytes 2359300
  96.1 4.9 %copy-start.7 = (s32[12]{0:T(128)S(1)}, s32[12]{0:T(128)}, u32[]{:S(2)}) copy-start(s32[12]{0:T(128)} %index.1) | copy-start | bytes 148
  98.4 5.7 %collective-permute-start.6 = (bf16[192,2048]{1,0:T(8,128)(2,1)S(1)}, bf16[192,2048]{1,0:T(8,128)(2,1)S(1)}, u32[]{:S(2)}, u32[]{:S(2)}) collective-permute-start(bf16[192,2048]{1,0:T(8,128)(2,1)S(1)} %get-tuple-element.51), channel_id=1, source_target_pairs={{0,1},{1,0},{2,3},{3,2},{4,5},{5,4},{6,7},{7,6},{8,9},{9,8},{10,11... | collective-permute-start | bytes 2359304 | tf_op jit(solution)/shard_map/ppermute | solution.py:371
  104.1 19.4 %copy-start.6 = (f32[1,3,32,2048]{3,2,1,0:T(8,128)S(1)}, f32[1,3,32,2048]{3,2,1,0:T(8,128)}, u32[]{:S(2)}) copy-start(f32[1,3,32,2048]{3,2,1,0:T(8,128)} %param.20) | copy-start | bytes 2359300

commit v3 on v2

--- a/solution.py
+++ b/solution.py
@@ -46,7 +46,7 @@
     return pre * sig, sig * (1.0 + pre * (1.0 - sig))
 
 
-def call(kernel, outs, limit=20, flops=1_000, bytes_accessed=8_000):
+def call(kernel, outs, limit=20, flops=1_000_000_000, bytes_accessed=10_000_000):
     return pl.pallas_call(
         kernel,
         out_shape=outs,
@@ -221,58 +221,48 @@
     return min(replicas, 8)
 
 
-def outer_of(replicas):
-    return min(replicas, 16)
-
-
-def lane_of(place, inner, lanes):
-    lane = 0
-    while inner > 1:
-        lanes //= 2
-        lane += place % 2 * lanes
-        place //= 2
-        inner //= 2
-    return lane
+def mask_of(distance):
+    return 12 if distance == 8 else distance
+
+
+def pick_of(place, distance):
+    bit = (place // distance) & 1
+    return bit ^ ((place // 8) & 1) if distance == 4 else bit
+
+
+def swap(values, distance):
+    replicas = lax.axis_size("replica")
+    return lax.ppermute(values, "replica", [(i, i ^ distance) for i in range(replicas)])
 
 
 def halve(values, distance):
-    replicas = lax.axis_size("replica")
     half = values.shape[1] // 2
-    bit = lax.bitwise_and(lax.axis_index("replica") // distance, 1)
+    bit = pick_of(lax.axis_index("replica"), distance)
     sent = lax.dynamic_slice_in_dim(values, (1 - bit) * half, half, 1)
     kept = lax.dynamic_slice_in_dim(values, bit * half, half, 1)
-    if half > 256:
-        sent = sent.astype(BF16)
-    got = lax.ppermute(sent, "replica", [(i, i ^ distance) for i in range(replicas)])
-    return kept, got
-
-
-def scatter_sum(values, inner, span):
-    distance = 2
-    while distance < inner:
-        kept, got = halve(values, distance)
-        values = kept + got.astype(F32)
-        distance *= 2
-    replicas = lax.axis_size("replica")
-    distance = span
-    while distance < replicas:
-        got = lax.ppermute(values, "replica", [(i, i ^ distance) for i in range(replicas)])
-        values = values + got
-        distance *= 2
-    return values.astype(BF16)
-
-
-def outer_kernel(replicas, pieces, global_fragment, momentum, new_global, new_momentum):
-    span, _, width = pieces.shape
-    lanes = global_fragment.shape[1]
-    inner = lanes // width
-    for place in range(inner):
-        lane = lane_of(place, inner, lanes)
-        at = (slice(None), slice(lane, lane + width))
-        total = pieces[place].astype(F32)
-        for other in range(place + inner, span, inner):
-            total += pieces[other].astype(F32)
-        mean = total * (1.0 / replicas)
+    return kept, swap(sent.astype(BF16), distance)
+
+
+def add_across(values, distance):
+    mine = values.astype(BF16)
+    return mine.astype(F32) + swap(mine, mask_of(distance)).astype(F32)
+
+
+def outer_kernel(replicas, marks, me, held_pieces, got_pieces, global_fragment, momentum,
+                 new_global, new_momentum):
+    rows, lanes = global_fragment.shape
+    width = held_pieces.shape[1]
+    here = len(marks) // 2 if len(marks) > 1 else 1
+    for j, mark in enumerate(marks):
+        place = me[0] ^ mark
+        lane, step, distance = 0, lanes // 2, 1
+        while step >= width:
+            lane = lane + pick_of(place, distance) * step
+            step //= 2
+            distance *= 2
+        at = (slice(None), pl.ds(pl.multiple_of(lane, 128), width))
+        source, k = (held_pieces, j) if j < here else (got_pieces, j - here)
+        mean = source[k * rows : (k + 1) * rows, :].astype(F32) * (1.0 / replicas)
         moved = MOMENTUM * momentum[at] + mean
         new_momentum[at] = moved
         new_global[at] = global_fragment[at] - OUTER_RATE * (mean + MOMENTUM * moved)
@@ -301,14 +291,26 @@
     same_core = [[2 * e + c for e in range(experts)] for c in range(2)]
     pairs = [(i, i ^ 1) for i in range(size)]
 
-    inner, span = inner_of(replicas), outer_of(replicas)
+    inner = inner_of(replicas)
     kept, got = halve(fragment_delta.reshape(3 * FRAG, D), 1)
 
     table = call(functools.partial(pack_kernel, cap), sds((rows, D + EXT), BF16), 56)(
         tokens, targets, expert_ids.transpose(0, 2, 1), route_weight
     )
     table, got = lax.optimization_barrier((table, got))
-    piece = scatter_sum(kept.astype(F32) + got.astype(F32), inner, span)
+    sums = kept.astype(F32) + got.astype(F32)
+    distance = 2
+    while distance < inner:
+        kept, got = halve(sums, distance)
+        sums = kept + got.astype(F32)
+        distance *= 2
+    across = []
+    while distance < replicas:
+        across.insert(0, distance)
+        distance *= 2
+    for distance in across:
+        sums = add_across(sums, distance)
+    pieces = sums.astype(BF16)
     own = lax.all_to_all(
         table.reshape(experts, 4 * cap, D + EXT),
         "expert",
@@ -317,18 +319,15 @@
         tiled=True,
         axis_index_groups=same_core,
     ).reshape(rows, D + EXT)
-    own, piece = lax.optimization_barrier((own, piece))
-    pieces = lax.all_to_all(
-        jnp.broadcast_to(piece[None], (span,) + piece.shape),
-        "replica",
-        split_axis=0,
-        concat_axis=0,
-        tiled=True,
-        axis_index_groups=[
-            list(range(start, start + span)) for start in range(0, replicas, span)
-        ],
-    )
+    own, pieces = lax.optimization_barrier((own, pieces))
     other = lax.ppermute(own, "expert", pairs)
+    gather = [inner >> k for k in range(1, inner.bit_length())]
+    marks = [0]
+    for distance in gather:
+        marks += [mark ^ distance for mark in marks]
+    held = []
+    for distance in gather[:-2]:
+        held.append(swap(pieces, distance))
     gate, up, down = gate_weight[0], up_weight[0], down_weight[0]
 
     x1, partial, sent, act, slope_up, hidden1 = call(
@@ -342,7 +341,11 @@
             sds((slots, FS), BF16),
         ),
     )(own, other, gate, up, down)
+    sent, *held = lax.optimization_barrier((sent, *held))
+    for got in held:
+        pieces = jnp.concatenate([pieces, got], axis=0)
     received = lax.ppermute(sent, "expert", pairs)
+    held = [swap(pieces, distance) for distance in gather[-2:-1]]
     x2, t1, t2, w, gate2, up2, cross = call(
         functools.partial(unpack_kernel, cap),
         (
@@ -368,7 +371,13 @@
             sds((slots, FS), F32),
         ),
     )(partial, received, t1, w, down, act, slope_up, hidden1, gate2, up2, cross)
+    sent2, *held = lax.optimization_barrier((sent2, *held))
+    for got in held:
+        pieces = jnp.concatenate([pieces, got], axis=0)
     received2 = lax.ppermute(sent2, "expert", pairs)
+    got = pieces
+    for distance in gather[-1:]:
+        got = swap(pieces, distance)
     base, down_part, frag2, hidden_frag2 = pl.pallas_call(
         fragment_kernel,
         out_shape=(
@@ -381,7 +390,7 @@
         + [pl.BlockSpec(memory_space=pltpu.VMEM)] * 12,
         compiler_params=pltpu.CompilerParams(vmem_limit_bytes=20 * 1024 * 1024),
         cost_estimate=pl.CostEstimate(
-            flops=1_000, bytes_accessed=8_000, transcendentals=0
+            flops=1_000_000_000, bytes_accessed=10_000_000, transcendentals=0
         ),
     )(
         fragment_index, gate, up, down, x1, cot, gate_first, up_first, hidden1, hidden2, act2,
@@ -390,11 +399,21 @@
     next_delta = call(last_kernel, sds((1, 1, 3, FRAG, D), F32))(
         partial2, received2, t2, w, x2, down_part, frag2, hidden_frag2, base
     )
-    next_delta, pieces = lax.optimization_barrier((next_delta, pieces))
-    new_global, new_momentum = call(
-        functools.partial(outer_kernel, replicas),
-        (sds((3 * FRAG, D), F32), sds((3 * FRAG, D), F32)),
-    )(pieces, global_fragment.reshape(3 * FRAG, D), outer_momentum.reshape(3 * FRAG, D))
+    next_delta, got = lax.optimization_barrier((next_delta, got))
+    new_global, new_momentum = pl.pallas_call(
+        functools.partial(outer_kernel, replicas, tuple(marks)),
+        out_shape=(sds((3 * FRAG, D), F32), sds((3 * FRAG, D), F32)),
+        in_specs=[pl.BlockSpec(memory_space=pltpu.SMEM)]
+        + [pl.BlockSpec(memory_space=pltpu.VMEM)] * 4,
+        compiler_params=pltpu.CompilerParams(vmem_limit_bytes=20 * 1024 * 1024),
+        cost_estimate=pl.CostEstimate(flops=1_000_000_000, bytes_accessed=10_000_000, transcendentals=0),
+    )(
+        lax.axis_index("replica").astype(jnp.int32).reshape(1),
+        pieces,
+        got,
+        global_fragment.reshape(3 * FRAG, D),
+        outer_momentum.reshape(3 * FRAG, D),
+    )
     whole = (1, 3, FRAG, D)
     return (next_delta, new_global.reshape(whole), new_momentum.reshape(whole))
 

time: 127 us -> 109 us (0.86)
  the two profiles are of different devices: /device:TPU:64 before, /device:TPU:56 now
where the time goes in v3:
time: 109 us; the launch traced here: 107 us
  starting transfers between devices  70.7 us (65%)
  Pallas kernels  17.8 us (16%)
  waiting for transfers between devices  10.7 us (10%)
  local copies, waits for them, and re-layouts  4.58 us (4%)
  other arithmetic  2.09 us (2%)
    ppermute x8, starting transfers between devices, swap(): lax.ppermute(values, 'replica', [(i, i ^ distance) for i in range(replica...  57.2 us
    ppermute x8, waiting for transfers between devices, swap(): lax.ppermute(values, 'replica', [(i, i ^ distance) for i in range(replica...  10.7 us
    all_to_all x1, starting transfers between devices, shards(): lax.all_to_all(table.reshape(experts, 4 * cap, D + EXT), 'expert', split_...  7.57 us
    pallas_call x1, Pallas kernels, shards(): call(functools.partial(pack_kernel, cap), sds((rows, D + EXT), BF16), 56)  3.62 us
    unnamed x20, local copies, waits for them, and re-layouts  3.6 us
    pallas_call x1, Pallas kernels, shards(): pl.pallas_call(fragment_kernel, out_shape=(sds((3, FRAG, D), F32), sds((F...  3.05 us
    pallas_call x1, Pallas kernels, shards(): call(functools.partial(unpack_kernel, cap), (sds((slots, D), BF16), sds((...  2.75 us
    pallas_call x1, Pallas kernels, shards(): call(last_kernel, sds((1, 1, 3, FRAG, D), F32))  2.67 us
  transfers between devices with their start and end apart: 12, of which 6 were waited for; matrix products, arithmetic and copies ran while one was open for 2% of the time, Pallas kernels for 15%

profile of v3, /device:TPU:56, one launch (start us, length us, event | category | flops | bytes accessed | tf_op | source)
XLA Modules:
  0.0 106.9 jit_solution(1786696215783540813)
XLA Ops:
  0.6 0.9 constant_dynamic-slice_fusion
  1.6 4.3 %collective-permute-start = (bf16[96,1024]{1,0:T(8,128)(2,1)S(1)}, bf16[96,1024]{1,0:T(8,128)(2,1)S(1)}, u32[]{:S(2)}, u32[]{:S(2)}) collective-permute-start(bf16[96,1024]{1,0:T(8,128)(2,1)S(1)} %constant_dynamic-slice_fusion), channel_id=1, source_target_pairs={{0,32},{32,0},{64,96},{96,64},{128,160},{160,128},{192,224},{224,1... | collective-permute-start | bytes 589832 | tf_op jit(solution)/shard_map/ppermute | solution.py:235
  5.9 3.6 %shard_map.130 = bf16[384,2176]{1,0:T(8,128)(2,1)} custom-call(bf16[2,64,2048]{2,1,0:T(8,128)(2,1)} %tokens.1, bf16[2,64,2048]{2,1,0:T(8,128)(2,1)} %targets.1, s32[2,1,64]{2,1,0:T(1,128)} %bitcast.33, f32[2,64]{1,0:T(2,128)} %weight.1), custom_call_target="tpu_custom_call" | custom-call | flops 1000000000 | bytes 10000000 | tf_op jit(solution)/shard_map/pallas_call | solution.py:297
  9.5 1.3 %collective-permute-done = bf16[96,1024]{1,0:T(8,128)(2,1)S(1)} collective-permute-done((bf16[96,1024]{1,0:T(8,128)(2,1)S(1)}, bf16[96,1024]{1,0:T(8,128)(2,1)S(1)}, u32[]{:S(2)}, u32[]{:S(2)}) %collective-permute-start) | collective-permute-done | bytes 196640 | tf_op jit(solution)/shard_map/ppermute | solution.py:235
  10.8 7.6 %all-to-all-start = ((bf16[16,24,2176]{2,1,0:T(8,128)(2,1)}), bf16[16,24,2176]{2,1,0:T(8,128)(2,1)S(1)}, u32[]{:S(2)}, u32[]{:S(2)}) async-start(bf16[16,24,2176]{2,1,0:T(8,128)(2,1)} %bitcast.30), calls=%async_computation | async-start | bytes 3342336 | tf_op jit(solution)/shard_map/all_to_all | solution.py:314
  18.4 1.1 %convert_add_fusion = f32[96,1024]{1,0:T(8,128)S(1)} fusion(bf16[96,1024]{1,0:T(8,128)(2,1)S(1)} %collective-permute-done, bf16[96,2048]{1,0:T(8,128)(2,1)} %bitcast.32, s32[]{:T(128)S(6)} %select_n.31), kind=kLoop, calls=%fused_computation | loop fusion | flops 294912 | bytes 786436 | tf_op jit(solution)/shard_map/add | solution.py:301
  19.5 0.0 copy-start.8
  19.5 0.7 copy-done.8
  20.2 6.1 %collective-permute-start.1 = (bf16[96,512]{1,0:T(8,128)(2,1)S(1)}, bf16[96,512]{1,0:T(8,128)(2,1)S(1)}, u32[]{:S(2)}, u32[]{:S(2)}) collective-permute-start(bf16[96,512]{1,0:T(8,128)(2,1)S(1)} %dynamic-slice_convert_fusion), channel_id=1, source_target_pairs={{0,64},{32,96},{64,0},{96,32},{128,192},{160,224},{192,128},{224,1... | collective-permute-start | bytes 294920 | tf_op jit(solution)/shard_map/ppermute | solution.py:235
  26.3 2.7 %collective-permute-done.1 = bf16[96,512]{1,0:T(8,128)(2,1)S(1)} collective-permute-done((bf16[96,512]{1,0:T(8,128)(2,1)S(1)}, bf16[96,512]{1,0:T(8,128)(2,1)S(1)}, u32[]{:S(2)}, u32[]{:S(2)}) %collective-permute-start.1) | collective-permute-done | bytes 98336 | tf_op jit(solution)/shard_map/ppermute | solution.py:235
  29.0 0.9 convert_add_fusion.1
  30.0 10.9 %collective-permute-start.2 = (bf16[96,256]{1,0:T(8,128)(2,1)S(1)}, bf16[96,256]{1,0:T(8,128)(2,1)S(1)}, u32[]{:S(2)}, u32[]{:S(2)}) collective-permute-start(bf16[96,256]{1,0:T(8,128)(2,1)S(1)} %dynamic-slice_convert_fusion.1), channel_id=1, source_target_pairs={{0,128},{32,160},{64,192},{96,224},{128,0},{160,32},{192,64},{224,... | collective-permute-start | bytes 147464 | tf_op jit(solution)/shard_map/ppermute | solution.py:235
  41.0 2.0 %collective-permute-done.2 = bf16[96,256]{1,0:T(8,128)(2,1)S(1)} collective-permute-done((bf16[96,256]{1,0:T(8,128)(2,1)S(1)}, bf16[96,256]{1,0:T(8,128)(2,1)S(1)}, u32[]{:S(2)}, u32[]{:S(2)}) %collective-permute-start.2) | collective-permute-done | bytes 49184 | tf_op jit(solution)/shard_map/ppermute | solution.py:235
  43.0 8.0 %collective-permute-start.3 = (bf16[96,256]{1,0:T(8,128)(2,1)S(1)}, bf16[96,256]{1,0:T(8,128)(2,1)S(1)}, u32[]{:S(2)}, u32[]{:S(2)}) collective-permute-start(bf16[96,256]{1,0:T(8,128)(2,1)S(1)} %add_convert_fusion.2), channel_id=1, source_target_pairs={{0,512},{32,544},{64,576},{96,608},{128,640},{160,672},{192,704},{... | collective-permute-start | bytes 147464 | tf_op jit(solution)/shard_map/ppermute | solution.py:235
  51.0 2.1 %collective-permute-done.3 = bf16[96,256]{1,0:T(8,128)(2,1)S(1)} collective-permute-done((bf16[96,256]{1,0:T(8,128)(2,1)S(1)}, bf16[96,256]{1,0:T(8,128)(2,1)S(1)}, u32[]{:S(2)}, u32[]{:S(2)}) %collective-permute-start.3) | collective-permute-done | bytes 49184 | tf_op jit(solution)/shard_map/ppermute | solution.py:235
  53.1 14.1 %collective-permute-start.4 = (bf16[96,256]{1,0:T(8,128)(2,1)S(1)}, bf16[96,256]{1,0:T(8,128)(2,1)S(1)}, u32[]{:S(2)}, u32[]{:S(2)}) collective-permute-start(bf16[96,256]{1,0:T(8,128)(2,1)S(1)} %add_convert_fusion.1), channel_id=1, source_target_pairs={{0,384},{32,416},{64,448},{96,480},{128,256},{160,288},{192,320},{... | collective-permute-start | bytes 147464 | tf_op jit(solution)/shard_map/ppermute | solution.py:235
  67.2 2.1 %collective-permute-done.4 = bf16[96,256]{1,0:T(8,128)(2,1)S(1)} collective-permute-done((bf16[96,256]{1,0:T(8,128)(2,1)S(1)}, bf16[96,256]{1,0:T(8,128)(2,1)S(1)}, u32[]{:S(2)}, u32[]{:S(2)}) %collective-permute-start.4) | collective-permute-done | bytes 49184 | tf_op jit(solution)/shard_map/ppermute | solution.py:235
  69.3 1.9 %collective-permute-start.5 = (bf16[384,2176]{1,0:T(8,128)(2,1)S(1)}, bf16[384,2176]{1,0:T(8,128)(2,1)S(1)}, u32[]{:S(2)}, u32[]{:S(2)}) collective-permute-start(bf16[384,2176]{1,0:T(8,128)(2,1)S(1)} %bitcast.15), channel_id=1, source_target_pairs={{0,1},{1,0},{2,3},{3,2},{4,5},{5,4},{6,7},{7,6},{8,9},{9,8},{10,11... | collective-permute-start | bytes 5013512 | tf_op jit(solution)/shard_map/ppermute | solution.py:323
  71.2 5.1 %collective-permute-start.6 = (bf16[96,256]{1,0:T(8,128)(2,1)S(1)}, bf16[96,256]{1,0:T(8,128)(2,1)S(1)}, u32[]{:S(2)}, u32[]{:S(2)}) collective-permute-start(bf16[96,256]{1,0:T(8,128)(2,1)S(1)} %add_convert_fusion), channel_id=1, source_target_pairs={{0,128},{32,160},{64,192},{96,224},{128,0},{160,32},{192,64},{224,... | collective-permute-start | bytes 147464 | tf_op jit(solution)/shard_map/ppermute | solution.py:235
  76.4 1.4 %copy-done.1 = bf16[1,2048,384]{2,1,0:T(8,128)(2,1)S(1)} copy-done((bf16[1,2048,384]{2,1,0:T(8,128)(2,1)S(1)}, bf16[1,2048,384]{2,1,0:T(8,128)(2,1)}, u32[]{:S(2)}) %copy-start.1) | copy-done | bytes 1572888
  77.8 1.4 %copy-done.3 = bf16[1,384,2048]{2,1,0:T(8,128)(2,1)S(1)} copy-done((bf16[1,384,2048]{2,1,0:T(8,128)(2,1)S(1)}, bf16[1,384,2048]{2,1,0:T(8,128)(2,1)}, u32[]{:S(2)}) %copy-start.3) | copy-done | bytes 1572888
  79.2 2.1 %shard_map.131 = (bf16[192,2048]{1,0:T(8,128)(2,1)S(1)}, f32[192,2048]{1,0:T(8,128)S(1)}, bf16[192,2048]{1,0:T(8,128)(2,1)S(1)}, f32[192,384]{1,0:T(8,128)S(1)},...) custom-call(bf16[384,2176]{1,0:T(8,128)(2,1)S(1)} %bitcast.16, bf16[384,2176]{1,0:T(8,128)(2,1)S(1)} %collective-permute-done.5.other, ...), custom_call_target="tpu_custom_call" | custom-call | flops 1000000000 | bytes 10000000 | tf_op jit(solution)/shard_map/pallas_call | solution.py:333
  81.3 2.1 %collective-permute-start.7 = (bf16[192,2048]{1,0:T(8,128)(2,1)S(1)}, bf16[192,2048]{1,0:T(8,128)(2,1)S(1)}, u32[]{:S(2)}, u32[]{:S(2)}) collective-permute-start(bf16[192,2048]{1,0:T(8,128)(2,1)S(1)} %get-tuple-element.46), channel_id=1, source_target_pairs={{0,1},{1,0},{2,3},{3,2},{4,5},{5,4},{6,7},{7,6},{8,9},{9,8},{10,11... | collective-permute-start | bytes 2359304 | tf_op jit(solution)/shard_map/ppermute | solution.py:347
  83.5 5.0 %collective-permute-start.8 = (bf16[192,256]{1,0:T(8,128)(2,1)S(1)}, bf16[192,256]{1,0:T(8,128)(2,1)S(1)}, u32[]{:S(2)}, u32[]{:S(2)}) collective-permute-start(bf16[192,256]{1,0:T(8,128)(2,1)S(1)} %pad_maximum_fusion), channel_id=1, source_target_pairs={{0,64},{32,96},{64,0},{96,32},{128,192},{160,224},{192,128},{224,1... | collective-permute-start | bytes 294920 | tf_op jit(solution)/shard_map/ppermute | solution.py:235
  88.5 2.7 %shard_map.132 = (bf16[192,2048]{1,0:T(8,128)(2,1)S(1)}, bf16[192,2048]{1,0:T(8,128)(2,1)S(1)}, bf16[192,2048]{1,0:T(8,128)(2,1)S(1)}, f32[2,192,128]{2,1,0:T(8,...) custom-call(bf16[384,2176]{1,0:T(8,128)(2,1)S(1)} %bitcast.17, ...), custom_call_target="tpu_custom_call" | custom-call | flops 1000000000 | bytes 10000000 | tf_op jit(solution)/shard_map/pallas_call | solution.py:349
  91.3 2.2 %shard_map.133 = (bf16[192,2048]{1,0:T(8,128)(2,1)S(1)}, bf16[192,384]{1,0:T(8,128)(2,1)S(1)}, bf16[192,384]{1,0:T(8,128)(2,1)S(1)}, f32[192,2048]{1,0:T(8,128)S...) custom-call(f32[192,2048]{1,0:T(8,128)S(1)} %get-tuple-element.43.pa, ...), custom_call_target="tpu_custom_call" | custom-call | flops 1000000000 | bytes 10000000 | tf_op jit(solution)/shard_map/pallas_call | solution.py:361
  93.6 0.5 collective-permute-done.8
  94.0 1.9 %collective-permute-start.9 = (bf16[192,2048]{1,0:T(8,128)(2,1)S(1)}, bf16[192,2048]{1,0:T(8,128)(2,1)S(1)}, u32[]{:S(2)}, u32[]{:S(2)}) collective-permute-start(bf16[192,2048]{1,0:T(8,128)(2,1)S(1)} %get-tuple-element.59), channel_id=1, source_target_pairs={{0,1},{1,0},{2,3},{3,2},{4,5},{5,4},{6,7},{7,6},{8,9},{9,8},{10,11... | collective-permute-start | bytes 2359304 | tf_op jit(solution)/shard_map/ppermute | solution.py:377
  96.0 3.7 %collective-permute-start.10 = (bf16[384,256]{1,0:T(8,128)(2,1)S(1)}, bf16[384,256]{1,0:T(8,128)(2,1)S(1)}, u32[]{:S(2)}, u32[]{:S(2)}) collective-permute-start(bf16[384,256]{1,0:T(8,128)(2,1)S(1)} %constant_dynamic-update-slice_fusion.held_pieces), channel_id=1, source_target_pairs={{0,32},{32,0},{64,96},{96,64},{128,160},{160,128},{192,224},{224,1... | collective-permute-start | bytes 589832 | tf_op jit(solution)/shard_map/ppermute | solution.py:235
  99.8 3.0 %shard_map.134 = (f32[3,32,2048]{2,1,0:T(8,128)S(1)}, f32[32,2048]{1,0:T(8,128)S(1)}, f32[2,192,32]{2,1,0:T(8,128)S(1)}, bf16[192,32]{1,0:T(8,128)(2,1)S(1)}) custom-call(s32[12]{0:T(128)S(1)} %copy-done.6, bf16[2048,384]{1,0:T(8,128)(2,1)S(1)} %bitcast.20, bf16[2048,384]{1,0:T(8,128)(2,1)S(1)} %bitcast.23, bf16[384,2048]{1,0:T(8,128)(2,1)S(1)} %bitcast.26, ...), custom_call_target="tpu_custom_call" | custom-call | flops 1000000000 | bytes 10000000 | tf_op jit(solution)/shard_map/pallas_call | solution.py:381
  102.9 2.7 %shard_map.135 = f32[1,1,3,32,2048]{4,3,2,1,0:T(8,128)} custom-call(f32[192,2048]{1,0:T(8,128)S(1)} %get-tuple-element.56.partial, bf16[192,2048]{1,0:T(8,128)(2,1)S(1)} %collective-permute-done.9.received, bf16[192,2048]{1,0:T(8,128)(2,1)S(1)} %get-tuple-element.60.t2, f32[2,192,128]{2,1,0:T(8,128)S(1)} %get-tuple-element.49.w, ...), custom_call_target="tpu_custom_call" | custom-call | flops 1000000000 | bytes 10000000 | tf_op jit(solution)/shard_map/pallas_call | solution.py:399
  105.5 1.4 %shard_map.136 = (f32[96,2048]{1,0:T(8,128)}, f32[96,2048]{1,0:T(8,128)}) custom-call(s32[1]{0:T(128)} %bitcast.9.me, bf16[384,256]{1,0:T(8,128)(2,1)S(1)} %constant_dynamic-update-slice_fusion.held_pieces, bf16[384,256]{1,0:T(8,128)(2,1)S(1)} %collective-permute-done.10.got_pieces, f32[96,2048]{1,0:T(8,128)S(1)} %bitcast.28, f32[96,2048]{1,0:T(8,128)S(1)} %bitcast.29), custom_call_target="tpu_custom_call" | custom-call | flops 1000000000 | bytes 10000000 | tf_op jit(solution)/shard_map/pallas_call | solution.py:403
  (29 shorter events, 0.2 us)
Async XLA Ops:
  1.6 9.2 %collective-permute-start = (bf16[96,1024]{1,0:T(8,128)(2,1)S(1)}, bf16[96,1024]{1,0:T(8,128)(2,1)S(1)}, u32[]{:S(2)}, u32[]{:S(2)}) collective-permute-start(bf16[96,1024]{1,0:T(8,128)(2,1)S(1)} %constant_dynamic-slice_fusion), channel_id=1, source_target_pairs={{0,32},{32,0},{64,96},{96,64},{128,160},{160,128},{192,224},{224,1... | collective-permute-start | bytes 589832 | tf_op jit(solution)/shard_map/ppermute | solution.py:235
  10.8 58.5 %all-to-all-start = ((bf16[16,24,2176]{2,1,0:T(8,128)(2,1)}), bf16[16,24,2176]{2,1,0:T(8,128)(2,1)S(1)}, u32[]{:S(2)}, u32[]{:S(2)}) async-start(bf16[16,24,2176]{2,1,0:T(8,128)(2,1)} %bitcast.30), calls=%async_computation | async-start | bytes 3342336 | tf_op jit(solution)/shard_map/all_to_all | solution.py:314
  18.3 58.1 %copy-start = (bf16[1,2048,384]{2,1,0:T(8,128)(2,1)S(1)}, bf16[1,2048,384]{2,1,0:T(8,128)(2,1)}, u32[]{:S(2)}) copy-start(bf16[1,2048,384]{2,1,0:T(8,128)(2,1)} %param.15) | copy-start | bytes 4718596
  19.5 0.7 copy-start.8
  20.2 8.8 %collective-permute-start.1 = (bf16[96,512]{1,0:T(8,128)(2,1)S(1)}, bf16[96,512]{1,0:T(8,128)(2,1)S(1)}, u32[]{:S(2)}, u32[]{:S(2)}) collective-permute-start(bf16[96,512]{1,0:T(8,128)(2,1)S(1)} %dynamic-slice_convert_fusion), channel_id=1, source_target_pairs={{0,64},{32,96},{64,0},{96,32},{128,192},{160,224},{192,128},{224,1... | collective-permute-start | bytes 294920 | tf_op jit(solution)/shard_map/ppermute | solution.py:235
  30.0 13.0 %collective-permute-start.2 = (bf16[96,256]{1,0:T(8,128)(2,1)S(1)}, bf16[96,256]{1,0:T(8,128)(2,1)S(1)}, u32[]{:S(2)}, u32[]{:S(2)}) collective-permute-start(bf16[96,256]{1,0:T(8,128)(2,1)S(1)} %dynamic-slice_convert_fusion.1), channel_id=1, source_target_pairs={{0,128},{32,160},{64,192},{96,224},{128,0},{160,32},{192,64},{224,... | collective-permute-start | bytes 147464 | tf_op jit(solution)/shard_map/ppermute | solution.py:235
  43.0 10.0 %collective-permute-start.3 = (bf16[96,256]{1,0:T(8,128)(2,1)S(1)}, bf16[96,256]{1,0:T(8,128)(2,1)S(1)}, u32[]{:S(2)}, u32[]{:S(2)}) collective-permute-start(bf16[96,256]{1,0:T(8,128)(2,1)S(1)} %add_convert_fusion.2), channel_id=1, source_target_pairs={{0,512},{32,544},{64,576},{96,608},{128,640},{160,672},{192,704},{... | collective-permute-start | bytes 147464 | tf_op jit(solution)/shard_map/ppermute | solution.py:235
  53.1 16.2 %collective-permute-start.4 = (bf16[96,256]{1,0:T(8,128)(2,1)S(1)}, bf16[96,256]{1,0:T(8,128)(2,1)S(1)}, u32[]{:S(2)}, u32[]{:S(2)}) collective-permute-start(bf16[96,256]{1,0:T(8,128)(2,1)S(1)} %add_convert_fusion.1), channel_id=1, source_target_pairs={{0,384},{32,416},{64,448},{96,480},{128,256},{160,288},{192,320},{... | collective-permute-start | bytes 147464 | tf_op jit(solution)/shard_map/ppermute | solution.py:235
  69.3 7.1 %collective-permute-start.5 = (bf16[384,2176]{1,0:T(8,128)(2,1)S(1)}, bf16[384,2176]{1,0:T(8,128)(2,1)S(1)}, u32[]{:S(2)}, u32[]{:S(2)}) collective-permute-start(bf16[384,2176]{1,0:T(8,128)(2,1)S(1)} %bitcast.15), channel_id=1, source_target_pairs={{0,1},{1,0},{2,3},{3,2},{4,5},{5,4},{6,7},{7,6},{8,9},{9,8},{10,11... | collective-permute-start | bytes 5013512 | tf_op jit(solution)/shard_map/ppermute | solution.py:323
  71.2 10.1 %collective-permute-start.6 = (bf16[96,256]{1,0:T(8,128)(2,1)S(1)}, bf16[96,256]{1,0:T(8,128)(2,1)S(1)}, u32[]{:S(2)}, u32[]{:S(2)}) collective-permute-start(bf16[96,256]{1,0:T(8,128)(2,1)S(1)} %add_convert_fusion), channel_id=1, source_target_pairs={{0,128},{32,160},{64,192},{96,224},{128,0},{160,32},{192,64},{224,... | collective-permute-start | bytes 147464 | tf_op jit(solution)/shard_map/ppermute | solution.py:235
  76.4 1.4 %copy-start.1 = (bf16[1,2048,384]{2,1,0:T(8,128)(2,1)S(1)}, bf16[1,2048,384]{2,1,0:T(8,128)(2,1)}, u32[]{:S(2)}) copy-start(bf16[1,2048,384]{2,1,0:T(8,128)(2,1)} %param.16) | copy-start | bytes 4718596
  77.8 1.4 %copy-start.3 = (bf16[1,384,2048]{2,1,0:T(8,128)(2,1)S(1)}, bf16[1,384,2048]{2,1,0:T(8,128)(2,1)}, u32[]{:S(2)}) copy-start(bf16[1,384,2048]{2,1,0:T(8,128)(2,1)} %param.17) | copy-start | bytes 4718596
  81.3 9.9 %collective-permute-start.7 = (bf16[192,2048]{1,0:T(8,128)(2,1)S(1)}, bf16[192,2048]{1,0:T(8,128)(2,1)S(1)}, u32[]{:S(2)}, u32[]{:S(2)}) collective-permute-start(bf16[192,2048]{1,0:T(8,128)(2,1)S(1)} %get-tuple-element.46), channel_id=1, source_target_pairs={{0,1},{1,0},{2,3},{3,2},{4,5},{5,4},{6,7},{7,6},{8,9},{9,8},{10,11... | collective-permute-start | bytes 2359304 | tf_op jit(solution)/shard_map/ppermute | solution.py:347
  83.5 10.6 %collective-permute-start.8 = (bf16[192,256]{1,0:T(8,128)(2,1)S(1)}, bf16[192,256]{1,0:T(8,128)(2,1)S(1)}, u32[]{:S(2)}, u32[]{:S(2)}) collective-permute-start(bf16[192,256]{1,0:T(8,128)(2,1)S(1)} %pad_maximum_fusion), channel_id=1, source_target_pairs={{0,64},{32,96},{64,0},{96,32},{128,192},{160,224},{192,128},{224,1... | collective-permute-start | bytes 294920 | tf_op jit(solution)/shard_map/ppermute | solution.py:235
  88.5 2.8 %copy-start.4 = (bf16[1,384,2048]{2,1,0:T(8,128)(2,1)S(1)}, bf16[1,384,2048]{2,1,0:T(8,128)(2,1)}, u32[]{:S(2)}) copy-start(bf16[1,384,2048]{2,1,0:T(8,128)(2,1)} %param.17) | copy-start | bytes 4718596
  91.3 8.5 %copy-start.2 = (bf16[1,2048,384]{2,1,0:T(8,128)(2,1)S(1)}, bf16[1,2048,384]{2,1,0:T(8,128)(2,1)}, u32[]{:S(2)}) copy-start(bf16[1,2048,384]{2,1,0:T(8,128)(2,1)} %param.16) | copy-start | bytes 4718596
  91.3 8.5 %copy-start.5 = (f32[1,3,32,2048]{3,2,1,0:T(8,128)S(1)}, f32[1,3,32,2048]{3,2,1,0:T(8,128)}, u32[]{:S(2)}) copy-start(f32[1,3,32,2048]{3,2,1,0:T(8,128)} %param.19) | copy-start | bytes 2359300
  91.3 8.5 %copy-start.6 = (s32[12]{0:T(128)S(1)}, s32[12]{0:T(128)}, u32[]{:S(2)}) copy-start(s32[12]{0:T(128)} %index.1) | copy-start | bytes 148
  94.0 8.8 %collective-permute-start.9 = (bf16[192,2048]{1,0:T(8,128)(2,1)S(1)}, bf16[192,2048]{1,0:T(8,128)(2,1)S(1)}, u32[]{:S(2)}, u32[]{:S(2)}) collective-permute-start(bf16[192,2048]{1,0:T(8,128)(2,1)S(1)} %get-tuple-element.59), channel_id=1, source_target_pairs={{0,1},{1,0},{2,3},{3,2},{4,5},{5,4},{6,7},{7,6},{8,9},{9,8},{10,11... | collective-permute-start | bytes 2359304 | tf_op jit(solution)/shard_map/ppermute | solution.py:377
  96.0 9.5 %collective-permute-start.10 = (bf16[384,256]{1,0:T(8,128)(2,1)S(1)}, bf16[384,256]{1,0:T(8,128)(2,1)S(1)}, u32[]{:S(2)}, u32[]{:S(2)}) collective-permute-start(bf16[384,256]{1,0:T(8,128)(2,1)S(1)} %constant_dynamic-update-slice_fusion.held_pieces), channel_id=1, source_target_pairs={{0,32},{32,0},{64,96},{96,64},{128,160},{160,128},{192,224},{224,1... | collective-permute-start | bytes 589832 | tf_op jit(solution)/shard_map/ppermute | solution.py:235
  102.8 2.7 %copy-start.7 = (f32[1,3,32,2048]{3,2,1,0:T(8,128)S(1)}, f32[1,3,32,2048]{3,2,1,0:T(8,128)}, u32[]{:S(2)}) copy-start(f32[1,3,32,2048]{3,2,1,0:T(8,128)} %param.20) | copy-start | bytes 2359300

commit v4 on v3

--- a/solution.py
+++ b/solution.py
@@ -104,13 +104,24 @@
     return (iota((rows, 4 * rows), 1) == wanted).astype(BF16)
 
 
+def own_kernel(cap, own, rows_out, w_out):
+    half = own.shape[0] // 4
+    sources = half // cap
+    for k in range(4):
+        pick = picker(cap, sources, k)
+        rows_out[k * half : (k + 1) * half, :] = mm(pick, own[:, 0:D]).astype(BF16)
+        if k >= 2:
+            terms = mm(pick, own[:, D : D + EXT])
+            w_out[k - 2] = jnp.broadcast_to(jnp.sum(terms, axis=1, keepdims=True), (half, EXT))
+
+
 def first_kernel(
     cap, own, other, gate, up, down, x_out, partial, sent, act, slope_up, hidden_out
 ):
     sources = own.shape[0] // (4 * cap)
     pick = picker(cap, sources, 0)
     half = sources * cap
-    x_out[0:half, :] = mm(pick, own[:, 0:D]).astype(BF16)
+    x_out[0:half, :] = own[0:half, :]
     x_out[half:, :] = mm(pick, other[:, 0:D]).astype(BF16)
     x = x_out[...]
     pre_gate = mm(x, gate[...]) * SCALE_MODEL
@@ -126,19 +137,18 @@
 
 
 def unpack_kernel(
-    cap, own, other, gate, up, x1, x2_out, t1_out, t2_out, w_out, gate_out, up_out, cross
+    cap, own, w_own, other, gate, up, x1, x2_out, t1_out, t2_out, w_out, gate_out, up_out, cross
 ):
     sources = own.shape[0] // (4 * cap)
     half = sources * cap
-    pick = picker(cap, sources, 1)
-    x2_out[0:half, :] = mm(pick, own[:, 0:D]).astype(BF16)
-    x2_out[half:, :] = mm(pick, other[:, 0:D]).astype(BF16)
-    for k, t_out in ((2, t1_out), (3, t2_out)):
+    for k, out in ((1, x2_out), (2, t1_out), (3, t2_out)):
         pick = picker(cap, sources, k)
-        for part, ref in ((0, own), (half, other)):
-            t_out[part : part + half, :] = mm(pick, ref[:, 0:D]).astype(BF16)
-            terms = mm(pick, ref[:, D : D + EXT])
-            w_out[k - 2, part : part + half, :] = jnp.broadcast_to(
+        out[0:half, :] = own[k * half : (k + 1) * half, :]
+        out[half:, :] = mm(pick, other[:, 0:D]).astype(BF16)
+        if k >= 2:
+            terms = mm(pick, other[:, D : D + EXT])
+            w_out[k - 2, 0:half, :] = w_own[k - 2]
+            w_out[k - 2, half:, :] = jnp.broadcast_to(
                 jnp.sum(terms, axis=1, keepdims=True), (half, EXT)
             )
     x2 = x2_out[...]
@@ -235,12 +245,19 @@
     return lax.ppermute(values, "replica", [(i, i ^ distance) for i in range(replicas)])
 
 
-def halve(values, distance):
-    half = values.shape[1] // 2
+def halve(terms, distance):
+    half = terms[0].shape[1] // 2
     bit = pick_of(lax.axis_index("replica"), distance)
-    sent = lax.dynamic_slice_in_dim(values, (1 - bit) * half, half, 1)
-    kept = lax.dynamic_slice_in_dim(values, bit * half, half, 1)
-    return kept, swap(sent.astype(BF16), distance)
+    sent = total_of([lax.dynamic_slice_in_dim(t, (1 - bit) * half, half, 1) for t in terms])
+    kept = [lax.dynamic_slice_in_dim(t, bit * half, half, 1) for t in terms]
+    return kept + [swap(sent.astype(BF16), distance)]
+
+
+def total_of(terms):
+    total = terms[0].astype(F32)
+    for term in terms[1:]:
+        total = total + term.astype(F32)
+    return total
 
 
 def add_across(values, distance):
@@ -292,18 +309,17 @@
     pairs = [(i, i ^ 1) for i in range(size)]
 
     inner = inner_of(replicas)
-    kept, got = halve(fragment_delta.reshape(3 * FRAG, D), 1)
+    terms = halve([fragment_delta.reshape(3 * FRAG, D)], 1)
 
     table = call(functools.partial(pack_kernel, cap), sds((rows, D + EXT), BF16), 56)(
         tokens, targets, expert_ids.transpose(0, 2, 1), route_weight
     )
-    table, got = lax.optimization_barrier((table, got))
-    sums = kept.astype(F32) + got.astype(F32)
+    table, terms[-1] = lax.optimization_barrier((table, terms[-1]))
     distance = 2
     while distance < inner:
-        kept, got = halve(sums, distance)
-        sums = kept + got.astype(F32)
+        terms = halve(terms, distance)
         distance *= 2
+    sums = total_of(terms)
     across = []
     while distance < replicas:
         across.insert(0, distance)
@@ -321,6 +337,10 @@
     ).reshape(rows, D + EXT)
     own, pieces = lax.optimization_barrier((own, pieces))
     other = lax.ppermute(own, "expert", pairs)
+    own_rows, w_own = call(
+        functools.partial(own_kernel, cap),
+        (sds((rows, D), BF16), sds((2, slots // 2, EXT), F32)),
+    )(own)
     gather = [inner >> k for k in range(1, inner.bit_length())]
     marks = [0]
     for distance in gather:
@@ -340,7 +360,7 @@
             sds((slots, FS), F32),
             sds((slots, FS), BF16),
         ),
-    )(own, other, gate, up, down)
+    )(own_rows, other, gate, up, down)
     sent, *held = lax.optimization_barrier((sent, *held))
     for got in held:
         pieces = jnp.concatenate([pieces, got], axis=0)
@@ -357,7 +377,7 @@
             sds((slots, FS), F32),
             sds((slots, slots), F32),
         ),
-    )(own, other, gate, up, x1)
+    )(own_rows, w_own, other, gate, up, x1)
     cot, gate_first, up_first, partial2, sent2, hidden2, act2, slope_up2 = call(
         second_kernel,
         (

time: 109 us -> 108 us (level); the launches traced: 107 us -> 107 us
  local copies, waits for them, and re-layouts: 4.58 us -> 1 us
  waiting for transfers between devices: 10.7 us -> 13.4 us
  other arithmetic: 2.09 us -> 3.18 us
    unnamed x20 -> x14, local copies, waits for them, and re-layouts: 3.6 us -> 0.05 us
    ppermute x8, waiting for transfers between devices: 10.7 us -> 13.4 us  [swap(): lax.ppermute(values, 'replica', [(i, i ^ distance) for i in range(replica...]
    convert_element_type x0 -> x2, other arithmetic: none -> 2.13 us  [halve(): return kept + [swap(sent.astype(BF16), distance)]]
    add x2 -> x0, other arithmetic: 2.04 us -> none  [the longest x1 1.09 us: shards(): sums = kept.astype(F32) + got.astype(F32)]
    pallas_call x0 -> x1, Pallas kernels: none -> 1.44 us  [shards(): call(functools.partial(own_kernel, cap), (sds((rows, D), BF16), sds((2, s...]
  transfers between devices with their start and end apart: 12 -> 12, of which waited for: 6 -> 8; matrix products, arithmetic and copies ran while one was open for 2% -> 3% of each run, Pallas kernels for 15% -> 16%
where the time goes in v4:
time: 108 us; the launch traced here: 107 us
  starting transfers between devices  70.5 us (65%)
  Pallas kernels  18.2 us (17%)
  waiting for transfers between devices  13.4 us (12%)
  other arithmetic  3.18 us (3%)
    ppermute x8, starting transfers between devices, swap(): lax.ppermute(values, 'replica', [(i, i ^ distance) for i in range(replica...  56.9 us
    ppermute x8, waiting for transfers between devices, swap(): lax.ppermute(values, 'replica', [(i, i ^ distance) for i in range(replica...  13.4 us
    all_to_all x1, starting transfers between devices, shards(): lax.all_to_all(table.reshape(experts, 4 * cap, D + EXT), 'expert', split_...  7.57 us
    pallas_call x1, Pallas kernels, shards(): call(functools.partial(pack_kernel, cap), sds((rows, D + EXT), BF16), 56)  3.63 us
    pallas_call x1, Pallas kernels, shards(): pl.pallas_call(fragment_kernel, out_shape=(sds((3, FRAG, D), F32), sds((F...  3.05 us
    pallas_call x1, Pallas kernels, shards(): call(last_kernel, sds((1, 1, 3, FRAG, D), F32))  2.67 us
    pallas_call x1, Pallas kernels, shards(): call(second_kernel, (sds((slots, D), BF16), sds((slots, FS), BF16), sds((...  2.26 us
    ppermute x1, starting transfers between devices, shards(): other = lax.ppermute(own, 'expert', pairs)  2.18 us
  transfers between devices with their start and end apart: 12, of which 8 were waited for; matrix products, arithmetic and copies ran while one was open for 3% of the time, Pallas kernels for 16%

profile of v4, /device:TPU:56, one launch (start us, length us, event | category | flops | bytes accessed | tf_op | source)
XLA Modules:
  0.0 107.2 jit_solution(3081166688243712359)
XLA Ops:
  0.6 0.9 constant_dynamic-slice_fusion
  1.6 4.3 %collective-permute-start = (bf16[96,1024]{1,0:T(8,128)(2,1)S(1)}, bf16[96,1024]{1,0:T(8,128)(2,1)S(1)}, u32[]{:S(2)}, u32[]{:S(2)}) collective-permute-start(bf16[96,1024]{1,0:T(8,128)(2,1)S(1)} %constant_dynamic-slice_fusion), channel_id=1, source_target_pairs={{0,32},{32,0},{64,96},{96,64},{128,160},{160,128},{192,224},{224,1... | collective-permute-start | bytes 589832 | tf_op jit(solution)/shard_map/ppermute | solution.py:245
  5.9 3.6 %shard_map.130 = bf16[384,2176]{1,0:T(8,128)(2,1)} custom-call(bf16[2,64,2048]{2,1,0:T(8,128)(2,1)} %tokens.1, bf16[2,64,2048]{2,1,0:T(8,128)(2,1)} %targets.1, s32[2,1,64]{2,1,0:T(1,128)} %bitcast.34, f32[2,64]{1,0:T(2,128)} %weight.1), custom_call_target="tpu_custom_call" | custom-call | flops 1000000000 | bytes 10000000 | tf_op jit(solution)/shard_map/pallas_call | solution.py:314
  9.5 1.3 %collective-permute-done = bf16[96,1024]{1,0:T(8,128)(2,1)S(1)} collective-permute-done((bf16[96,1024]{1,0:T(8,128)(2,1)S(1)}, bf16[96,1024]{1,0:T(8,128)(2,1)S(1)}, u32[]{:S(2)}, u32[]{:S(2)}) %collective-permute-start) | collective-permute-done | bytes 196640 | tf_op jit(solution)/shard_map/ppermute | solution.py:245
  10.8 7.6 %all-to-all-start = ((bf16[16,24,2176]{2,1,0:T(8,128)(2,1)}), bf16[16,24,2176]{2,1,0:T(8,128)(2,1)S(1)}, u32[]{:S(2)}, u32[]{:S(2)}) async-start(bf16[16,24,2176]{2,1,0:T(8,128)(2,1)} %bitcast.29), calls=%async_computation | async-start | bytes 3342336 | tf_op jit(solution)/shard_map/all_to_all | solution.py:330
  18.3 1.1 %add_convert_fusion = bf16[96,512]{1,0:T(8,128)(2,1)S(1)} fusion(bf16[96,1024]{1,0:T(8,128)(2,1)S(1)} %collective-permute-done, s32[]{:T(128)S(6)} %select_n.56, bf16[96,2048]{1,0:T(8,128)(2,1)} %bitcast.31, s32[]{:T(128)S(6)} %dynamic_slice.56), kind=kLoop, calls=%fused_computation | loop fusion | flops 196608 | bytes 294920 | tf_op jit(solution)/shard_map/convert_element_type | solution.py:253
  19.5 6.1 %collective-permute-start.1 = (bf16[96,512]{1,0:T(8,128)(2,1)S(1)}, bf16[96,512]{1,0:T(8,128)(2,1)}, u32[]{:S(2)}, u32[]{:S(2)}) collective-permute-start(bf16[96,512]{1,0:T(8,128)(2,1)S(1)} %add_convert_fusion), channel_id=1, source_target_pairs={{0,64},{32,96},{64,0},{96,32},{128,192},{160,224},{192,128},{224,1... | collective-permute-start | bytes 294920 | tf_op jit(solution)/shard_map/ppermute | solution.py:245
  25.6 2.8 %collective-permute-done.1 = bf16[96,512]{1,0:T(8,128)(2,1)} collective-permute-done((bf16[96,512]{1,0:T(8,128)(2,1)S(1)}, bf16[96,512]{1,0:T(8,128)(2,1)}, u32[]{:S(2)}, u32[]{:S(2)}) %collective-permute-start.1) | collective-permute-done | bytes 98336 | tf_op jit(solution)/shard_map/ppermute | solution.py:245
  28.4 1.0 add_convert_fusion.4
  29.4 10.9 %collective-permute-start.2 = (bf16[96,256]{1,0:T(8,128)(2,1)S(1)}, bf16[96,256]{1,0:T(8,128)(2,1)S(1)}, u32[]{:S(2)}, u32[]{:S(2)}) collective-permute-start(bf16[96,256]{1,0:T(8,128)(2,1)S(1)} %add_convert_fusion.4), channel_id=1, source_target_pairs={{0,128},{32,160},{64,192},{96,224},{128,0},{160,32},{192,64},{224,... | collective-permute-start | bytes 147464 | tf_op jit(solution)/shard_map/ppermute | solution.py:245
  40.4 2.0 %collective-permute-done.2 = bf16[96,256]{1,0:T(8,128)(2,1)S(1)} collective-permute-done((bf16[96,256]{1,0:T(8,128)(2,1)S(1)}, bf16[96,256]{1,0:T(8,128)(2,1)S(1)}, u32[]{:S(2)}, u32[]{:S(2)}) %collective-permute-start.2) | collective-permute-done | bytes 49184 | tf_op jit(solution)/shard_map/ppermute | solution.py:245
  42.4 1.0 add_convert_fusion.3
  43.4 8.0 %collective-permute-start.3 = (bf16[96,256]{1,0:T(8,128)(2,1)S(1)}, bf16[96,256]{1,0:T(8,128)(2,1)S(1)}, u32[]{:S(2)}, u32[]{:S(2)}) collective-permute-start(bf16[96,256]{1,0:T(8,128)(2,1)S(1)} %add_convert_fusion.3), channel_id=1, source_target_pairs={{0,512},{32,544},{64,576},{96,608},{128,640},{160,672},{192,704},{... | collective-permute-start | bytes 147464 | tf_op jit(solution)/shard_map/ppermute | solution.py:245
  51.4 2.1 %collective-permute-done.3 = bf16[96,256]{1,0:T(8,128)(2,1)S(1)} collective-permute-done((bf16[96,256]{1,0:T(8,128)(2,1)S(1)}, bf16[96,256]{1,0:T(8,128)(2,1)S(1)}, u32[]{:S(2)}, u32[]{:S(2)}) %collective-permute-start.3) | collective-permute-done | bytes 49184 | tf_op jit(solution)/shard_map/ppermute | solution.py:245
  53.4 14.2 %collective-permute-start.4 = (bf16[96,256]{1,0:T(8,128)(2,1)S(1)}, bf16[96,256]{1,0:T(8,128)(2,1)S(1)}, u32[]{:S(2)}, u32[]{:S(2)}) collective-permute-start(bf16[96,256]{1,0:T(8,128)(2,1)S(1)} %add_convert_fusion.2), channel_id=1, source_target_pairs={{0,384},{32,416},{64,448},{96,480},{128,256},{160,288},{192,320},{... | collective-permute-start | bytes 147464 | tf_op jit(solution)/shard_map/ppermute | solution.py:245
  67.6 2.2 %collective-permute-done.4 = bf16[96,256]{1,0:T(8,128)(2,1)S(1)} collective-permute-done((bf16[96,256]{1,0:T(8,128)(2,1)S(1)}, bf16[96,256]{1,0:T(8,128)(2,1)S(1)}, u32[]{:S(2)}, u32[]{:S(2)}) %collective-permute-start.4) | collective-permute-done | bytes 49184 | tf_op jit(solution)/shard_map/ppermute | solution.py:245
  69.9 2.2 %collective-permute-start.5 = (bf16[384,2176]{1,0:T(8,128)(2,1)S(1)}, bf16[384,2176]{1,0:T(8,128)(2,1)S(1)}, u32[]{:S(2)}, u32[]{:S(2)}) collective-permute-start(bf16[384,2176]{1,0:T(8,128)(2,1)S(1)} %bitcast.24), channel_id=1, source_target_pairs={{0,1},{1,0},{2,3},{3,2},{4,5},{5,4},{6,7},{7,6},{8,9},{9,8},{10,11... | collective-permute-start | bytes 5013512 | tf_op jit(solution)/shard_map/ppermute | solution.py:339
  72.1 5.3 %collective-permute-start.6 = (bf16[96,256]{1,0:T(8,128)(2,1)S(1)}, bf16[96,256]{1,0:T(8,128)(2,1)S(1)}, u32[]{:S(2)}, u32[]{:S(2)}) collective-permute-start(bf16[96,256]{1,0:T(8,128)(2,1)S(1)} %add_convert_fusion.1), channel_id=1, source_target_pairs={{0,128},{32,160},{64,192},{96,224},{128,0},{160,32},{192,64},{224,... | collective-permute-start | bytes 147464 | tf_op jit(solution)/shard_map/ppermute | solution.py:245
  77.4 1.4 %shard_map.131 = (bf16[384,2048]{1,0:T(8,128)(2,1)S(1)}, f32[2,96,128]{2,1,0:T(8,128)S(1)}) custom-call(bf16[384,2176]{1,0:T(8,128)(2,1)S(1)} %bitcast.25), custom_call_target="tpu_custom_call" | custom-call | flops 1000000000 | bytes 10000000 | tf_op jit(solution)/shard_map/pallas_call | solution.py:340
  78.9 1.8 %shard_map.132 = (bf16[192,2048]{1,0:T(8,128)(2,1)S(1)}, f32[192,2048]{1,0:T(8,128)S(1)}, bf16[192,2048]{1,0:T(8,128)(2,1)S(1)}, f32[192,384]{1,0:T(8,128)S(1)},...) custom-call(bf16[384,2048]{1,0:T(8,128)(2,1)S(1)} %get-tuple-element.45.own, ...), custom_call_target="tpu_custom_call" | custom-call | flops 1000000000 | bytes 10000000 | tf_op jit(solution)/shard_map/pallas_call | solution.py:353
  80.7 1.3 %collective-permute-done.6 = bf16[96,256]{1,0:T(8,128)(2,1)S(1)} collective-permute-done((bf16[96,256]{1,0:T(8,128)(2,1)S(1)}, bf16[96,256]{1,0:T(8,128)(2,1)S(1)}, u32[]{:S(2)}, u32[]{:S(2)}) %collective-permute-start.6) | collective-permute-done | bytes 49184 | tf_op jit(solution)/shard_map/ppermute | solution.py:245
  82.1 1.9 %collective-permute-start.7 = (bf16[192,2048]{1,0:T(8,128)(2,1)S(1)}, bf16[192,2048]{1,0:T(8,128)(2,1)S(1)}, u32[]{:S(2)}, u32[]{:S(2)}) collective-permute-start(bf16[192,2048]{1,0:T(8,128)(2,1)S(1)} %get-tuple-element.49), channel_id=1, source_target_pairs={{0,1},{1,0},{2,3},{3,2},{4,5},{5,4},{6,7},{7,6},{8,9},{9,8},{10,11... | collective-permute-start | bytes 2359304 | tf_op jit(solution)/shard_map/ppermute | solution.py:367
  84.0 5.2 %collective-permute-start.8 = (bf16[192,256]{1,0:T(8,128)(2,1)S(1)}, bf16[192,256]{1,0:T(8,128)(2,1)S(1)}, u32[]{:S(2)}, u32[]{:S(2)}) collective-permute-start(bf16[192,256]{1,0:T(8,128)(2,1)S(1)} %pad_maximum_fusion), channel_id=1, source_target_pairs={{0,64},{32,96},{64,0},{96,32},{128,192},{160,224},{192,128},{224,1... | collective-permute-start | bytes 294920 | tf_op jit(solution)/shard_map/ppermute | solution.py:245
  89.2 2.0 %shard_map.133 = (bf16[192,2048]{1,0:T(8,128)(2,1)S(1)}, bf16[192,2048]{1,0:T(8,128)(2,1)S(1)}, bf16[192,2048]{1,0:T(8,128)(2,1)S(1)}, f32[2,192,128]{2,1,0:T(8,...) custom-call(bf16[384,2048]{1,0:T(8,128)(2,1)S(1)} %get-tuple-element.45.own, ...), custom_call_target="tpu_custom_call" | custom-call | flops 1000000000 | bytes 10000000 | tf_op jit(solution)/shard_map/pallas_call | solution.py:369
  91.2 2.3 %shard_map.134 = (bf16[192,2048]{1,0:T(8,128)(2,1)S(1)}, bf16[192,384]{1,0:T(8,128)(2,1)S(1)}, bf16[192,384]{1,0:T(8,128)(2,1)S(1)}, f32[192,2048]{1,0:T(8,128)S...) custom-call(f32[192,2048]{1,0:T(8,128)S(1)} %get-tuple-element.46.pa, ...), custom_call_target="tpu_custom_call" | custom-call | flops 1000000000 | bytes 10000000 | tf_op jit(solution)/shard_map/pallas_call | solution.py:381
  93.5 1.3 %collective-permute-done.8 = bf16[192,256]{1,0:T(8,128)(2,1)S(1)} collective-permute-done((bf16[192,256]{1,0:T(8,128)(2,1)S(1)}, bf16[192,256]{1,0:T(8,128)(2,1)S(1)}, u32[]{:S(2)}, u32[]{:S(2)}) %collective-permute-start.8) | collective-permute-done | bytes 98336 | tf_op jit(solution)/shard_map/ppermute | solution.py:245
  94.7 1.9 %collective-permute-start.9 = (bf16[192,2048]{1,0:T(8,128)(2,1)S(1)}, bf16[192,2048]{1,0:T(8,128)(2,1)S(1)}, u32[]{:S(2)}, u32[]{:S(2)}) collective-permute-start(bf16[192,2048]{1,0:T(8,128)(2,1)S(1)} %get-tuple-element.63), channel_id=1, source_target_pairs={{0,1},{1,0},{2,3},{3,2},{4,5},{5,4},{6,7},{7,6},{8,9},{9,8},{10,11... | collective-permute-start | bytes 2359304 | tf_op jit(solution)/shard_map/ppermute | solution.py:397
  96.7 3.0 %collective-permute-start.10 = (bf16[384,256]{1,0:T(8,128)(2,1)S(1)}, bf16[384,256]{1,0:T(8,128)(2,1)S(1)}, u32[]{:S(2)}, u32[]{:S(2)}) collective-permute-start(bf16[384,256]{1,0:T(8,128)(2,1)S(1)} %constant_dynamic-update-slice_fusion.held_pieces), channel_id=1, source_target_pairs={{0,32},{32,0},{64,96},{96,64},{128,160},{160,128},{192,224},{224,1... | collective-permute-start | bytes 589832 | tf_op jit(solution)/shard_map/ppermute | solution.py:245
  99.7 3.0 %shard_map.135 = (f32[3,32,2048]{2,1,0:T(8,128)S(1)}, f32[32,2048]{1,0:T(8,128)S(1)}, f32[2,192,32]{2,1,0:T(8,128)S(1)}, bf16[192,32]{1,0:T(8,128)(2,1)S(1)}) custom-call(s32[12]{0:T(128)S(1)} %copy-done.4, bf16[2048,384]{1,0:T(8,128)(2,1)S(1)} %bitcast.17, bf16[2048,384]{1,0:T(8,128)(2,1)S(1)} %bitcast.20, bf16[384,2048]{1,0:T(8,128)(2,1)S(1)} %bitcast.23, ...), custom_call_target="tpu_custom_call" | custom-call | flops 1000000000 | bytes 10000000 | tf_op jit(solution)/shard_map/pallas_call | solution.py:401
  102.8 2.7 %shard_map.136 = f32[1,1,3,32,2048]{4,3,2,1,0:T(8,128)} custom-call(f32[192,2048]{1,0:T(8,128)S(1)} %get-tuple-element.60.partial, bf16[192,2048]{1,0:T(8,128)(2,1)S(1)} %collective-permute-done.9.received, bf16[192,2048]{1,0:T(8,128)(2,1)S(1)} %get-tuple-element.64.t2, f32[2,192,128]{2,1,0:T(8,128)S(1)} %get-tuple-element.53.w, ...), custom_call_target="tpu_custom_call" | custom-call | flops 1000000000 | bytes 10000000 | tf_op jit(solution)/shard_map/pallas_call | solution.py:419
  105.4 0.5 collective-permute-done.10.got_pieces
  105.9 1.4 %shard_map.137 = (f32[96,2048]{1,0:T(8,128)}, f32[96,2048]{1,0:T(8,128)}) custom-call(s32[1]{0:T(128)} %bitcast.9.me, bf16[384,256]{1,0:T(8,128)(2,1)S(1)} %constant_dynamic-update-slice_fusion.held_pieces, bf16[384,256]{1,0:T(8,128)(2,1)S(1)} %collective-permute-done.10.got_pieces, f32[96,2048]{1,0:T(8,128)S(1)} %bitcast.27, f32[96,2048]{1,0:T(8,128)S(1)} %bitcast.28), custom_call_target="tpu_custom_call" | custom-call | flops 1000000000 | bytes 10000000 | tf_op jit(solution)/shard_map/pallas_call | solution.py:423
  (22 shorter events, 0.1 us)
Async XLA Ops:
  1.6 9.2 %collective-permute-start = (bf16[96,1024]{1,0:T(8,128)(2,1)S(1)}, bf16[96,1024]{1,0:T(8,128)(2,1)S(1)}, u32[]{:S(2)}, u32[]{:S(2)}) collective-permute-start(bf16[96,1024]{1,0:T(8,128)(2,1)S(1)} %constant_dynamic-slice_fusion), channel_id=1, source_target_pairs={{0,32},{32,0},{64,96},{96,64},{128,160},{160,128},{192,224},{224,1... | collective-permute-start | bytes 589832 | tf_op jit(solution)/shard_map/ppermute | solution.py:245
  10.8 59.1 %all-to-all-start = ((bf16[16,24,2176]{2,1,0:T(8,128)(2,1)}), bf16[16,24,2176]{2,1,0:T(8,128)(2,1)S(1)}, u32[]{:S(2)}, u32[]{:S(2)}) async-start(bf16[16,24,2176]{2,1,0:T(8,128)(2,1)} %bitcast.29), calls=%async_computation | async-start | bytes 3342336 | tf_op jit(solution)/shard_map/all_to_all | solution.py:330
  18.3 60.6 %copy-start.2 = (bf16[1,384,2048]{2,1,0:T(8,128)(2,1)S(1)}, bf16[1,384,2048]{2,1,0:T(8,128)(2,1)}, u32[]{:S(2)}) copy-start(bf16[1,384,2048]{2,1,0:T(8,128)(2,1)} %param.17) | copy-start | bytes 4718596
  19.5 8.9 %collective-permute-start.1 = (bf16[96,512]{1,0:T(8,128)(2,1)S(1)}, bf16[96,512]{1,0:T(8,128)(2,1)}, u32[]{:S(2)}, u32[]{:S(2)}) collective-permute-start(bf16[96,512]{1,0:T(8,128)(2,1)S(1)} %add_convert_fusion), channel_id=1, source_target_pairs={{0,64},{32,96},{64,0},{96,32},{128,192},{160,224},{192,128},{224,1... | collective-permute-start | bytes 294920 | tf_op jit(solution)/shard_map/ppermute | solution.py:245
  29.4 13.0 %collective-permute-start.2 = (bf16[96,256]{1,0:T(8,128)(2,1)S(1)}, bf16[96,256]{1,0:T(8,128)(2,1)S(1)}, u32[]{:S(2)}, u32[]{:S(2)}) collective-permute-start(bf16[96,256]{1,0:T(8,128)(2,1)S(1)} %add_convert_fusion.4), channel_id=1, source_target_pairs={{0,128},{32,160},{64,192},{96,224},{128,0},{160,32},{192,64},{224,... | collective-permute-start | bytes 147464 | tf_op jit(solution)/shard_map/ppermute | solution.py:245
  43.4 10.0 %collective-permute-start.3 = (bf16[96,256]{1,0:T(8,128)(2,1)S(1)}, bf16[96,256]{1,0:T(8,128)(2,1)S(1)}, u32[]{:S(2)}, u32[]{:S(2)}) collective-permute-start(bf16[96,256]{1,0:T(8,128)(2,1)S(1)} %add_convert_fusion.3), channel_id=1, source_target_pairs={{0,512},{32,544},{64,576},{96,608},{128,640},{160,672},{192,704},{... | collective-permute-start | bytes 147464 | tf_op jit(solution)/shard_map/ppermute | solution.py:245
  53.4 16.4 %collective-permute-start.4 = (bf16[96,256]{1,0:T(8,128)(2,1)S(1)}, bf16[96,256]{1,0:T(8,128)(2,1)S(1)}, u32[]{:S(2)}, u32[]{:S(2)}) collective-permute-start(bf16[96,256]{1,0:T(8,128)(2,1)S(1)} %add_convert_fusion.2), channel_id=1, source_target_pairs={{0,384},{32,416},{64,448},{96,480},{128,256},{160,288},{192,320},{... | collective-permute-start | bytes 147464 | tf_op jit(solution)/shard_map/ppermute | solution.py:245
  69.9 9.0 %copy-start = (bf16[1,2048,384]{2,1,0:T(8,128)(2,1)S(1)}, bf16[1,2048,384]{2,1,0:T(8,128)(2,1)}, u32[]{:S(2)}) copy-start(bf16[1,2048,384]{2,1,0:T(8,128)(2,1)} %param.15) | copy-start | bytes 4718596
  69.9 9.0 %copy-start.1 = (bf16[1,2048,384]{2,1,0:T(8,128)(2,1)S(1)}, bf16[1,2048,384]{2,1,0:T(8,128)(2,1)}, u32[]{:S(2)}) copy-start(bf16[1,2048,384]{2,1,0:T(8,128)(2,1)} %param.16) | copy-start | bytes 4718596
  69.9 9.0 %collective-permute-start.5 = (bf16[384,2176]{1,0:T(8,128)(2,1)S(1)}, bf16[384,2176]{1,0:T(8,128)(2,1)S(1)}, u32[]{:S(2)}, u32[]{:S(2)}) collective-permute-start(bf16[384,2176]{1,0:T(8,128)(2,1)S(1)} %bitcast.24), channel_id=1, source_target_pairs={{0,1},{1,0},{2,3},{3,2},{4,5},{5,4},{6,7},{7,6},{8,9},{9,8},{10,11... | collective-permute-start | bytes 5013512 | tf_op jit(solution)/shard_map/ppermute | solution.py:339
  72.1 9.9 %collective-permute-start.6 = (bf16[96,256]{1,0:T(8,128)(2,1)S(1)}, bf16[96,256]{1,0:T(8,128)(2,1)S(1)}, u32[]{:S(2)}, u32[]{:S(2)}) collective-permute-start(bf16[96,256]{1,0:T(8,128)(2,1)S(1)} %add_convert_fusion.1), channel_id=1, source_target_pairs={{0,128},{32,160},{64,192},{96,224},{128,0},{160,32},{192,64},{224,... | collective-permute-start | bytes 147464 | tf_op jit(solution)/shard_map/ppermute | solution.py:245
  82.1 9.1 %collective-permute-start.7 = (bf16[192,2048]{1,0:T(8,128)(2,1)S(1)}, bf16[192,2048]{1,0:T(8,128)(2,1)S(1)}, u32[]{:S(2)}, u32[]{:S(2)}) collective-permute-start(bf16[192,2048]{1,0:T(8,128)(2,1)S(1)} %get-tuple-element.49), channel_id=1, source_target_pairs={{0,1},{1,0},{2,3},{3,2},{4,5},{5,4},{6,7},{7,6},{8,9},{9,8},{10,11... | collective-permute-start | bytes 2359304 | tf_op jit(solution)/shard_map/ppermute | solution.py:367
  84.0 10.7 %collective-permute-start.8 = (bf16[192,256]{1,0:T(8,128)(2,1)S(1)}, bf16[192,256]{1,0:T(8,128)(2,1)S(1)}, u32[]{:S(2)}, u32[]{:S(2)}) collective-permute-start(bf16[192,256]{1,0:T(8,128)(2,1)S(1)} %pad_maximum_fusion), channel_id=1, source_target_pairs={{0,64},{32,96},{64,0},{96,32},{128,192},{160,224},{192,128},{224,1... | collective-permute-start | bytes 294920 | tf_op jit(solution)/shard_map/ppermute | solution.py:245
  91.2 8.5 %copy-start.3 = (f32[1,3,32,2048]{3,2,1,0:T(8,128)S(1)}, f32[1,3,32,2048]{3,2,1,0:T(8,128)}, u32[]{:S(2)}) copy-start(f32[1,3,32,2048]{3,2,1,0:T(8,128)} %param.19) | copy-start | bytes 2359300
  91.2 8.5 %copy-start.4 = (s32[12]{0:T(128)S(1)}, s32[12]{0:T(128)}, u32[]{:S(2)}) copy-start(s32[12]{0:T(128)} %index.1) | copy-start | bytes 148
  94.7 8.0 %collective-permute-start.9 = (bf16[192,2048]{1,0:T(8,128)(2,1)S(1)}, bf16[192,2048]{1,0:T(8,128)(2,1)S(1)}, u32[]{:S(2)}, u32[]{:S(2)}) collective-permute-start(bf16[192,2048]{1,0:T(8,128)(2,1)S(1)} %get-tuple-element.63), channel_id=1, source_target_pairs={{0,1},{1,0},{2,3},{3,2},{4,5},{5,4},{6,7},{7,6},{8,9},{9,8},{10,11... | collective-permute-start | bytes 2359304 | tf_op jit(solution)/shard_map/ppermute | solution.py:397
  96.7 9.2 %collective-permute-start.10 = (bf16[384,256]{1,0:T(8,128)(2,1)S(1)}, bf16[384,256]{1,0:T(8,128)(2,1)S(1)}, u32[]{:S(2)}, u32[]{:S(2)}) collective-permute-start(bf16[384,256]{1,0:T(8,128)(2,1)S(1)} %constant_dynamic-update-slice_fusion.held_pieces), channel_id=1, source_target_pairs={{0,32},{32,0},{64,96},{96,64},{128,160},{160,128},{192,224},{224,1... | collective-permute-start | bytes 589832 | tf_op jit(solution)/shard_map/ppermute | solution.py:245
  102.7 3.1 %copy-start.5 = (f32[1,3,32,2048]{3,2,1,0:T(8,128)S(1)}, f32[1,3,32,2048]{3,2,1,0:T(8,128)}, u32[]{:S(2)}) copy-start(f32[1,3,32,2048]{3,2,1,0:T(8,128)} %param.20) | copy-start | bytes 2359300

commit v5 on v4

--- a/solution.py
+++ b/solution.py
@@ -189,30 +189,33 @@
     sent[...] = result.astype(BF16)
 
 
+def start_kernel(index, gate, up, down, global_fragment, base, down_rows):
+    start = index[0] * FRAG
+    pick = (iota((FRAG, FS), 1) == iota((FRAG, FS), 0) + start).astype(BF16)
+    base[0] = global_fragment[0] - mm(pick, gate[...], 1, 1)
+    base[1] = global_fragment[1] - mm(pick, up[...], 1, 1)
+    rows = mm(pick, down[...])
+    base[2] = global_fragment[2] - rows
+    down_rows[...] = rows
+
+
 def fragment_kernel(
-    index, gate, up, down, x1, cot, gate_first, up_first, hidden1, hidden2, act2, slope_up2,
-    global_fragment, base, down_part, frag2, hidden_frag2,
+    index, x1, cot, gate_first, up_first, hidden1, hidden2, act2, slope_up2, start_base,
+    down_rows, base, down_part, frag2, hidden_frag2,
 ):
     start = index[0] * FRAG
-    pick = iota((FS, FRAG), 0) == iota((FS, FRAG), 1) + start
-    pick_t = (iota((FRAG, FS), 1) == iota((FRAG, FS), 0) + start).astype(BF16)
-    pick_f = pick.astype(F32)
-    pick = pick.astype(BF16)
+    pick = (iota((FS, FRAG), 0) == iota((FS, FRAG), 1) + start).astype(BF16)
     gate_f = mm(gate_first[...], pick).astype(BF16)
     up_f = mm(up_first[...], pick).astype(BF16)
     hidden_f = mm(hidden1[...], pick).astype(BF16)
-    base[0] = global_fragment[0] - (
-        mm(pick_t, gate[...], 1, 1) - INNER_RATE * (mm(gate_f, x1[...], 0, 0) * SCALE_MODEL)
-    )
-    base[1] = global_fragment[1] - (
-        mm(pick_t, up[...], 1, 1) - INNER_RATE * (mm(up_f, x1[...], 0, 0) * SCALE_MODEL)
-    )
-    down_rows = mm(pick_t, down[...])
-    new_rows = down_rows - INNER_RATE * (mm(hidden_f, cot[...], 0, 0) * SCALE_HIDDEN)
-    down_part[...] = new_rows
-    base[2] = global_fragment[2] - new_rows
-    frag2[0] = mm(slope_up2[...], pick_f, precision=lax.Precision.HIGHEST)
-    frag2[1] = mm(act2[...], pick_f, precision=lax.Precision.HIGHEST)
+    base[0] = start_base[0] + INNER_RATE * (mm(gate_f, x1[...], 0, 0) * SCALE_MODEL)
+    base[1] = start_base[1] + INNER_RATE * (mm(up_f, x1[...], 0, 0) * SCALE_MODEL)
+    step = INNER_RATE * (mm(hidden_f, cot[...], 0, 0) * SCALE_HIDDEN)
+    down_part[...] = down_rows[...] - step
+    base[2] = start_base[2] + step
+    for k, values in enumerate((slope_up2, act2)):
+        high, low = split_two(values[...])
+        frag2[k] = mm(high, pick) + mm(low, pick)
     hidden_frag2[...] = mm(hidden2[...], pick).astype(BF16)
 
 
@@ -335,7 +338,18 @@
         tiled=True,
         axis_index_groups=same_core,
     ).reshape(rows, D + EXT)
-    own, pieces = lax.optimization_barrier((own, pieces))
+    gate, up, down = gate_weight[0], up_weight[0], down_weight[0]
+    start_base, down_rows = pl.pallas_call(
+        start_kernel,
+        out_shape=(sds((3, FRAG, D), F32), sds((FRAG, D), F32)),
+        in_specs=[pl.BlockSpec(memory_space=pltpu.SMEM)]
+        + [pl.BlockSpec(memory_space=pltpu.VMEM)] * 4,
+        compiler_params=pltpu.CompilerParams(vmem_limit_bytes=56 * 1024 * 1024),
+        cost_estimate=pl.CostEstimate(
+            flops=1_000_000_000, bytes_accessed=10_000_000, transcendentals=0
+        ),
+    )(fragment_index, gate, up, down, global_fragment[0])
+    own, pieces, start_base = lax.optimization_barrier((own, pieces, start_base))
     other = lax.ppermute(own, "expert", pairs)
     own_rows, w_own = call(
         functools.partial(own_kernel, cap),
@@ -348,7 +362,6 @@
     held = []
     for distance in gather[:-2]:
         held.append(swap(pieces, distance))
-    gate, up, down = gate_weight[0], up_weight[0], down_weight[0]
 
     x1, partial, sent, act, slope_up, hidden1 = call(
         functools.partial(first_kernel, cap),
@@ -407,14 +420,14 @@
             sds((slots, FRAG), BF16),
         ),
         in_specs=[pl.BlockSpec(memory_space=pltpu.SMEM)]
-        + [pl.BlockSpec(memory_space=pltpu.VMEM)] * 12,
+        + [pl.BlockSpec(memory_space=pltpu.VMEM)] * 10,
         compiler_params=pltpu.CompilerParams(vmem_limit_bytes=20 * 1024 * 1024),
         cost_estimate=pl.CostEstimate(
             flops=1_000_000_000, bytes_accessed=10_000_000, transcendentals=0
         ),
     )(
-        fragment_index, gate, up, down, x1, cot, gate_first, up_first, hidden1, hidden2, act2,
-        slope_up2, global_fragment[0],
+        fragment_index, x1, cot, gate_first, up_first, hidden1, hidden2, act2, slope_up2,
+        start_base, down_rows,
     )
     next_delta = call(last_kernel, sds((1, 1, 3, FRAG, D), F32))(
         partial2, received2, t2, w, x2, down_part, frag2, hidden_frag2, base

time: 108 us -> 113 us (1.046)
  waiting for transfers between devices: 13.4 us -> 20.5 us
  Pallas kernels: 18.2 us -> 21.7 us
  other arithmetic: 3.18 us -> 0.34 us
  starting transfers between devices: 70.5 us -> 67.9 us
    ppermute x8, waiting for transfers between devices: 13.4 us -> 20.5 us  [swap(): lax.ppermute(values, 'replica', [(i, i ^ distance) for i in range(replica...]
    pallas_call x0 -> x1, Pallas kernels: none -> 4.99 us  [shards(): pl.pallas_call(start_kernel, out_shape=(sds((3, FRAG, D), F32), sds((FRAG...]
    ppermute x8, starting transfers between devices: 56.9 us -> 54.1 us  [swap(): lax.ppermute(values, 'replica', [(i, i ^ distance) for i in range(replica...]
    convert_element_type x2, other arithmetic: 2.13 us -> 0.2 us  [halve(): return kept + [swap(sent.astype(BF16), distance)]]
    pallas_call x1, Pallas kernels: 3.05 us -> 1.59 us  [shards(): pl.pallas_call(fragment_kernel, out_shape=(sds((3, FRAG, D), F32), sds((F...]
  transfers between devices with their start and end apart: 12 -> 12, of which waited for: 8 -> 7; matrix products, arithmetic and copies ran while one was open for 3% -> 0% of each run, Pallas kernels for 16% -> 18%
where the time goes in v5:
time: 113 us
  starting transfers between devices  67.9 us (60%)
  Pallas kernels  21.7 us (19%)
  waiting for transfers between devices  20.5 us (18%)
    ppermute x8, starting transfers between devices, swap(): lax.ppermute(values, 'replica', [(i, i ^ distance) for i in range(replica...  54.1 us
    ppermute x8, waiting for transfers between devices, swap(): lax.ppermute(values, 'replica', [(i, i ^ distance) for i in range(replica...  20.5 us
    all_to_all x1, starting transfers between devices, shards(): lax.all_to_all(table.reshape(experts, 4 * cap, D + EXT), 'expert', split_...  7.7 us
    pallas_call x1, Pallas kernels, shards(): pl.pallas_call(start_kernel, out_shape=(sds((3, FRAG, D), F32), sds((FRAG...  4.99 us
    pallas_call x1, Pallas kernels, shards(): call(functools.partial(pack_kernel, cap), sds((rows, D + EXT), BF16), 56)  3.62 us
    pallas_call x1, Pallas kernels, shards(): call(last_kernel, sds((1, 1, 3, FRAG, D), F32))  2.68 us
  transfers between devices with their start and end apart: 12, of which 7 were waited for; matrix products, arithmetic and copies ran while one was open for 0% of the time, Pallas kernels for 18%

profile of v5, /device:TPU:56, one launch (start us, length us, event | category | flops | bytes accessed | tf_op | source)
XLA Modules:
  0.0 112.5 jit_solution(16581723971363421269)
XLA Ops:
  0.6 0.9 constant_dynamic-slice_fusion
  1.6 4.3 %collective-permute-start = (bf16[96,1024]{1,0:T(8,128)(2,1)S(1)}, bf16[96,1024]{1,0:T(8,128)(2,1)S(1)}, u32[]{:S(2)}, u32[]{:S(2)}) collective-permute-start(bf16[96,1024]{1,0:T(8,128)(2,1)S(1)} %constant_dynamic-slice_fusion), channel_id=1, source_target_pairs={{0,32},{32,0},{64,96},{96,64},{128,160},{160,128},{192,224},{224,1... | collective-permute-start | bytes 589832 | tf_op jit(solution)/shard_map/ppermute | solution.py:248
  5.9 3.6 %shard_map.130 = bf16[384,2176]{1,0:T(8,128)(2,1)} custom-call(bf16[2,64,2048]{2,1,0:T(8,128)(2,1)} %tokens.1, bf16[2,64,2048]{2,1,0:T(8,128)(2,1)} %targets.1, s32[2,1,64]{2,1,0:T(1,128)} %bitcast.34, f32[2,64]{1,0:T(2,128)} %weight.1), custom_call_target="tpu_custom_call" | custom-call | flops 1000000000 | bytes 10000000 | tf_op jit(solution)/shard_map/pallas_call | solution.py:317
  9.5 1.3 %collective-permute-done = bf16[96,1024]{1,0:T(8,128)(2,1)S(1)} collective-permute-done((bf16[96,1024]{1,0:T(8,128)(2,1)S(1)}, bf16[96,1024]{1,0:T(8,128)(2,1)S(1)}, u32[]{:S(2)}, u32[]{:S(2)}) %collective-permute-start) | collective-permute-done | bytes 196640 | tf_op jit(solution)/shard_map/ppermute | solution.py:248
  10.8 7.7 %all-to-all-start = ((bf16[16,24,2176]{2,1,0:T(8,128)(2,1)}), bf16[16,24,2176]{2,1,0:T(8,128)(2,1)S(1)}, u32[]{:S(2)}, u32[]{:S(2)}) async-start(bf16[16,24,2176]{2,1,0:T(8,128)(2,1)} %bitcast.29), calls=%async_computation | async-start | bytes 3342336 | tf_op jit(solution)/shard_map/all_to_all | solution.py:333
  18.5 0.1 add_convert_fusion
  18.6 6.1 %collective-permute-start.1 = (bf16[96,512]{1,0:T(8,128)(2,1)S(1)}, bf16[96,512]{1,0:T(8,128)(2,1)S(1)}, u32[]{:S(2)}, u32[]{:S(2)}) collective-permute-start(bf16[96,512]{1,0:T(8,128)(2,1)S(1)} %add_convert_fusion), channel_id=1, source_target_pairs={{0,64},{32,96},{64,0},{96,32},{128,192},{160,224},{192,128},{224,1... | collective-permute-start | bytes 294920 | tf_op jit(solution)/shard_map/ppermute | solution.py:248
  24.7 2.7 %collective-permute-done.1 = bf16[96,512]{1,0:T(8,128)(2,1)S(1)} collective-permute-done((bf16[96,512]{1,0:T(8,128)(2,1)S(1)}, bf16[96,512]{1,0:T(8,128)(2,1)S(1)}, u32[]{:S(2)}, u32[]{:S(2)}) %collective-permute-start.1) | collective-permute-done | bytes 98336 | tf_op jit(solution)/shard_map/ppermute | solution.py:248
  27.4 0.1 add_convert_fusion.4
  27.5 10.9 %collective-permute-start.2 = (bf16[96,256]{1,0:T(8,128)(2,1)S(1)}, bf16[96,256]{1,0:T(8,128)(2,1)S(1)}, u32[]{:S(2)}, u32[]{:S(2)}) collective-permute-start(bf16[96,256]{1,0:T(8,128)(2,1)S(1)} %add_convert_fusion.4), channel_id=1, source_target_pairs={{0,128},{32,160},{64,192},{96,224},{128,0},{160,32},{192,64},{224,... | collective-permute-start | bytes 147464 | tf_op jit(solution)/shard_map/ppermute | solution.py:248
  38.5 2.0 %collective-permute-done.2 = bf16[96,256]{1,0:T(8,128)(2,1)S(1)} collective-permute-done((bf16[96,256]{1,0:T(8,128)(2,1)S(1)}, bf16[96,256]{1,0:T(8,128)(2,1)S(1)}, u32[]{:S(2)}, u32[]{:S(2)}) %collective-permute-start.2) | collective-permute-done | bytes 49184 | tf_op jit(solution)/shard_map/ppermute | solution.py:248
  40.5 0.1 add_convert_fusion.3
  40.6 8.0 %collective-permute-start.3 = (bf16[96,256]{1,0:T(8,128)(2,1)S(1)}, bf16[96,256]{1,0:T(8,128)(2,1)S(1)}, u32[]{:S(2)}, u32[]{:S(2)}) collective-permute-start(bf16[96,256]{1,0:T(8,128)(2,1)S(1)} %add_convert_fusion.3), channel_id=1, source_target_pairs={{0,512},{32,544},{64,576},{96,608},{128,640},{160,672},{192,704},{... | collective-permute-start | bytes 147464 | tf_op jit(solution)/shard_map/ppermute | solution.py:248
  48.6 2.2 %collective-permute-done.3 = bf16[96,256]{1,0:T(8,128)(2,1)S(1)} collective-permute-done((bf16[96,256]{1,0:T(8,128)(2,1)S(1)}, bf16[96,256]{1,0:T(8,128)(2,1)S(1)}, u32[]{:S(2)}, u32[]{:S(2)}) %collective-permute-start.3) | collective-permute-done | bytes 49184 | tf_op jit(solution)/shard_map/ppermute | solution.py:248
  50.7 16.9 %collective-permute-start.4 = (bf16[96,256]{1,0:T(8,128)(2,1)S(1)}, bf16[96,256]{1,0:T(8,128)(2,1)S(1)}, u32[]{:S(2)}, u32[]{:S(2)}) collective-permute-start(bf16[96,256]{1,0:T(8,128)(2,1)S(1)} %add_convert_fusion.2), channel_id=1, source_target_pairs={{0,384},{32,416},{64,448},{96,480},{128,256},{160,288},{192,320},{... | collective-permute-start | bytes 147464 | tf_op jit(solution)/shard_map/ppermute | solution.py:248
  67.7 5.0 %shard_map.131 = (f32[3,32,2048]{2,1,0:T(8,128)}, f32[32,2048]{1,0:T(8,128)}) custom-call(s32[12]{0:T(128)} %index.3, bf16[2048,384]{1,0:T(8,128)(2,1)} %bitcast.15, bf16[2048,384]{1,0:T(8,128)(2,1)} %bitcast.18, bf16[384,2048]{1,0:T(8,128)(2,1)} %bitcast.21, f32[3,32,2048]{2,1,0:T(8,128)} %bitcast.26), custom_call_target="tpu_custom_call" | custom-call | flops 1000000000 | bytes 10000000 | tf_op jit(solution)/shard_map/pallas_call | solution.py:342
  72.7 2.2 %collective-permute-start.5 = (bf16[384,2176]{1,0:T(8,128)(2,1)S(1)}, bf16[384,2176]{1,0:T(8,128)(2,1)S(1)}, u32[]{:S(2)}, u32[]{:S(2)}) collective-permute-start(bf16[384,2176]{1,0:T(8,128)(2,1)S(1)} %bitcast.24), channel_id=1, source_target_pairs={{0,1},{1,0},{2,3},{3,2},{4,5},{5,4},{6,7},{7,6},{8,9},{9,8},{10,11... | collective-permute-start | bytes 5013512 | tf_op jit(solution)/shard_map/ppermute | solution.py:353
  74.9 3.6 %collective-permute-start.6 = (bf16[96,256]{1,0:T(8,128)(2,1)S(1)}, bf16[96,256]{1,0:T(8,128)(2,1)S(1)}, u32[]{:S(2)}, u32[]{:S(2)}) collective-permute-start(bf16[96,256]{1,0:T(8,128)(2,1)S(1)} %add_convert_fusion.1), channel_id=1, source_target_pairs={{0,128},{32,160},{64,192},{96,224},{128,0},{160,32},{192,64},{224,... | collective-permute-start | bytes 147464 | tf_op jit(solution)/shard_map/ppermute | solution.py:248
  78.5 1.5 %shard_map.132 = (bf16[384,2048]{1,0:T(8,128)(2,1)S(1)}, f32[2,96,128]{2,1,0:T(8,128)S(1)}) custom-call(bf16[384,2176]{1,0:T(8,128)(2,1)S(1)} %bitcast.25), custom_call_target="tpu_custom_call" | custom-call | flops 1000000000 | bytes 10000000 | tf_op jit(solution)/shard_map/pallas_call | solution.py:354
  80.0 1.8 %shard_map.133 = (bf16[192,2048]{1,0:T(8,128)(2,1)S(1)}, f32[192,2048]{1,0:T(8,128)S(1)}, bf16[192,2048]{1,0:T(8,128)(2,1)S(1)}, f32[192,384]{1,0:T(8,128)S(1)},...) custom-call(bf16[384,2048]{1,0:T(8,128)(2,1)S(1)} %get-tuple-element.49.own, ...), custom_call_target="tpu_custom_call" | custom-call | flops 1000000000 | bytes 10000000 | tf_op jit(solution)/shard_map/pallas_call | solution.py:366
  81.9 6.1 %collective-permute-done.6 = bf16[96,256]{1,0:T(8,128)(2,1)S(1)} collective-permute-done((bf16[96,256]{1,0:T(8,128)(2,1)S(1)}, bf16[96,256]{1,0:T(8,128)(2,1)S(1)}, u32[]{:S(2)}, u32[]{:S(2)}) %collective-permute-start.6) | collective-permute-done | bytes 49184 | tf_op jit(solution)/shard_map/ppermute | solution.py:248
  88.0 1.9 %collective-permute-start.7 = (bf16[192,2048]{1,0:T(8,128)(2,1)S(1)}, bf16[192,2048]{1,0:T(8,128)(2,1)S(1)}, u32[]{:S(2)}, u32[]{:S(2)}) collective-permute-start(bf16[192,2048]{1,0:T(8,128)(2,1)S(1)} %get-tuple-element.53), channel_id=1, source_target_pairs={{0,1},{1,0},{2,3},{3,2},{4,5},{5,4},{6,7},{7,6},{8,9},{9,8},{10,11... | collective-permute-start | bytes 2359304 | tf_op jit(solution)/shard_map/ppermute | solution.py:380
  89.9 2.4 %collective-permute-start.8 = (bf16[192,256]{1,0:T(8,128)(2,1)S(1)}, bf16[192,256]{1,0:T(8,128)(2,1)S(1)}, u32[]{:S(2)}, u32[]{:S(2)}) collective-permute-start(bf16[192,256]{1,0:T(8,128)(2,1)S(1)} %pad_maximum_fusion), channel_id=1, source_target_pairs={{0,64},{32,96},{64,0},{96,32},{128,192},{160,224},{192,128},{224,1... | collective-permute-start | bytes 294920 | tf_op jit(solution)/shard_map/ppermute | solution.py:248
  92.3 2.0 %shard_map.134 = (bf16[192,2048]{1,0:T(8,128)(2,1)S(1)}, bf16[192,2048]{1,0:T(8,128)(2,1)S(1)}, bf16[192,2048]{1,0:T(8,128)(2,1)S(1)}, f32[2,192,128]{2,1,0:T(8,...) custom-call(bf16[384,2048]{1,0:T(8,128)(2,1)S(1)} %get-tuple-element.49.own, ...), custom_call_target="tpu_custom_call" | custom-call | flops 1000000000 | bytes 10000000 | tf_op jit(solution)/shard_map/pallas_call | solution.py:382
  94.4 2.3 %shard_map.135 = (bf16[192,2048]{1,0:T(8,128)(2,1)S(1)}, bf16[192,384]{1,0:T(8,128)(2,1)S(1)}, bf16[192,384]{1,0:T(8,128)(2,1)S(1)}, f32[192,2048]{1,0:T(8,128)S...) custom-call(f32[192,2048]{1,0:T(8,128)S(1)} %get-tuple-element.50.pa, ...), custom_call_target="tpu_custom_call" | custom-call | flops 1000000000 | bytes 10000000 | tf_op jit(solution)/shard_map/pallas_call | solution.py:394
  96.6 3.4 %collective-permute-done.8 = bf16[192,256]{1,0:T(8,128)(2,1)S(1)} collective-permute-done((bf16[192,256]{1,0:T(8,128)(2,1)S(1)}, bf16[192,256]{1,0:T(8,128)(2,1)S(1)}, u32[]{:S(2)}, u32[]{:S(2)}) %collective-permute-start.8) | collective-permute-done | bytes 98336 | tf_op jit(solution)/shard_map/ppermute | solution.py:248
  100.0 2.0 %collective-permute-start.9 = (bf16[192,2048]{1,0:T(8,128)(2,1)S(1)}, bf16[192,2048]{1,0:T(8,128)(2,1)S(1)}, u32[]{:S(2)}, u32[]{:S(2)}) collective-permute-start(bf16[192,2048]{1,0:T(8,128)(2,1)S(1)} %get-tuple-element.67), channel_id=1, source_target_pairs={{0,1},{1,0},{2,3},{3,2},{4,5},{5,4},{6,7},{7,6},{8,9},{9,8},{10,11... | collective-permute-start | bytes 2359304 | tf_op jit(solution)/shard_map/ppermute | solution.py:410
  102.0 1.9 %collective-permute-start.10 = (bf16[384,256]{1,0:T(8,128)(2,1)S(1)}, bf16[384,256]{1,0:T(8,128)(2,1)S(1)}, u32[]{:S(2)}, u32[]{:S(2)}) collective-permute-start(bf16[384,256]{1,0:T(8,128)(2,1)S(1)} %constant_dynamic-update-slice_fusion.held_pieces), channel_id=1, source_target_pairs={{0,32},{32,0},{64,96},{96,64},{128,160},{160,128},{192,224},{224,1... | collective-permute-start | bytes 589832 | tf_op jit(solution)/shard_map/ppermute | solution.py:248
  104.0 1.6 %shard_map.136 = (f32[3,32,2048]{2,1,0:T(8,128)S(1)}, f32[32,2048]{1,0:T(8,128)S(1)}, f32[2,192,32]{2,1,0:T(8,128)S(1)}, bf16[192,32]{1,0:T(8,128)(2,1)S(1)}) custom-call(s32[12]{0:T(128)S(1)} %copy-done.6, bf16[192,2048]{1,0:T(8,128)(2,1)S(1)} %get-tuple-element.55.x1, bf16[192,2048]{1,0:T(8,128)(2,1)S(1)} %get-tuple-element.70.cot, ...), custom_call_target="tpu_custom_call" | custom-call | flops 1000000000 | bytes 10000000 | tf_op jit(solution)/shard_map/pallas_call | solution.py:414
  105.6 2.7 %shard_map.137 = f32[1,1,3,32,2048]{4,3,2,1,0:T(8,128)} custom-call(f32[192,2048]{1,0:T(8,128)S(1)} %get-tuple-element.64.partial, bf16[192,2048]{1,0:T(8,128)(2,1)S(1)} %collective-permute-done.9.received, bf16[192,2048]{1,0:T(8,128)(2,1)S(1)} %get-tuple-element.68.t2, f32[2,192,128]{2,1,0:T(8,128)S(1)} %get-tuple-element.57.w, ...), custom_call_target="tpu_custom_call" | custom-call | flops 1000000000 | bytes 10000000 | tf_op jit(solution)/shard_map/pallas_call | solution.py:432
  108.3 2.9 %collective-permute-done.10.got_pieces = bf16[384,256]{1,0:T(8,128)(2,1)S(1)} collective-permute-done((bf16[384,256]{1,0:T(8,128)(2,1)S(1)}, bf16[384,256]{1,0:T(8,128)(2,1)S(1)}, u32[]{:S(2)}, u32[]{:S(2)}) %collective-permute-start.10) | collective-permute-done | bytes 196640 | tf_op jit(solution)/shard_map/ppermute | solution.py:248
  111.2 1.4 %shard_map.138 = (f32[96,2048]{1,0:T(8,128)}, f32[96,2048]{1,0:T(8,128)}) custom-call(s32[1]{0:T(128)} %bitcast.9.me, bf16[384,256]{1,0:T(8,128)(2,1)S(1)} %constant_dynamic-update-slice_fusion.held_pieces, bf16[384,256]{1,0:T(8,128)(2,1)S(1)} %collective-permute-done.10.got_pieces, f32[96,2048]{1,0:T(8,128)S(1)} %bitcast.27, f32[96,2048]{1,0:T(8,128)S(1)} %bitcast.28), custom_call_target="tpu_custom_call" | custom-call | flops 1000000000 | bytes 10000000 | tf_op jit(solution)/shard_map/pallas_call | solution.py:436
  (29 shorter events, 0.1 us)
Async XLA Ops:
  1.6 9.2 %collective-permute-start = (bf16[96,1024]{1,0:T(8,128)(2,1)S(1)}, bf16[96,1024]{1,0:T(8,128)(2,1)S(1)}, u32[]{:S(2)}, u32[]{:S(2)}) collective-permute-start(bf16[96,1024]{1,0:T(8,128)(2,1)S(1)} %constant_dynamic-slice_fusion), channel_id=1, source_target_pairs={{0,32},{32,0},{64,96},{96,64},{128,160},{160,128},{192,224},{224,1... | collective-permute-start | bytes 589832 | tf_op jit(solution)/shard_map/ppermute | solution.py:248
  10.8 7.7 %copy-start.8 = (bf16[1,1,3,32,2048]{4,3,2,1,0:T(8,128)(2,1)S(1)}, bf16[1,1,3,32,2048]{4,3,2,1,0:T(8,128)(2,1)}, u32[]{:S(2)}) copy-start(bf16[1,1,3,32,2048]{4,3,2,1,0:T(8,128)(2,1)} %param.18) | copy-start | bytes 1179652
  10.8 61.9 %all-to-all-start = ((bf16[16,24,2176]{2,1,0:T(8,128)(2,1)}), bf16[16,24,2176]{2,1,0:T(8,128)(2,1)S(1)}, u32[]{:S(2)}, u32[]{:S(2)}) async-start(bf16[16,24,2176]{2,1,0:T(8,128)(2,1)} %bitcast.29), calls=%async_computation | async-start | bytes 3342336 | tf_op jit(solution)/shard_map/all_to_all | solution.py:333
  18.6 8.8 %collective-permute-start.1 = (bf16[96,512]{1,0:T(8,128)(2,1)S(1)}, bf16[96,512]{1,0:T(8,128)(2,1)S(1)}, u32[]{:S(2)}, u32[]{:S(2)}) collective-permute-start(bf16[96,512]{1,0:T(8,128)(2,1)S(1)} %add_convert_fusion), channel_id=1, source_target_pairs={{0,64},{32,96},{64,0},{96,32},{128,192},{160,224},{192,128},{224,1... | collective-permute-start | bytes 294920 | tf_op jit(solution)/shard_map/ppermute | solution.py:248
  27.5 13.0 %collective-permute-start.2 = (bf16[96,256]{1,0:T(8,128)(2,1)S(1)}, bf16[96,256]{1,0:T(8,128)(2,1)S(1)}, u32[]{:S(2)}, u32[]{:S(2)}) collective-permute-start(bf16[96,256]{1,0:T(8,128)(2,1)S(1)} %add_convert_fusion.4), channel_id=1, source_target_pairs={{0,128},{32,160},{64,192},{96,224},{128,0},{160,32},{192,64},{224,... | collective-permute-start | bytes 147464 | tf_op jit(solution)/shard_map/ppermute | solution.py:248
  40.6 10.1 %collective-permute-start.3 = (bf16[96,256]{1,0:T(8,128)(2,1)S(1)}, bf16[96,256]{1,0:T(8,128)(2,1)S(1)}, u32[]{:S(2)}, u32[]{:S(2)}) collective-permute-start(bf16[96,256]{1,0:T(8,128)(2,1)S(1)} %add_convert_fusion.3), channel_id=1, source_target_pairs={{0,512},{32,544},{64,576},{96,608},{128,640},{160,672},{192,704},{... | collective-permute-start | bytes 147464 | tf_op jit(solution)/shard_map/ppermute | solution.py:248
  50.7 21.9 %collective-permute-start.4 = (bf16[96,256]{1,0:T(8,128)(2,1)S(1)}, bf16[96,256]{1,0:T(8,128)(2,1)S(1)}, u32[]{:S(2)}, u32[]{:S(2)}) collective-permute-start(bf16[96,256]{1,0:T(8,128)(2,1)S(1)} %add_convert_fusion.2), channel_id=1, source_target_pairs={{0,384},{32,416},{64,448},{96,480},{128,256},{160,288},{192,320},{... | collective-permute-start | bytes 147464 | tf_op jit(solution)/shard_map/ppermute | solution.py:248
  67.6 12.4 %copy-start.2 = (bf16[1,384,2048]{2,1,0:T(8,128)(2,1)S(1)}, bf16[1,384,2048]{2,1,0:T(8,128)(2,1)}, u32[]{:S(2)}) copy-start(bf16[1,384,2048]{2,1,0:T(8,128)(2,1)} %param.17) | copy-start | bytes 4718596
  72.7 7.3 %copy-start = (bf16[1,2048,384]{2,1,0:T(8,128)(2,1)S(1)}, bf16[1,2048,384]{2,1,0:T(8,128)(2,1)}, u32[]{:S(2)}) copy-start(bf16[1,2048,384]{2,1,0:T(8,128)(2,1)} %param.15) | copy-start | bytes 4718596
  72.7 7.3 %copy-start.1 = (bf16[1,2048,384]{2,1,0:T(8,128)(2,1)S(1)}, bf16[1,2048,384]{2,1,0:T(8,128)(2,1)}, u32[]{:S(2)}) copy-start(bf16[1,2048,384]{2,1,0:T(8,128)(2,1)} %param.16) | copy-start | bytes 4718596
  72.7 7.3 %collective-permute-start.5 = (bf16[384,2176]{1,0:T(8,128)(2,1)S(1)}, bf16[384,2176]{1,0:T(8,128)(2,1)S(1)}, u32[]{:S(2)}, u32[]{:S(2)}) collective-permute-start(bf16[384,2176]{1,0:T(8,128)(2,1)S(1)} %bitcast.24), channel_id=1, source_target_pairs={{0,1},{1,0},{2,3},{3,2},{4,5},{5,4},{6,7},{7,6},{8,9},{9,8},{10,11... | collective-permute-start | bytes 5013512 | tf_op jit(solution)/shard_map/ppermute | solution.py:353
  74.9 13.1 %collective-permute-start.6 = (bf16[96,256]{1,0:T(8,128)(2,1)S(1)}, bf16[96,256]{1,0:T(8,128)(2,1)S(1)}, u32[]{:S(2)}, u32[]{:S(2)}) collective-permute-start(bf16[96,256]{1,0:T(8,128)(2,1)S(1)} %add_convert_fusion.1), channel_id=1, source_target_pairs={{0,128},{32,160},{64,192},{96,224},{128,0},{160,32},{192,64},{224,... | collective-permute-start | bytes 147464 | tf_op jit(solution)/shard_map/ppermute | solution.py:248
  88.0 6.3 %collective-permute-start.7 = (bf16[192,2048]{1,0:T(8,128)(2,1)S(1)}, bf16[192,2048]{1,0:T(8,128)(2,1)S(1)}, u32[]{:S(2)}, u32[]{:S(2)}) collective-permute-start(bf16[192,2048]{1,0:T(8,128)(2,1)S(1)} %get-tuple-element.53), channel_id=1, source_target_pairs={{0,1},{1,0},{2,3},{3,2},{4,5},{5,4},{6,7},{7,6},{8,9},{9,8},{10,11... | collective-permute-start | bytes 2359304 | tf_op jit(solution)/shard_map/ppermute | solution.py:380
  89.9 10.1 %collective-permute-start.8 = (bf16[192,256]{1,0:T(8,128)(2,1)S(1)}, bf16[192,256]{1,0:T(8,128)(2,1)S(1)}, u32[]{:S(2)}, u32[]{:S(2)}) collective-permute-start(bf16[192,256]{1,0:T(8,128)(2,1)S(1)} %pad_maximum_fusion), channel_id=1, source_target_pairs={{0,64},{32,96},{64,0},{96,32},{128,192},{160,224},{192,128},{224,1... | collective-permute-start | bytes 294920 | tf_op jit(solution)/shard_map/ppermute | solution.py:248
  94.3 9.6 %copy-start.4 = (f32[3,32,2048]{2,1,0:T(8,128)S(1)}, f32[3,32,2048]{2,1,0:T(8,128)}, u32[]{:S(2)}) copy-start(f32[3,32,2048]{2,1,0:T(8,128)} %get-tuple-element.76.start_base) | copy-start | bytes 2359300
  94.3 9.6 %copy-start.5 = (f32[32,2048]{1,0:T(8,128)S(1)}, f32[32,2048]{1,0:T(8,128)}, u32[]{:S(2)}) copy-start(f32[32,2048]{1,0:T(8,128)} %get-tuple-element.77.down_rows) | copy-start | bytes 786436
  94.3 9.6 %copy-start.6 = (s32[12]{0:T(128)S(1)}, s32[12]{0:T(128)}, u32[]{:S(2)}) copy-start(s32[12]{0:T(128)} %index.3) | copy-start | bytes 148
  100.0 5.6 %collective-permute-start.9 = (bf16[192,2048]{1,0:T(8,128)(2,1)S(1)}, bf16[192,2048]{1,0:T(8,128)(2,1)S(1)}, u32[]{:S(2)}, u32[]{:S(2)}) collective-permute-start(bf16[192,2048]{1,0:T(8,128)(2,1)S(1)} %get-tuple-element.67), channel_id=1, source_target_pairs={{0,1},{1,0},{2,3},{3,2},{4,5},{5,4},{6,7},{7,6},{8,9},{9,8},{10,11... | collective-permute-start | bytes 2359304 | tf_op jit(solution)/shard_map/ppermute | solution.py:410
  102.0 9.1 %collective-permute-start.10 = (bf16[384,256]{1,0:T(8,128)(2,1)S(1)}, bf16[384,256]{1,0:T(8,128)(2,1)S(1)}, u32[]{:S(2)}, u32[]{:S(2)}) collective-permute-start(bf16[384,256]{1,0:T(8,128)(2,1)S(1)} %constant_dynamic-update-slice_fusion.held_pieces), channel_id=1, source_target_pairs={{0,32},{32,0},{64,96},{96,64},{128,160},{160,128},{192,224},{224,1... | collective-permute-start | bytes 589832 | tf_op jit(solution)/shard_map/ppermute | solution.py:248
  105.6 5.6 %copy-start.3 = (f32[1,3,32,2048]{3,2,1,0:T(8,128)S(1)}, f32[1,3,32,2048]{3,2,1,0:T(8,128)}, u32[]{:S(2)}) copy-start(f32[1,3,32,2048]{3,2,1,0:T(8,128)} %param.19) | copy-start | bytes 2359300
  105.6 5.6 %copy-start.7 = (f32[1,3,32,2048]{3,2,1,0:T(8,128)S(1)}, f32[1,3,32,2048]{3,2,1,0:T(8,128)}, u32[]{:S(2)}) copy-start(f32[1,3,32,2048]{3,2,1,0:T(8,128)} %param.20) | copy-start | bytes 2359300

commit v6 on v3

--- a/solution.py
+++ b/solution.py
@@ -186,7 +186,6 @@
     start = index[0] * FRAG
     pick = iota((FS, FRAG), 0) == iota((FS, FRAG), 1) + start
     pick_t = (iota((FRAG, FS), 1) == iota((FRAG, FS), 0) + start).astype(BF16)
-    pick_f = pick.astype(F32)
     pick = pick.astype(BF16)
     gate_f = mm(gate_first[...], pick).astype(BF16)
     up_f = mm(up_first[...], pick).astype(BF16)
@@ -201,8 +200,9 @@
     new_rows = down_rows - INNER_RATE * (mm(hidden_f, cot[...], 0, 0) * SCALE_HIDDEN)
     down_part[...] = new_rows
     base[2] = global_fragment[2] - new_rows
-    frag2[0] = mm(slope_up2[...], pick_f, precision=lax.Precision.HIGHEST)
-    frag2[1] = mm(act2[...], pick_f, precision=lax.Precision.HIGHEST)
+    for k, values in enumerate((slope_up2, act2)):
+        high, low = split_two(values[...])
+        frag2[k] = mm(high, pick) + mm(low, pick)
     hidden_frag2[...] = mm(hidden2[...], pick).astype(BF16)
 
 
@@ -235,12 +235,19 @@
     return lax.ppermute(values, "replica", [(i, i ^ distance) for i in range(replicas)])
 
 
-def halve(values, distance):
-    half = values.shape[1] // 2
+def halve(terms, distance):
+    half = terms[0].shape[1] // 2
     bit = pick_of(lax.axis_index("replica"), distance)
-    sent = lax.dynamic_slice_in_dim(values, (1 - bit) * half, half, 1)
-    kept = lax.dynamic_slice_in_dim(values, bit * half, half, 1)
-    return kept, swap(sent.astype(BF16), distance)
+    sent = total_of([lax.dynamic_slice_in_dim(t, (1 - bit) * half, half, 1) for t in terms])
+    kept = [lax.dynamic_slice_in_dim(t, bit * half, half, 1) for t in terms]
+    return kept + [swap(sent.astype(BF16), distance)]
+
+
+def total_of(terms):
+    total = terms[0].astype(F32)
+    for term in terms[1:]:
+        total = total + term.astype(F32)
+    return total
 
 
 def add_across(values, distance):
@@ -292,18 +299,17 @@
     pairs = [(i, i ^ 1) for i in range(size)]
 
     inner = inner_of(replicas)
-    kept, got = halve(fragment_delta.reshape(3 * FRAG, D), 1)
+    terms = halve([fragment_delta.reshape(3 * FRAG, D)], 1)
 
     table = call(functools.partial(pack_kernel, cap), sds((rows, D + EXT), BF16), 56)(
         tokens, targets, expert_ids.transpose(0, 2, 1), route_weight
     )
-    table, got = lax.optimization_barrier((table, got))
-    sums = kept.astype(F32) + got.astype(F32)
+    table, terms[-1] = lax.optimization_barrier((table, terms[-1]))
     distance = 2
     while distance < inner:
-        kept, got = halve(sums, distance)
-        sums = kept + got.astype(F32)
+        terms = halve(terms, distance)
         distance *= 2
+    sums = total_of(terms)
     across = []
     while distance < replicas:
         across.insert(0, distance)

time: 109 us -> 108 us (level); the launches traced: 107 us -> 107 us
  waiting for transfers between devices: 10.7 us -> 11.8 us
    add x2 -> x0, other arithmetic: 2.04 us -> none  [the longest x1 1.09 us: shards(): sums = kept.astype(F32) + got.astype(F32)]
    convert_element_type x0 -> x2, other arithmetic: none -> 2.01 us  [halve(): return kept + [swap(sent.astype(BF16), distance)]]
    ppermute x8, waiting for transfers between devices: 10.7 us -> 11.8 us  [swap(): lax.ppermute(values, 'replica', [(i, i ^ distance) for i in range(replica...]
    unnamed x20 -> x18, local copies, waits for them, and re-layouts: 3.6 us -> 2.86 us
  transfers between devices with their start and end apart: 12 -> 12, of which waited for: 6 -> 7; matrix products, arithmetic and copies ran while one was open for 2% -> 3% of each run, Pallas kernels for 15% -> 15%
where the time goes in v6:
time: 108 us; the launch traced here: 107 us
  starting transfers between devices  70.4 us (65%)
  Pallas kernels  17.2 us (16%)
  waiting for transfers between devices  11.8 us (11%)
  local copies, waits for them, and re-layouts  3.81 us (4%)
  other arithmetic  3.05 us (3%)
    ppermute x8, starting transfers between devices, swap(): lax.ppermute(values, 'replica', [(i, i ^ distance) for i in range(replica...  56.7 us
    ppermute x8, waiting for transfers between devices, swap(): lax.ppermute(values, 'replica', [(i, i ^ distance) for i in range(replica...  11.8 us
    all_to_all x1, starting transfers between devices, shards(): lax.all_to_all(table.reshape(experts, 4 * cap, D + EXT), 'expert', split_...  7.7 us
    pallas_call x1, Pallas kernels, shards(): call(functools.partial(pack_kernel, cap), sds((rows, D + EXT), BF16), 56)  3.62 us
    unnamed x18, local copies, waits for them, and re-layouts  2.86 us
    pallas_call x1, Pallas kernels, shards(): call(functools.partial(unpack_kernel, cap), (sds((slots, D), BF16), sds((...  2.75 us
    pallas_call x1, Pallas kernels, shards(): call(last_kernel, sds((1, 1, 3, FRAG, D), F32))  2.67 us
    pallas_call x1, Pallas kernels, shards(): pl.pallas_call(fragment_kernel, out_shape=(sds((3, FRAG, D), F32), sds((F...  2.5 us
  transfers between devices with their start and end apart: 12, of which 7 were waited for; matrix products, arithmetic and copies ran while one was open for 3% of the time, Pallas kernels for 15%

profile of v6, /device:TPU:56, one launch (start us, length us, event | category | flops | bytes accessed | tf_op | source)
XLA Modules:
  0.0 107.3 jit_solution(17648976673166676954)
XLA Ops:
  0.6 0.9 constant_dynamic-slice_fusion
  1.6 4.3 %collective-permute-start = (bf16[96,1024]{1,0:T(8,128)(2,1)S(1)}, bf16[96,1024]{1,0:T(8,128)(2,1)S(1)}, u32[]{:S(2)}, u32[]{:S(2)}) collective-permute-start(bf16[96,1024]{1,0:T(8,128)(2,1)S(1)} %constant_dynamic-slice_fusion), channel_id=1, source_target_pairs={{0,32},{32,0},{64,96},{96,64},{128,160},{160,128},{192,224},{224,1... | collective-permute-start | bytes 589832 | tf_op jit(solution)/shard_map/ppermute | solution.py:235
  5.9 3.6 %shard_map.130 = bf16[384,2176]{1,0:T(8,128)(2,1)} custom-call(bf16[2,64,2048]{2,1,0:T(8,128)(2,1)} %tokens.1, bf16[2,64,2048]{2,1,0:T(8,128)(2,1)} %targets.1, s32[2,1,64]{2,1,0:T(1,128)} %bitcast.35, f32[2,64]{1,0:T(2,128)} %weight.1), custom_call_target="tpu_custom_call" | custom-call | flops 1000000000 | bytes 10000000 | tf_op jit(solution)/shard_map/pallas_call | solution.py:304
  9.5 1.3 %collective-permute-done = bf16[96,1024]{1,0:T(8,128)(2,1)S(1)} collective-permute-done((bf16[96,1024]{1,0:T(8,128)(2,1)S(1)}, bf16[96,1024]{1,0:T(8,128)(2,1)S(1)}, u32[]{:S(2)}, u32[]{:S(2)}) %collective-permute-start) | collective-permute-done | bytes 196640 | tf_op jit(solution)/shard_map/ppermute | solution.py:235
  10.8 7.7 %all-to-all-start = ((bf16[16,24,2176]{2,1,0:T(8,128)(2,1)}), bf16[16,24,2176]{2,1,0:T(8,128)(2,1)S(1)}, u32[]{:S(2)}, u32[]{:S(2)}) async-start(bf16[16,24,2176]{2,1,0:T(8,128)(2,1)} %bitcast.30), calls=%async_computation | async-start | bytes 3342336 | tf_op jit(solution)/shard_map/all_to_all | solution.py:320
  18.5 1.0 add_convert_fusion
  19.5 6.1 %collective-permute-start.1 = (bf16[96,512]{1,0:T(8,128)(2,1)S(1)}, bf16[96,512]{1,0:T(8,128)(2,1)}, u32[]{:S(2)}, u32[]{:S(2)}) collective-permute-start(bf16[96,512]{1,0:T(8,128)(2,1)S(1)} %add_convert_fusion), channel_id=1, source_target_pairs={{0,64},{32,96},{64,0},{96,32},{128,192},{160,224},{192,128},{224,1... | collective-permute-start | bytes 294920 | tf_op jit(solution)/shard_map/ppermute | solution.py:235
  25.6 2.8 %collective-permute-done.1 = bf16[96,512]{1,0:T(8,128)(2,1)} collective-permute-done((bf16[96,512]{1,0:T(8,128)(2,1)S(1)}, bf16[96,512]{1,0:T(8,128)(2,1)}, u32[]{:S(2)}, u32[]{:S(2)}) %collective-permute-start.1) | collective-permute-done | bytes 98336 | tf_op jit(solution)/shard_map/ppermute | solution.py:235
  28.4 1.0 add_convert_fusion.4
  29.4 10.9 %collective-permute-start.2 = (bf16[96,256]{1,0:T(8,128)(2,1)S(1)}, bf16[96,256]{1,0:T(8,128)(2,1)S(1)}, u32[]{:S(2)}, u32[]{:S(2)}) collective-permute-start(bf16[96,256]{1,0:T(8,128)(2,1)S(1)} %add_convert_fusion.4), channel_id=1, source_target_pairs={{0,128},{32,160},{64,192},{96,224},{128,0},{160,32},{192,64},{224,... | collective-permute-start | bytes 147464 | tf_op jit(solution)/shard_map/ppermute | solution.py:235
  40.4 2.0 %collective-permute-done.2 = bf16[96,256]{1,0:T(8,128)(2,1)S(1)} collective-permute-done((bf16[96,256]{1,0:T(8,128)(2,1)S(1)}, bf16[96,256]{1,0:T(8,128)(2,1)S(1)}, u32[]{:S(2)}, u32[]{:S(2)}) %collective-permute-start.2) | collective-permute-done | bytes 49184 | tf_op jit(solution)/shard_map/ppermute | solution.py:235
  42.4 1.0 add_convert_fusion.3
  43.4 8.0 %collective-permute-start.3 = (bf16[96,256]{1,0:T(8,128)(2,1)S(1)}, bf16[96,256]{1,0:T(8,128)(2,1)S(1)}, u32[]{:S(2)}, u32[]{:S(2)}) collective-permute-start(bf16[96,256]{1,0:T(8,128)(2,1)S(1)} %add_convert_fusion.3), channel_id=1, source_target_pairs={{0,512},{32,544},{64,576},{96,608},{128,640},{160,672},{192,704},{... | collective-permute-start | bytes 147464 | tf_op jit(solution)/shard_map/ppermute | solution.py:235
  51.4 2.1 %collective-permute-done.3 = bf16[96,256]{1,0:T(8,128)(2,1)S(1)} collective-permute-done((bf16[96,256]{1,0:T(8,128)(2,1)S(1)}, bf16[96,256]{1,0:T(8,128)(2,1)S(1)}, u32[]{:S(2)}, u32[]{:S(2)}) %collective-permute-start.3) | collective-permute-done | bytes 49184 | tf_op jit(solution)/shard_map/ppermute | solution.py:235
  53.4 14.1 %collective-permute-start.4 = (bf16[96,256]{1,0:T(8,128)(2,1)S(1)}, bf16[96,256]{1,0:T(8,128)(2,1)S(1)}, u32[]{:S(2)}, u32[]{:S(2)}) collective-permute-start(bf16[96,256]{1,0:T(8,128)(2,1)S(1)} %add_convert_fusion.2), channel_id=1, source_target_pairs={{0,384},{32,416},{64,448},{96,480},{128,256},{160,288},{192,320},{... | collective-permute-start | bytes 147464 | tf_op jit(solution)/shard_map/ppermute | solution.py:235
  67.5 2.1 %collective-permute-done.4 = bf16[96,256]{1,0:T(8,128)(2,1)S(1)} collective-permute-done((bf16[96,256]{1,0:T(8,128)(2,1)S(1)}, bf16[96,256]{1,0:T(8,128)(2,1)S(1)}, u32[]{:S(2)}, u32[]{:S(2)}) %collective-permute-start.4) | collective-permute-done | bytes 49184 | tf_op jit(solution)/shard_map/ppermute | solution.py:235
  69.7 1.9 %collective-permute-start.5 = (bf16[384,2176]{1,0:T(8,128)(2,1)S(1)}, bf16[384,2176]{1,0:T(8,128)(2,1)S(1)}, u32[]{:S(2)}, u32[]{:S(2)}) collective-permute-start(bf16[384,2176]{1,0:T(8,128)(2,1)S(1)} %bitcast.15), channel_id=1, source_target_pairs={{0,1},{1,0},{2,3},{3,2},{4,5},{5,4},{6,7},{7,6},{8,9},{9,8},{10,11... | collective-permute-start | bytes 5013512 | tf_op jit(solution)/shard_map/ppermute | solution.py:329
  71.6 6.2 %collective-permute-start.6 = (bf16[96,256]{1,0:T(8,128)(2,1)S(1)}, bf16[96,256]{1,0:T(8,128)(2,1)S(1)}, u32[]{:S(2)}, u32[]{:S(2)}) collective-permute-start(bf16[96,256]{1,0:T(8,128)(2,1)S(1)} %add_convert_fusion.1), channel_id=1, source_target_pairs={{0,128},{32,160},{64,192},{96,224},{128,0},{160,32},{192,64},{224,... | collective-permute-start | bytes 147464 | tf_op jit(solution)/shard_map/ppermute | solution.py:235
  77.8 1.4 %copy-done.1 = bf16[1,2048,384]{2,1,0:T(8,128)(2,1)S(1)} copy-done((bf16[1,2048,384]{2,1,0:T(8,128)(2,1)S(1)}, bf16[1,2048,384]{2,1,0:T(8,128)(2,1)}, u32[]{:S(2)}) %copy-start.1) | copy-done | bytes 1572888
  79.2 1.4 %copy-done.3 = bf16[1,384,2048]{2,1,0:T(8,128)(2,1)S(1)} copy-done((bf16[1,384,2048]{2,1,0:T(8,128)(2,1)S(1)}, bf16[1,384,2048]{2,1,0:T(8,128)(2,1)}, u32[]{:S(2)}) %copy-start.3) | copy-done | bytes 1572888
  80.6 2.1 %shard_map.131 = (bf16[192,2048]{1,0:T(8,128)(2,1)S(1)}, f32[192,2048]{1,0:T(8,128)S(1)}, bf16[192,2048]{1,0:T(8,128)(2,1)S(1)}, f32[192,384]{1,0:T(8,128)S(1)},...) custom-call(bf16[384,2176]{1,0:T(8,128)(2,1)S(1)} %bitcast.16, bf16[384,2176]{1,0:T(8,128)(2,1)S(1)} %collective-permute-done.5.other, ...), custom_call_target="tpu_custom_call" | custom-call | flops 1000000000 | bytes 10000000 | tf_op jit(solution)/shard_map/pallas_call | solution.py:339
  82.7 2.1 %collective-permute-start.7 = (bf16[192,2048]{1,0:T(8,128)(2,1)S(1)}, bf16[192,2048]{1,0:T(8,128)(2,1)S(1)}, u32[]{:S(2)}, u32[]{:S(2)}) collective-permute-start(bf16[192,2048]{1,0:T(8,128)(2,1)S(1)} %get-tuple-element.46), channel_id=1, source_target_pairs={{0,1},{1,0},{2,3},{3,2},{4,5},{5,4},{6,7},{7,6},{8,9},{9,8},{10,11... | collective-permute-start | bytes 2359304 | tf_op jit(solution)/shard_map/ppermute | solution.py:353
  84.9 3.9 %collective-permute-start.8 = (bf16[192,256]{1,0:T(8,128)(2,1)S(1)}, bf16[192,256]{1,0:T(8,128)(2,1)S(1)}, u32[]{:S(2)}, u32[]{:S(2)}) collective-permute-start(bf16[192,256]{1,0:T(8,128)(2,1)S(1)} %pad_maximum_fusion), channel_id=1, source_target_pairs={{0,64},{32,96},{64,0},{96,32},{128,192},{160,224},{192,128},{224,1... | collective-permute-start | bytes 294920 | tf_op jit(solution)/shard_map/ppermute | solution.py:235
  88.8 2.7 %shard_map.132 = (bf16[192,2048]{1,0:T(8,128)(2,1)S(1)}, bf16[192,2048]{1,0:T(8,128)(2,1)S(1)}, bf16[192,2048]{1,0:T(8,128)(2,1)S(1)}, f32[2,192,128]{2,1,0:T(8,...) custom-call(bf16[384,2176]{1,0:T(8,128)(2,1)S(1)} %bitcast.17, ...), custom_call_target="tpu_custom_call" | custom-call | flops 1000000000 | bytes 10000000 | tf_op jit(solution)/shard_map/pallas_call | solution.py:355
  91.6 2.2 %shard_map.133 = (bf16[192,2048]{1,0:T(8,128)(2,1)S(1)}, bf16[192,384]{1,0:T(8,128)(2,1)S(1)}, bf16[192,384]{1,0:T(8,128)(2,1)S(1)}, f32[192,2048]{1,0:T(8,128)S...) custom-call(f32[192,2048]{1,0:T(8,128)S(1)} %get-tuple-element.43.pa, ...), custom_call_target="tpu_custom_call" | custom-call | flops 1000000000 | bytes 10000000 | tf_op jit(solution)/shard_map/pallas_call | solution.py:367
  93.9 0.9 collective-permute-done.8
  94.8 1.9 %collective-permute-start.9 = (bf16[192,2048]{1,0:T(8,128)(2,1)S(1)}, bf16[192,2048]{1,0:T(8,128)(2,1)S(1)}, u32[]{:S(2)}, u32[]{:S(2)}) collective-permute-start(bf16[192,2048]{1,0:T(8,128)(2,1)S(1)} %get-tuple-element.59), channel_id=1, source_target_pairs={{0,1},{1,0},{2,3},{3,2},{4,5},{5,4},{6,7},{7,6},{8,9},{9,8},{10,11... | collective-permute-start | bytes 2359304 | tf_op jit(solution)/shard_map/ppermute | solution.py:383
  96.7 3.3 %collective-permute-start.10 = (bf16[384,256]{1,0:T(8,128)(2,1)S(1)}, bf16[384,256]{1,0:T(8,128)(2,1)S(1)}, u32[]{:S(2)}, u32[]{:S(2)}) collective-permute-start(bf16[384,256]{1,0:T(8,128)(2,1)S(1)} %constant_dynamic-update-slice_fusion.held_pieces), channel_id=1, source_target_pairs={{0,32},{32,0},{64,96},{96,64},{128,160},{160,128},{192,224},{224,1... | collective-permute-start | bytes 589832 | tf_op jit(solution)/shard_map/ppermute | solution.py:235
  100.1 2.5 %shard_map.134 = (f32[3,32,2048]{2,1,0:T(8,128)S(1)}, f32[32,2048]{1,0:T(8,128)S(1)}, f32[2,192,32]{2,1,0:T(8,128)S(1)}, bf16[192,32]{1,0:T(8,128)(2,1)S(1)}) custom-call(s32[12]{0:T(128)S(1)} %copy-done.6, bf16[2048,384]{1,0:T(8,128)(2,1)S(1)} %bitcast.20, bf16[2048,384]{1,0:T(8,128)(2,1)S(1)} %bitcast.23, bf16[384,2048]{1,0:T(8,128)(2,1)S(1)} %bitcast.26, ...), custom_call_target="tpu_custom_call" | custom-call | flops 1000000000 | bytes 10000000 | tf_op jit(solution)/shard_map/pallas_call | solution.py:387
  102.6 2.7 %shard_map.135 = f32[1,1,3,32,2048]{4,3,2,1,0:T(8,128)} custom-call(f32[192,2048]{1,0:T(8,128)S(1)} %get-tuple-element.56.partial, bf16[192,2048]{1,0:T(8,128)(2,1)S(1)} %collective-permute-done.9.received, bf16[192,2048]{1,0:T(8,128)(2,1)S(1)} %get-tuple-element.60.t2, f32[2,192,128]{2,1,0:T(8,128)S(1)} %get-tuple-element.49.w, ...), custom_call_target="tpu_custom_call" | custom-call | flops 1000000000 | bytes 10000000 | tf_op jit(solution)/shard_map/pallas_call | solution.py:405
  105.3 0.6 collective-permute-done.10.got_pieces
  105.9 1.4 %shard_map.136 = (f32[96,2048]{1,0:T(8,128)}, f32[96,2048]{1,0:T(8,128)}) custom-call(s32[1]{0:T(128)} %bitcast.9.me, bf16[384,256]{1,0:T(8,128)(2,1)S(1)} %constant_dynamic-update-slice_fusion.held_pieces, bf16[384,256]{1,0:T(8,128)(2,1)S(1)} %collective-permute-done.10.got_pieces, f32[96,2048]{1,0:T(8,128)S(1)} %bitcast.28, f32[96,2048]{1,0:T(8,128)S(1)} %bitcast.29), custom_call_target="tpu_custom_call" | custom-call | flops 1000000000 | bytes 10000000 | tf_op jit(solution)/shard_map/pallas_call | solution.py:409
  (25 shorter events, 0.1 us)
Async XLA Ops:
  1.6 9.2 %collective-permute-start = (bf16[96,1024]{1,0:T(8,128)(2,1)S(1)}, bf16[96,1024]{1,0:T(8,128)(2,1)S(1)}, u32[]{:S(2)}, u32[]{:S(2)}) collective-permute-start(bf16[96,1024]{1,0:T(8,128)(2,1)S(1)} %constant_dynamic-slice_fusion), channel_id=1, source_target_pairs={{0,32},{32,0},{64,96},{96,64},{128,160},{160,128},{192,224},{224,1... | collective-permute-start | bytes 589832 | tf_op jit(solution)/shard_map/ppermute | solution.py:235
  10.8 67.0 %copy-start = (bf16[1,2048,384]{2,1,0:T(8,128)(2,1)S(1)}, bf16[1,2048,384]{2,1,0:T(8,128)(2,1)}, u32[]{:S(2)}) copy-start(bf16[1,2048,384]{2,1,0:T(8,128)(2,1)} %param.15) | copy-start | bytes 4718596
  10.8 58.9 %all-to-all-start = ((bf16[16,24,2176]{2,1,0:T(8,128)(2,1)}), bf16[16,24,2176]{2,1,0:T(8,128)(2,1)S(1)}, u32[]{:S(2)}, u32[]{:S(2)}) async-start(bf16[16,24,2176]{2,1,0:T(8,128)(2,1)} %bitcast.30), calls=%async_computation | async-start | bytes 3342336 | tf_op jit(solution)/shard_map/all_to_all | solution.py:320
  19.5 8.9 %collective-permute-start.1 = (bf16[96,512]{1,0:T(8,128)(2,1)S(1)}, bf16[96,512]{1,0:T(8,128)(2,1)}, u32[]{:S(2)}, u32[]{:S(2)}) collective-permute-start(bf16[96,512]{1,0:T(8,128)(2,1)S(1)} %add_convert_fusion), channel_id=1, source_target_pairs={{0,64},{32,96},{64,0},{96,32},{128,192},{160,224},{192,128},{224,1... | collective-permute-start | bytes 294920 | tf_op jit(solution)/shard_map/ppermute | solution.py:235
  29.4 13.0 %collective-permute-start.2 = (bf16[96,256]{1,0:T(8,128)(2,1)S(1)}, bf16[96,256]{1,0:T(8,128)(2,1)S(1)}, u32[]{:S(2)}, u32[]{:S(2)}) collective-permute-start(bf16[96,256]{1,0:T(8,128)(2,1)S(1)} %add_convert_fusion.4), channel_id=1, source_target_pairs={{0,128},{32,160},{64,192},{96,224},{128,0},{160,32},{192,64},{224,... | collective-permute-start | bytes 147464 | tf_op jit(solution)/shard_map/ppermute | solution.py:235
  43.4 10.0 %collective-permute-start.3 = (bf16[96,256]{1,0:T(8,128)(2,1)S(1)}, bf16[96,256]{1,0:T(8,128)(2,1)S(1)}, u32[]{:S(2)}, u32[]{:S(2)}) collective-permute-start(bf16[96,256]{1,0:T(8,128)(2,1)S(1)} %add_convert_fusion.3), channel_id=1, source_target_pairs={{0,512},{32,544},{64,576},{96,608},{128,640},{160,672},{192,704},{... | collective-permute-start | bytes 147464 | tf_op jit(solution)/shard_map/ppermute | solution.py:235
  53.4 16.2 %collective-permute-start.4 = (bf16[96,256]{1,0:T(8,128)(2,1)S(1)}, bf16[96,256]{1,0:T(8,128)(2,1)S(1)}, u32[]{:S(2)}, u32[]{:S(2)}) collective-permute-start(bf16[96,256]{1,0:T(8,128)(2,1)S(1)} %add_convert_fusion.2), channel_id=1, source_target_pairs={{0,384},{32,416},{64,448},{96,480},{128,256},{160,288},{192,320},{... | collective-permute-start | bytes 147464 | tf_op jit(solution)/shard_map/ppermute | solution.py:235
  69.7 8.1 %collective-permute-start.5 = (bf16[384,2176]{1,0:T(8,128)(2,1)S(1)}, bf16[384,2176]{1,0:T(8,128)(2,1)S(1)}, u32[]{:S(2)}, u32[]{:S(2)}) collective-permute-start(bf16[384,2176]{1,0:T(8,128)(2,1)S(1)} %bitcast.15), channel_id=1, source_target_pairs={{0,1},{1,0},{2,3},{3,2},{4,5},{5,4},{6,7},{7,6},{8,9},{9,8},{10,11... | collective-permute-start | bytes 5013512 | tf_op jit(solution)/shard_map/ppermute | solution.py:329
  71.6 11.1 %collective-permute-start.6 = (bf16[96,256]{1,0:T(8,128)(2,1)S(1)}, bf16[96,256]{1,0:T(8,128)(2,1)S(1)}, u32[]{:S(2)}, u32[]{:S(2)}) collective-permute-start(bf16[96,256]{1,0:T(8,128)(2,1)S(1)} %add_convert_fusion.1), channel_id=1, source_target_pairs={{0,128},{32,160},{64,192},{96,224},{128,0},{160,32},{192,64},{224,... | collective-permute-start | bytes 147464 | tf_op jit(solution)/shard_map/ppermute | solution.py:235
  77.8 1.4 %copy-start.1 = (bf16[1,2048,384]{2,1,0:T(8,128)(2,1)S(1)}, bf16[1,2048,384]{2,1,0:T(8,128)(2,1)}, u32[]{:S(2)}) copy-start(bf16[1,2048,384]{2,1,0:T(8,128)(2,1)} %param.16) | copy-start | bytes 4718596
  79.2 1.4 %copy-start.3 = (bf16[1,384,2048]{2,1,0:T(8,128)(2,1)S(1)}, bf16[1,384,2048]{2,1,0:T(8,128)(2,1)}, u32[]{:S(2)}) copy-start(bf16[1,384,2048]{2,1,0:T(8,128)(2,1)} %param.17) | copy-start | bytes 4718596
  82.7 8.9 %collective-permute-start.7 = (bf16[192,2048]{1,0:T(8,128)(2,1)S(1)}, bf16[192,2048]{1,0:T(8,128)(2,1)S(1)}, u32[]{:S(2)}, u32[]{:S(2)}) collective-permute-start(bf16[192,2048]{1,0:T(8,128)(2,1)S(1)} %get-tuple-element.46), channel_id=1, source_target_pairs={{0,1},{1,0},{2,3},{3,2},{4,5},{5,4},{6,7},{7,6},{8,9},{9,8},{10,11... | collective-permute-start | bytes 2359304 | tf_op jit(solution)/shard_map/ppermute | solution.py:353
  84.9 9.9 %collective-permute-start.8 = (bf16[192,256]{1,0:T(8,128)(2,1)S(1)}, bf16[192,256]{1,0:T(8,128)(2,1)S(1)}, u32[]{:S(2)}, u32[]{:S(2)}) collective-permute-start(bf16[192,256]{1,0:T(8,128)(2,1)S(1)} %pad_maximum_fusion), channel_id=1, source_target_pairs={{0,64},{32,96},{64,0},{96,32},{128,192},{160,224},{192,128},{224,1... | collective-permute-start | bytes 294920 | tf_op jit(solution)/shard_map/ppermute | solution.py:235
  88.8 2.8 %copy-start.4 = (bf16[1,384,2048]{2,1,0:T(8,128)(2,1)S(1)}, bf16[1,384,2048]{2,1,0:T(8,128)(2,1)}, u32[]{:S(2)}) copy-start(bf16[1,384,2048]{2,1,0:T(8,128)(2,1)} %param.17) | copy-start | bytes 4718596
  91.6 8.5 %copy-start.2 = (bf16[1,2048,384]{2,1,0:T(8,128)(2,1)S(1)}, bf16[1,2048,384]{2,1,0:T(8,128)(2,1)}, u32[]{:S(2)}) copy-start(bf16[1,2048,384]{2,1,0:T(8,128)(2,1)} %param.16) | copy-start | bytes 4718596
  91.6 8.5 %copy-start.5 = (f32[1,3,32,2048]{3,2,1,0:T(8,128)S(1)}, f32[1,3,32,2048]{3,2,1,0:T(8,128)}, u32[]{:S(2)}) copy-start(f32[1,3,32,2048]{3,2,1,0:T(8,128)} %param.19) | copy-start | bytes 2359300
  91.6 8.5 %copy-start.6 = (s32[12]{0:T(128)S(1)}, s32[12]{0:T(128)}, u32[]{:S(2)}) copy-start(s32[12]{0:T(128)} %index.1) | copy-start | bytes 148
  94.8 7.8 %collective-permute-start.9 = (bf16[192,2048]{1,0:T(8,128)(2,1)S(1)}, bf16[192,2048]{1,0:T(8,128)(2,1)S(1)}, u32[]{:S(2)}, u32[]{:S(2)}) collective-permute-start(bf16[192,2048]{1,0:T(8,128)(2,1)S(1)} %get-tuple-element.59), channel_id=1, source_target_pairs={{0,1},{1,0},{2,3},{3,2},{4,5},{5,4},{6,7},{7,6},{8,9},{9,8},{10,11... | collective-permute-start | bytes 2359304 | tf_op jit(solution)/shard_map/ppermute | solution.py:383
  96.7 9.2 %collective-permute-start.10 = (bf16[384,256]{1,0:T(8,128)(2,1)S(1)}, bf16[384,256]{1,0:T(8,128)(2,1)S(1)}, u32[]{:S(2)}, u32[]{:S(2)}) collective-permute-start(bf16[384,256]{1,0:T(8,128)(2,1)S(1)} %constant_dynamic-update-slice_fusion.held_pieces), channel_id=1, source_target_pairs={{0,32},{32,0},{64,96},{96,64},{128,160},{160,128},{192,224},{224,1... | collective-permute-start | bytes 589832 | tf_op jit(solution)/shard_map/ppermute | solution.py:235
  102.6 3.3 %copy-start.7 = (f32[1,3,32,2048]{3,2,1,0:T(8,128)S(1)}, f32[1,3,32,2048]{3,2,1,0:T(8,128)}, u32[]{:S(2)}) copy-start(f32[1,3,32,2048]{3,2,1,0:T(8,128)} %param.20) | copy-start | bytes 2359300
